TPU v7x, 32 devices: a whole 2x2x4 slice. The times are simulated.
32 devices in a mesh: layer: 8 (over z, core), row: 4 (over y, x).
Axes of the slice: x: 2, y: 2, z: 4, core: 2. Of those that a mesh axis runs over, the one named last changes fastest.
Arguments:
- propagator: float32 [8, 16384, 6, 128], P('layer', 'row'), may hold values from -0.15625 to 0.15625
- col_blocks: int32 [8, 128, 6], P('layer', 'row'), may hold values from 0 to 127, as said below
- sources: bfloat16 [8, 8, 56, 16384], P(None, 'layer', None, 'row'), may hold values from -6 to 6
- incoming: bfloat16 [8, 56, 16384], P('layer', None, 'row'), may hold values from -6 to 6
Outputs:
- outgoing: bfloat16 [8, 8, 56, 16384], P(None, 'layer', None, 'row')
Inputs may be any that keep to these rules, and one draw needn't show every extreme that they name: col_blocks[l, r, k] differs from r by at most 32; slot 0 is r itself, slots 1 and 2 are r - 32 and r + 32 kept within 0 .. 127; entries of one row block may repeat.
All inputs are finite; a program needn't handle non-finite values.
Results may differ from a plain program's by a relative error of at most 0.0043.
Values may be sent and summed in bfloat16 or wider, within the bound.
No kernel may reach another device: no remote copies, remote signals or barrier semaphores. Data moves between devices by JAX's collectives and lax.ppermute only.
A program may use at most 64 MiB of HBM per device.

v0:
```python
import functools

import jax
import jax.numpy as jnp
from jax import lax
from jax.experimental import pallas as pl
from jax.experimental.pallas import tpu as pltpu
from jax.sharding import PartitionSpec as P

MIB = 1024 * 1024


def convert_kernel(prop_ref, weights_ref, blocks, arrived):
    row_blocks = weights_ref.shape[0]
    flight, slots, blk, _ = blocks.shape

    def fetch(r, slot):
        rows = pl.ds(pl.multiple_of(r * blk, blk), blk)
        return pltpu.make_async_copy(prop_ref.at[:, rows, :], blocks.at[slot], arrived.at[slot])

    for r in range(flight):
        fetch(r, r).start()

    def step(r, carry):
        slot = lax.rem(r, flight)
        fetch(r, slot).wait()
        for k in range(slots):
            weights_ref[r, k * blk:(k + 1) * blk, :] = blocks[slot, k].astype(jnp.bfloat16).T

        @pl.when(r + flight < row_blocks)
        def _():
            fetch(r + flight, slot).start()

        return carry

    lax.fori_loop(0, row_blocks, step, 0)


def convert_weights(prop):
    slots, rows, blk = prop.shape
    flight = min(8, rows // blk)
    return pl.pallas_call(
        convert_kernel,
        in_specs=[pl.BlockSpec(memory_space=pltpu.HBM)],
        out_specs=pl.BlockSpec(memory_space=pltpu.VMEM),
        out_shape=jax.ShapeDtypeStruct((rows // blk, slots * blk, blk), jnp.bfloat16),
        scratch_shapes=[
            pltpu.VMEM((flight, slots, blk, blk), jnp.float32),
            pltpu.SemaphoreType.DMA((flight,)),
        ],
        compiler_params=pltpu.CompilerParams(vmem_limit_bytes=44 * MIB),
        cost_estimate=pl.CostEstimate(flops=0, bytes_accessed=prop.size * 4, transcendentals=0),
        name="convert_weights",
    )(prop)


def tick_kernel(tick, first, cols_ref, weights_ref, far_ref, near_ref, own_ref, source_ref, before_ref, out_ref, window):
    del before_ref
    shots, width = own_ref.shape
    row_blocks, depth, blk = weights_ref.shape
    slots = depth // blk
    window[:, :width] = near_ref[...]
    window[:, width:2 * width] = own_ref[...]
    window[:, 2 * width:] = far_ref[...]

    def step(r, carry):
        picked = []
        for k in range(slots):
            start = pl.multiple_of(cols_ref[r * slots + k] * blk, blk)
            picked.append(window[:, pl.ds(start, blk)])
        mixed = jnp.dot(jnp.concatenate(picked, axis=1), weights_ref[r], preferred_element_type=jnp.float32)
        here = pl.ds(pl.multiple_of(r * blk, blk), blk)
        out_ref[:, here] = (mixed + source_ref[tick, 0, first:first + shots, here].astype(jnp.float32)).astype(out_ref.dtype)
        return carry

    lax.fori_loop(0, row_blocks, step, 0, unroll=8)


def apply_layer(tick, first, cols, weights, far, near, own, sources, before):
    shots, width = own.shape
    vmem = pl.BlockSpec(memory_space=pltpu.VMEM)
    return pl.pallas_call(
        functools.partial(tick_kernel, tick, first),
        in_specs=[pl.BlockSpec(memory_space=pltpu.SMEM)] + [vmem] * 5 + [pl.BlockSpec(memory_space=pl.ANY)],
        out_specs=vmem,
        out_shape=jax.ShapeDtypeStruct((shots, width), jnp.bfloat16),
        scratch_shapes=[pltpu.VMEM((shots, 3 * width), jnp.bfloat16)],
        compiler_params=pltpu.CompilerParams(vmem_limit_bytes=8 * MIB),
        cost_estimate=pl.CostEstimate(
            flops=2 * shots * weights.size, bytes_accessed=weights.size * 2, transcendentals=0
        ),
        name="apply_layer",
    )(cols, weights, far, near, own, sources, before)


def partner(r, rows, far):
    other = (r + 1 if r % 2 else r - 1) if far else r ^ 1
    return other if 0 <= other < rows else None


def send(value, layers, up, targets):
    rows = len(targets)
    pairs = []
    for l in range(layers - up):
        for r, target in enumerate(targets):
            if target is not None:
                pairs.append((l * rows + r, (l + up) * rows + target))
    return lax.ppermute(value, ("layer", "row"), pairs)


def body(propagator, col_blocks, sources, incoming):
    _, row_count, slots, blk = propagator.shape
    ticks, _, shots, _ = sources.shape
    layers = lax.axis_size("layer")
    rows = lax.axis_size("row")
    near = [partner(r, rows, False) for r in range(rows)]
    far = [partner(r, rows, True) for r in range(rows)]
    block_count = row_count // blk
    place = lax.axis_index("row")
    side = lax.div(col_blocks[0], block_count) - place
    third = 1 + side * (2 * lax.rem(place, 2) - 1)
    cols = (third * block_count + lax.rem(col_blocks[0], block_count)).reshape(-1)
    cut = (shots // 16 + 1) // 2 * 16
    panels = [(0, cut), (cut, shots)]
    arriving = []
    for a, b in panels:
        own = incoming[0, a:b]
        distant = send(own, layers, 0, far)
        arriving.append((distant, send(own, layers, 0, near), own))
    weights = convert_weights(jnp.transpose(propagator[0], (1, 0, 2)))
    before = weights
    history = []
    for tick in range(ticks):
        produced = []
        for i in range(len(panels)):
            done = apply_layer(tick, panels[i][0], cols, weights, *arriving[i], sources, before)
            before = done
            produced.append(done)
            if tick + 1 < ticks:
                distant = send(done, layers, 1, far)
                beside = send(done, layers, 1, near)
                arriving[i] = (distant, beside, send(done, layers, 1, range(rows)))
        history.append(jnp.concatenate(produced, axis=0))
    return jnp.stack(history)[:, None]


def solution(mesh):
    return jax.shard_map(
        body,
        mesh=mesh,
        in_specs=(
            P("layer", "row", None, None),
            P("layer", "row", None),
            P(None, "layer", None, "row"),
            P("layer", None, "row"),
        ),
        out_specs=P(None, "layer", None, "row"),
        check_vma=False,
    )
```

profile of v0, /device:TPU:11, one launch (start us, length us, event | category | flops | bytes accessed | tf_op | source)
XLA Modules:
  0.0 172.7 jit_solution(1420624179038054815)
XLA Ops:
  1.0 3.1 %collective-permute-start = (bf16[32,4096]{1,0:T(8,128)(2,1)S(1)}, bf16[32,4096]{1,0:T(8,128)(2,1)S(1)}, u32[]{:S(2)}, u32[]{:S(2)}) collective-permute-start(bf16[32,4096]{1,0:T(8,128)(2,1)S(1)} %slice_bitcast_fusion.own_ref), channel_id=1, source_target_pairs={{1,2},{2,1},{5,6},{6,5},{9,10},{10,9},{13,14},{14,13},{17,18},{18,... | collective-permute-start | bytes 786440 | tf_op jit(solution)/shard_map/ppermute | solution.py:108
  5.1 3.1 %collective-permute-start.2 = (bf16[24,4096]{1,0:T(8,128)(2,1)S(1)}, bf16[24,4096]{1,0:T(8,128)(2,1)S(1)}, u32[]{:S(2)}, u32[]{:S(2)}) collective-permute-start(bf16[24,4096]{1,0:T(8,128)(2,1)S(1)} %slice_bitcast_fusion.1.own_ref), channel_id=1, source_target_pairs={{1,2},{2,1},{5,6},{6,5},{9,10},{10,9},{13,14},{14,13},{17,18},{18,... | collective-permute-start | bytes 589832 | tf_op jit(solution)/shard_map/ppermute | solution.py:108
  9.2 5.9 %convert_weights.1.weights_ref.before_ref = bf16[32,768,128]{2,1,0:T(8,128)(2,1)S(1)} custom-call(f32[6,4096,128]{2,1,0:T(8,128)} %bitcast.42), custom_call_target="tpu_custom_call" | custom-call | bytes 12582912 | tf_op jit(solution)/shard_map/convert_weights/pallas_call | solution.py:42
  15.1 2.1 %apply_layer.16.before_ref = bf16[32,4096]{1,0:T(8,128)(2,1)S(1)} custom-call(s32[192]{0:T(256)S(1)} %fusion.11.cols_ref, bf16[32,768,128]{2,1,0:T(8,128)(2,1)S(1)} %convert_weights.1.weights_ref.before_ref, bf16[32,4096]{1,0:T(8,128)(2,1)S(1)} %collective-permute-done.far_ref, bf16[32,4096]{1,0:T(8,128)(2,1)S(1)} %collective-permute-done.1.near_ref, ...), custom_call_target="tpu_custom_call" | custom-call | flops 201326592 | bytes 6291456 | tf_op jit(solution)/shard_map/apply_layer/pallas_call | solution.py:82
  17.2 6.2 %collective-permute-start.4 = (bf16[32,4096]{1,0:T(8,128)(2,1)S(1)}, bf16[32,4096]{1,0:T(8,128)(2,1)S(1)}, u32[]{:S(2)}, u32[]{:S(2)}) collective-permute-start(bf16[32,4096]{1,0:T(8,128)(2,1)S(1)} %apply_layer.16.before_ref), channel_id=1, source_target_pairs={{1,6},{2,5},{5,10},{6,9},{9,14},{10,13},{13,18},{14,17},{17,22},{1... | collective-permute-start | bytes 786440 | tf_op jit(solution)/shard_map/ppermute | solution.py:108
  29.3 7.0 %collective-permute-start.7 = (bf16[24,4096]{1,0:T(8,128)(2,1)S(1)}, bf16[24,4096]{1,0:T(8,128)(2,1)S(1)}, u32[]{:S(2)}, u32[]{:S(2)}) collective-permute-start(bf16[24,4096]{1,0:T(8,128)(2,1)S(1)} %apply_layer.17.before_ref), channel_id=1, source_target_pairs={{1,6},{2,5},{5,10},{6,9},{9,14},{10,13},{13,18},{14,17},{17,22},{1... | collective-permute-start | bytes 589832 | tf_op jit(solution)/shard_map/ppermute | solution.py:108
  40.2 2.1 %apply_layer.18.before_ref = bf16[32,4096]{1,0:T(8,128)(2,1)S(1)} custom-call(s32[192]{0:T(256)S(1)} %fusion.11.cols_ref, bf16[32,768,128]{2,1,0:T(8,128)(2,1)S(1)} %convert_weights.1.weights_ref.before_ref, bf16[32,4096]{1,0:T(8,128)(2,1)S(1)} %collective-permute-done.4.far_ref, bf16[32,4096]{1,0:T(8,128)(2,1)S(1)} %collective-permute-done.5.near_ref, ...), custom_call_target="tpu_custom_call" | custom-call | flops 201326592 | bytes 6291456 | tf_op jit(solution)/shard_map/apply_layer/pallas_call | solution.py:82
  42.3 4.5 %collective-permute-start.10 = (bf16[32,4096]{1,0:T(8,128)(2,1)S(1)}, bf16[32,4096]{1,0:T(8,128)(2,1)S(1)}, u32[]{:S(2)}, u32[]{:S(2)}) collective-permute-start(bf16[32,4096]{1,0:T(8,128)(2,1)S(1)} %apply_layer.18.before_ref), channel_id=1, source_target_pairs={{1,6},{2,5},{5,10},{6,9},{9,14},{10,13},{13,18},{14,17},{17,22},{1... | collective-permute-start | bytes 786440 | tf_op jit(solution)/shard_map/ppermute | solution.py:108
  48.7 2.1 %collective-permute-start.12 = (bf16[32,4096]{1,0:T(8,128)(2,1)S(1)}, bf16[32,4096]{1,0:T(8,128)(2,1)S(1)}, u32[]{:S(2)}, u32[]{:S(2)}) collective-permute-start(bf16[32,4096]{1,0:T(8,128)(2,1)S(1)} %apply_layer.18.before_ref), channel_id=1, source_target_pairs={{0,4},{1,5},{2,6},{3,7},{4,8},{5,9},{6,10},{7,11},{8,12},{9,13},{1... | collective-permute-start | bytes 786440 | tf_op jit(solution)/shard_map/ppermute | solution.py:108
  52.9 2.8 %collective-permute-start.13 = (bf16[24,4096]{1,0:T(8,128)(2,1)S(1)}, bf16[24,4096]{1,0:T(8,128)(2,1)S(1)}, u32[]{:S(2)}, u32[]{:S(2)}) collective-permute-start(bf16[24,4096]{1,0:T(8,128)(2,1)S(1)} %apply_layer.19.before_ref), channel_id=1, source_target_pairs={{1,6},{2,5},{5,10},{6,9},{9,14},{10,13},{13,18},{14,17},{17,22},{1... | collective-permute-start | bytes 589832 | tf_op jit(solution)/shard_map/ppermute | solution.py:108
  59.6 2.1 %apply_layer.20.before_ref = bf16[32,4096]{1,0:T(8,128)(2,1)S(1)} custom-call(s32[192]{0:T(256)S(1)} %fusion.11.cols_ref, bf16[32,768,128]{2,1,0:T(8,128)(2,1)S(1)} %convert_weights.1.weights_ref.before_ref, bf16[32,4096]{1,0:T(8,128)(2,1)S(1)} %collective-permute-done.10.far_ref, bf16[32,4096]{1,0:T(8,128)(2,1)S(1)} %collective-permute-done.11.near_ref, ...), custom_call_target="tpu_custom_call" | custom-call | flops 201326592 | bytes 6291456 | tf_op jit(solution)/shard_map/apply_layer/pallas_call | solution.py:82
  61.7 6.7 %collective-permute-start.16 = (bf16[32,4096]{1,0:T(8,128)(2,1)S(1)}, bf16[32,4096]{1,0:T(8,128)(2,1)S(1)}, u32[]{:S(2)}, u32[]{:S(2)}) collective-permute-start(bf16[32,4096]{1,0:T(8,128)(2,1)S(1)} %apply_layer.20.before_ref), channel_id=1, source_target_pairs={{1,6},{2,5},{5,10},{6,9},{9,14},{10,13},{13,18},{14,17},{17,22},{1... | collective-permute-start | bytes 786440 | tf_op jit(solution)/shard_map/ppermute | solution.py:108
  72.3 2.0 %apply_layer.21.before_ref = bf16[24,4096]{1,0:T(8,128)(2,1)S(1)} custom-call(s32[192]{0:T(256)S(1)} %fusion.11.cols_ref, bf16[32,768,128]{2,1,0:T(8,128)(2,1)S(1)} %convert_weights.1.weights_ref.before_ref, bf16[24,4096]{1,0:T(8,128)(2,1)S(1)} %collective-permute-done.13.far_ref, bf16[24,4096]{1,0:T(8,128)(2,1)S(1)} %collective-permute-done.14.near_ref, ...), custom_call_target="tpu_custom_call" | custom-call | flops 150994944 | bytes 6291456 | tf_op jit(solution)/shard_map/apply_layer/pallas_call | solution.py:82
  74.3 2.6 %collective-permute-start.19 = (bf16[24,4096]{1,0:T(8,128)(2,1)S(1)}, bf16[24,4096]{1,0:T(8,128)(2,1)S(1)}, u32[]{:S(2)}, u32[]{:S(2)}) collective-permute-start(bf16[24,4096]{1,0:T(8,128)(2,1)S(1)} %apply_layer.21.before_ref), channel_id=1, source_target_pairs={{1,6},{2,5},{5,10},{6,9},{9,14},{10,13},{13,18},{14,17},{17,22},{1... | collective-permute-start | bytes 589832 | tf_op jit(solution)/shard_map/ppermute | solution.py:108
  80.8 2.1 %apply_layer.22.before_ref = bf16[32,4096]{1,0:T(8,128)(2,1)S(1)} custom-call(s32[192]{0:T(256)S(1)} %fusion.11.cols_ref, bf16[32,768,128]{2,1,0:T(8,128)(2,1)S(1)} %convert_weights.1.weights_ref.before_ref, bf16[32,4096]{1,0:T(8,128)(2,1)S(1)} %collective-permute-done.16.far_ref, bf16[32,4096]{1,0:T(8,128)(2,1)S(1)} %collective-permute-done.17.near_ref, ...), custom_call_target="tpu_custom_call" | custom-call | flops 201326592 | bytes 6291456 | tf_op jit(solution)/shard_map/apply_layer/pallas_call | solution.py:82
  82.9 6.0 %collective-permute-start.22 = (bf16[32,4096]{1,0:T(8,128)(2,1)S(1)}, bf16[32,4096]{1,0:T(8,128)(2,1)S(1)}, u32[]{:S(2)}, u32[]{:S(2)}) collective-permute-start(bf16[32,4096]{1,0:T(8,128)(2,1)S(1)} %apply_layer.22.before_ref), channel_id=1, source_target_pairs={{1,6},{2,5},{5,10},{6,9},{9,14},{10,13},{13,18},{14,17},{17,22},{1... | collective-permute-start | bytes 786440 | tf_op jit(solution)/shard_map/ppermute | solution.py:108
  92.9 2.0 %apply_layer.23.before_ref = bf16[24,4096]{1,0:T(8,128)(2,1)S(1)} custom-call(s32[192]{0:T(256)S(1)} %fusion.11.cols_ref, bf16[32,768,128]{2,1,0:T(8,128)(2,1)S(1)} %convert_weights.1.weights_ref.before_ref, bf16[24,4096]{1,0:T(8,128)(2,1)S(1)} %collective-permute-done.19.far_ref, bf16[24,4096]{1,0:T(8,128)(2,1)S(1)} %collective-permute-done.20.near_ref, ...), custom_call_target="tpu_custom_call" | custom-call | flops 150994944 | bytes 6291456 | tf_op jit(solution)/shard_map/apply_layer/pallas_call | solution.py:82
  94.9 2.8 %collective-permute-start.25 = (bf16[24,4096]{1,0:T(8,128)(2,1)S(1)}, bf16[24,4096]{1,0:T(8,128)(2,1)S(1)}, u32[]{:S(2)}, u32[]{:S(2)}) collective-permute-start(bf16[24,4096]{1,0:T(8,128)(2,1)S(1)} %apply_layer.23.before_ref), channel_id=1, source_target_pairs={{1,6},{2,5},{5,10},{6,9},{9,14},{10,13},{13,18},{14,17},{17,22},{1... | collective-permute-start | bytes 589832 | tf_op jit(solution)/shard_map/ppermute | solution.py:108
  101.7 2.1 %apply_layer.24.before_ref = bf16[32,4096]{1,0:T(8,128)(2,1)S(1)} custom-call(s32[192]{0:T(256)S(1)} %fusion.11.cols_ref, bf16[32,768,128]{2,1,0:T(8,128)(2,1)S(1)} %convert_weights.1.weights_ref.before_ref, bf16[32,4096]{1,0:T(8,128)(2,1)S(1)} %collective-permute-done.22.far_ref, bf16[32,4096]{1,0:T(8,128)(2,1)S(1)} %collective-permute-done.23.near_ref, ...), custom_call_target="tpu_custom_call" | custom-call | flops 201326592 | bytes 6291456 | tf_op jit(solution)/shard_map/apply_layer/pallas_call | solution.py:82
  103.8 5.7 %collective-permute-start.28 = (bf16[32,4096]{1,0:T(8,128)(2,1)S(1)}, bf16[32,4096]{1,0:T(8,128)(2,1)S(1)}, u32[]{:S(2)}, u32[]{:S(2)}) collective-permute-start(bf16[32,4096]{1,0:T(8,128)(2,1)S(1)} %apply_layer.24.before_ref), channel_id=1, source_target_pairs={{1,6},{2,5},{5,10},{6,9},{9,14},{10,13},{13,18},{14,17},{17,22},{1... | collective-permute-start | bytes 786440 | tf_op jit(solution)/shard_map/ppermute | solution.py:108
  113.3 2.0 %apply_layer.25.before_ref = bf16[24,4096]{1,0:T(8,128)(2,1)S(1)} custom-call(s32[192]{0:T(256)S(1)} %fusion.11.cols_ref, bf16[32,768,128]{2,1,0:T(8,128)(2,1)S(1)} %convert_weights.1.weights_ref.before_ref, bf16[24,4096]{1,0:T(8,128)(2,1)S(1)} %collective-permute-done.25.far_ref, bf16[24,4096]{1,0:T(8,128)(2,1)S(1)} %collective-permute-done.26.near_ref, ...), custom_call_target="tpu_custom_call" | custom-call | flops 150994944 | bytes 6291456 | tf_op jit(solution)/shard_map/apply_layer/pallas_call | solution.py:82
  115.4 2.8 %collective-permute-start.31 = (bf16[24,4096]{1,0:T(8,128)(2,1)S(1)}, bf16[24,4096]{1,0:T(8,128)(2,1)S(1)}, u32[]{:S(2)}, u32[]{:S(2)}) collective-permute-start(bf16[24,4096]{1,0:T(8,128)(2,1)S(1)} %apply_layer.25.before_ref), channel_id=1, source_target_pairs={{1,6},{2,5},{5,10},{6,9},{9,14},{10,13},{13,18},{14,17},{17,22},{1... | collective-permute-start | bytes 589832 | tf_op jit(solution)/shard_map/ppermute | solution.py:108
  122.2 2.1 %apply_layer.26.before_ref = bf16[32,4096]{1,0:T(8,128)(2,1)S(1)} custom-call(s32[192]{0:T(256)S(1)} %fusion.11.cols_ref, bf16[32,768,128]{2,1,0:T(8,128)(2,1)S(1)} %convert_weights.1.weights_ref.before_ref, bf16[32,4096]{1,0:T(8,128)(2,1)S(1)} %collective-permute-done.28.far_ref, bf16[32,4096]{1,0:T(8,128)(2,1)S(1)} %collective-permute-done.29.near_ref, ...), custom_call_target="tpu_custom_call" | custom-call | flops 201326592 | bytes 6291456 | tf_op jit(solution)/shard_map/apply_layer/pallas_call | solution.py:82
  124.2 5.7 %collective-permute-start.34 = (bf16[32,4096]{1,0:T(8,128)(2,1)S(1)}, bf16[32,4096]{1,0:T(8,128)(2,1)S(1)}, u32[]{:S(2)}, u32[]{:S(2)}) collective-permute-start(bf16[32,4096]{1,0:T(8,128)(2,1)S(1)} %apply_layer.26.before_ref), channel_id=1, source_target_pairs={{1,6},{2,5},{5,10},{6,9},{9,14},{10,13},{13,18},{14,17},{17,22},{1... | collective-permute-start | bytes 786440 | tf_op jit(solution)/shard_map/ppermute | solution.py:108
  136.0 2.8 %collective-permute-start.37 = (bf16[24,4096]{1,0:T(8,128)(2,1)S(1)}, bf16[24,4096]{1,0:T(8,128)(2,1)S(1)}, u32[]{:S(2)}, u32[]{:S(2)}) collective-permute-start(bf16[24,4096]{1,0:T(8,128)(2,1)S(1)} %apply_layer.27.before_ref), channel_id=1, source_target_pairs={{1,6},{2,5},{5,10},{6,9},{9,14},{10,13},{13,18},{14,17},{17,22},{1... | collective-permute-start | bytes 589832 | tf_op jit(solution)/shard_map/ppermute | solution.py:108
  142.7 2.1 %apply_layer.28.before_ref = bf16[32,4096]{1,0:T(8,128)(2,1)S(1)} custom-call(s32[192]{0:T(256)S(1)} %fusion.11.cols_ref, bf16[32,768,128]{2,1,0:T(8,128)(2,1)S(1)} %convert_weights.1.weights_ref.before_ref, bf16[32,4096]{1,0:T(8,128)(2,1)S(1)} %collective-permute-done.34.far_ref, bf16[32,4096]{1,0:T(8,128)(2,1)S(1)} %collective-permute-done.35.near_ref, ...), custom_call_target="tpu_custom_call" | custom-call | flops 201326592 | bytes 6291456 | tf_op jit(solution)/shard_map/apply_layer/pallas_call | solution.py:82
  144.8 5.8 %collective-permute-start.40 = (bf16[32,4096]{1,0:T(8,128)(2,1)S(1)}, bf16[32,4096]{1,0:T(8,128)(2,1)S(1)}, u32[]{:S(2)}, u32[]{:S(2)}) collective-permute-start(bf16[32,4096]{1,0:T(8,128)(2,1)S(1)} %apply_layer.28.before_ref), channel_id=1, source_target_pairs={{1,6},{2,5},{5,10},{6,9},{9,14},{10,13},{13,18},{14,17},{17,22},{1... | collective-permute-start | bytes 786440 | tf_op jit(solution)/shard_map/ppermute | solution.py:108
  154.5 2.0 %apply_layer.29.before_ref = bf16[24,4096]{1,0:T(8,128)(2,1)S(1)} custom-call(s32[192]{0:T(256)S(1)} %fusion.11.cols_ref, bf16[32,768,128]{2,1,0:T(8,128)(2,1)S(1)} %convert_weights.1.weights_ref.before_ref, bf16[24,4096]{1,0:T(8,128)(2,1)S(1)} %collective-permute-done.37.far_ref, bf16[24,4096]{1,0:T(8,128)(2,1)S(1)} %collective-permute-done.38.near_ref, ...), custom_call_target="tpu_custom_call" | custom-call | flops 150994944 | bytes 6291456 | tf_op jit(solution)/shard_map/apply_layer/pallas_call | solution.py:82
  156.5 2.8 %collective-permute-start.43 = (bf16[24,4096]{1,0:T(8,128)(2,1)S(1)}, bf16[24,4096]{1,0:T(8,128)(2,1)S(1)}, u32[]{:S(2)}, u32[]{:S(2)}) collective-permute-start(bf16[24,4096]{1,0:T(8,128)(2,1)S(1)} %apply_layer.29.before_ref), channel_id=1, source_target_pairs={{1,6},{2,5},{5,10},{6,9},{9,14},{10,13},{13,18},{14,17},{17,22},{1... | collective-permute-start | bytes 589832 | tf_op jit(solution)/shard_map/ppermute | solution.py:108
  163.3 2.1 %apply_layer.30.before_ref = bf16[32,4096]{1,0:T(8,128)(2,1)S(1)} custom-call(s32[192]{0:T(256)S(1)} %fusion.11.cols_ref, bf16[32,768,128]{2,1,0:T(8,128)(2,1)S(1)} %convert_weights.1.weights_ref.before_ref, bf16[32,4096]{1,0:T(8,128)(2,1)S(1)} %collective-permute-done.40.far_ref, bf16[32,4096]{1,0:T(8,128)(2,1)S(1)} %collective-permute-done.41.near_ref, ...), custom_call_target="tpu_custom_call" | custom-call | flops 201326592 | bytes 6291456 | tf_op jit(solution)/shard_map/apply_layer/pallas_call | solution.py:82
  165.4 3.2 %collective-permute-done.43.far_ref = bf16[24,4096]{1,0:T(8,128)(2,1)S(1)} collective-permute-done((bf16[24,4096]{1,0:T(8,128)(2,1)S(1)}, bf16[24,4096]{1,0:T(8,128)(2,1)S(1)}, u32[]{:S(2)}, u32[]{:S(2)}) %collective-permute-start.43) | collective-permute-done | bytes 196640 | tf_op jit(solution)/shard_map/ppermute | solution.py:108
  168.8 2.0 %apply_layer.31 = bf16[24,4096]{1,0:T(8,128)(2,1)S(1)} custom-call(s32[192]{0:T(256)S(1)} %fusion.11.cols_ref, bf16[32,768,128]{2,1,0:T(8,128)(2,1)S(1)} %convert_weights.1.weights_ref.before_ref, bf16[24,4096]{1,0:T(8,128)(2,1)S(1)} %collective-permute-done.43.far_ref, bf16[24,4096]{1,0:T(8,128)(2,1)S(1)} %collective-permute-done.44.near_ref, ...), custom_call_target="tpu_custom_call" | custom-call | flops 150994944 | bytes 6291456 | tf_op jit(solution)/shard_map/apply_layer/pallas_call | solution.py:82
  (94 shorter events, 63.2 us)
Async XLA Ops:
  1.0 14.1 %collective-permute-start = (bf16[32,4096]{1,0:T(8,128)(2,1)S(1)}, bf16[32,4096]{1,0:T(8,128)(2,1)S(1)}, u32[]{:S(2)}, u32[]{:S(2)}) collective-permute-start(bf16[32,4096]{1,0:T(8,128)(2,1)S(1)} %slice_bitcast_fusion.own_ref), channel_id=1, source_target_pairs={{1,2},{2,1},{5,6},{6,5},{9,10},{10,9},{13,14},{14,13},{17,18},{18,... | collective-permute-start | bytes 786440 | tf_op jit(solution)/shard_map/ppermute | solution.py:108
  5.1 22.1 %collective-permute-start.2 = (bf16[24,4096]{1,0:T(8,128)(2,1)S(1)}, bf16[24,4096]{1,0:T(8,128)(2,1)S(1)}, u32[]{:S(2)}, u32[]{:S(2)}) collective-permute-start(bf16[24,4096]{1,0:T(8,128)(2,1)S(1)} %slice_bitcast_fusion.1.own_ref), channel_id=1, source_target_pairs={{1,2},{2,1},{5,6},{6,5},{9,10},{10,9},{13,14},{14,13},{17,18},{18,... | collective-permute-start | bytes 589832 | tf_op jit(solution)/shard_map/ppermute | solution.py:108
  8.2 19.1 %collective-permute-start.3 = (bf16[24,4096]{1,0:T(8,128)(2,1)S(1)}, bf16[24,4096]{1,0:T(8,128)(2,1)S(1)}, u32[]{:S(2)}, u32[]{:S(2)}) collective-permute-start(bf16[24,4096]{1,0:T(8,128)(2,1)S(1)} %slice_bitcast_fusion.1.own_ref), channel_id=1, source_target_pairs={{0,1},{1,0},{2,3},{3,2},{4,5},{5,4},{6,7},{7,6},{8,9},{9,8},{10,11... | collective-permute-start | bytes 589832 | tf_op jit(solution)/shard_map/ppermute | solution.py:108
  17.2 21.0 %collective-permute-start.4 = (bf16[32,4096]{1,0:T(8,128)(2,1)S(1)}, bf16[32,4096]{1,0:T(8,128)(2,1)S(1)}, u32[]{:S(2)}, u32[]{:S(2)}) collective-permute-start(bf16[32,4096]{1,0:T(8,128)(2,1)S(1)} %apply_layer.16.before_ref), channel_id=1, source_target_pairs={{1,6},{2,5},{5,10},{6,9},{9,14},{10,13},{13,18},{14,17},{17,22},{1... | collective-permute-start | bytes 786440 | tf_op jit(solution)/shard_map/ppermute | solution.py:108
  23.4 16.8 %collective-permute-start.5 = (bf16[32,4096]{1,0:T(8,128)(2,1)S(1)}, bf16[32,4096]{1,0:T(8,128)(2,1)S(1)}, u32[]{:S(2)}, u32[]{:S(2)}) collective-permute-start(bf16[32,4096]{1,0:T(8,128)(2,1)S(1)} %apply_layer.16.before_ref), channel_id=1, source_target_pairs={{0,5},{1,4},{2,7},{3,6},{4,9},{5,8},{6,11},{7,10},{8,13},{9,12},{1... | collective-permute-start | bytes 786440 | tf_op jit(solution)/shard_map/ppermute | solution.py:108
  25.3 14.8 %collective-permute-start.6 = (bf16[32,4096]{1,0:T(8,128)(2,1)S(1)}, bf16[32,4096]{1,0:T(8,128)(2,1)S(1)}, u32[]{:S(2)}, u32[]{:S(2)}) collective-permute-start(bf16[32,4096]{1,0:T(8,128)(2,1)S(1)} %apply_layer.16.before_ref), channel_id=1, source_target_pairs={{0,4},{1,5},{2,6},{3,7},{4,8},{5,9},{6,10},{7,11},{8,12},{9,13},{1... | collective-permute-start | bytes 786440 | tf_op jit(solution)/shard_map/ppermute | solution.py:108
  29.3 19.4 %collective-permute-start.7 = (bf16[24,4096]{1,0:T(8,128)(2,1)S(1)}, bf16[24,4096]{1,0:T(8,128)(2,1)S(1)}, u32[]{:S(2)}, u32[]{:S(2)}) collective-permute-start(bf16[24,4096]{1,0:T(8,128)(2,1)S(1)} %apply_layer.17.before_ref), channel_id=1, source_target_pairs={{1,6},{2,5},{5,10},{6,9},{9,14},{10,13},{13,18},{14,17},{17,22},{1... | collective-permute-start | bytes 589832 | tf_op jit(solution)/shard_map/ppermute | solution.py:108
  36.3 14.5 %collective-permute-start.8 = (bf16[24,4096]{1,0:T(8,128)(2,1)S(1)}, bf16[24,4096]{1,0:T(8,128)(2,1)S(1)}, u32[]{:S(2)}, u32[]{:S(2)}) collective-permute-start(bf16[24,4096]{1,0:T(8,128)(2,1)S(1)} %apply_layer.17.before_ref), channel_id=1, source_target_pairs={{0,5},{1,4},{2,7},{3,6},{4,9},{5,8},{6,11},{7,10},{8,13},{9,12},{1... | collective-permute-start | bytes 589832 | tf_op jit(solution)/shard_map/ppermute | solution.py:108
  42.3 15.4 %collective-permute-start.10 = (bf16[32,4096]{1,0:T(8,128)(2,1)S(1)}, bf16[32,4096]{1,0:T(8,128)(2,1)S(1)}, u32[]{:S(2)}, u32[]{:S(2)}) collective-permute-start(bf16[32,4096]{1,0:T(8,128)(2,1)S(1)} %apply_layer.18.before_ref), channel_id=1, source_target_pairs={{1,6},{2,5},{5,10},{6,9},{9,14},{10,13},{13,18},{14,17},{17,22},{1... | collective-permute-start | bytes 786440 | tf_op jit(solution)/shard_map/ppermute | solution.py:108
  46.8 12.8 %collective-permute-start.11 = (bf16[32,4096]{1,0:T(8,128)(2,1)S(1)}, bf16[32,4096]{1,0:T(8,128)(2,1)S(1)}, u32[]{:S(2)}, u32[]{:S(2)}) collective-permute-start(bf16[32,4096]{1,0:T(8,128)(2,1)S(1)} %apply_layer.18.before_ref), channel_id=1, source_target_pairs={{0,5},{1,4},{2,7},{3,6},{4,9},{5,8},{6,11},{7,10},{8,13},{9,12},{1... | collective-permute-start | bytes 786440 | tf_op jit(solution)/shard_map/ppermute | solution.py:108
  52.9 17.4 %collective-permute-start.13 = (bf16[24,4096]{1,0:T(8,128)(2,1)S(1)}, bf16[24,4096]{1,0:T(8,128)(2,1)S(1)}, u32[]{:S(2)}, u32[]{:S(2)}) collective-permute-start(bf16[24,4096]{1,0:T(8,128)(2,1)S(1)} %apply_layer.19.before_ref), channel_id=1, source_target_pairs={{1,6},{2,5},{5,10},{6,9},{9,14},{10,13},{13,18},{14,17},{17,22},{1... | collective-permute-start | bytes 589832 | tf_op jit(solution)/shard_map/ppermute | solution.py:108
  55.7 16.6 %collective-permute-start.14 = (bf16[24,4096]{1,0:T(8,128)(2,1)S(1)}, bf16[24,4096]{1,0:T(8,128)(2,1)S(1)}, u32[]{:S(2)}, u32[]{:S(2)}) collective-permute-start(bf16[24,4096]{1,0:T(8,128)(2,1)S(1)} %apply_layer.19.before_ref), channel_id=1, source_target_pairs={{0,5},{1,4},{2,7},{3,6},{4,9},{5,8},{6,11},{7,10},{8,13},{9,12},{1... | collective-permute-start | bytes 589832 | tf_op jit(solution)/shard_map/ppermute | solution.py:108
  57.6 14.6 %collective-permute-start.15 = (bf16[24,4096]{1,0:T(8,128)(2,1)S(1)}, bf16[24,4096]{1,0:T(8,128)(2,1)S(1)}, u32[]{:S(2)}, u32[]{:S(2)}) collective-permute-start(bf16[24,4096]{1,0:T(8,128)(2,1)S(1)} %apply_layer.19.before_ref), channel_id=1, source_target_pairs={{0,4},{1,5},{2,6},{3,7},{4,8},{5,9},{6,10},{7,11},{8,12},{9,13},{1... | collective-permute-start | bytes 589832 | tf_op jit(solution)/shard_map/ppermute | solution.py:108
  61.7 17.2 %collective-permute-start.16 = (bf16[32,4096]{1,0:T(8,128)(2,1)S(1)}, bf16[32,4096]{1,0:T(8,128)(2,1)S(1)}, u32[]{:S(2)}, u32[]{:S(2)}) collective-permute-start(bf16[32,4096]{1,0:T(8,128)(2,1)S(1)} %apply_layer.20.before_ref), channel_id=1, source_target_pairs={{1,6},{2,5},{5,10},{6,9},{9,14},{10,13},{13,18},{14,17},{17,22},{1... | collective-permute-start | bytes 786440 | tf_op jit(solution)/shard_map/ppermute | solution.py:108
  74.3 16.5 %collective-permute-start.19 = (bf16[24,4096]{1,0:T(8,128)(2,1)S(1)}, bf16[24,4096]{1,0:T(8,128)(2,1)S(1)}, u32[]{:S(2)}, u32[]{:S(2)}) collective-permute-start(bf16[24,4096]{1,0:T(8,128)(2,1)S(1)} %apply_layer.21.before_ref), channel_id=1, source_target_pairs={{1,6},{2,5},{5,10},{6,9},{9,14},{10,13},{13,18},{14,17},{17,22},{1... | collective-permute-start | bytes 589832 | tf_op jit(solution)/shard_map/ppermute | solution.py:108
  76.9 15.9 %collective-permute-start.20 = (bf16[24,4096]{1,0:T(8,128)(2,1)S(1)}, bf16[24,4096]{1,0:T(8,128)(2,1)S(1)}, u32[]{:S(2)}, u32[]{:S(2)}) collective-permute-start(bf16[24,4096]{1,0:T(8,128)(2,1)S(1)} %apply_layer.21.before_ref), channel_id=1, source_target_pairs={{0,5},{1,4},{2,7},{3,6},{4,9},{5,8},{6,11},{7,10},{8,13},{9,12},{1... | collective-permute-start | bytes 589832 | tf_op jit(solution)/shard_map/ppermute | solution.py:108
  78.9 14.0 %collective-permute-start.21 = (bf16[24,4096]{1,0:T(8,128)(2,1)S(1)}, bf16[24,4096]{1,0:T(8,128)(2,1)S(1)}, u32[]{:S(2)}, u32[]{:S(2)}) collective-permute-start(bf16[24,4096]{1,0:T(8,128)(2,1)S(1)} %apply_layer.21.before_ref), channel_id=1, source_target_pairs={{0,4},{1,5},{2,6},{3,7},{4,8},{5,9},{6,10},{7,11},{8,12},{9,13},{1... | collective-permute-start | bytes 589832 | tf_op jit(solution)/shard_map/ppermute | solution.py:108
  82.9 16.8 %collective-permute-start.22 = (bf16[32,4096]{1,0:T(8,128)(2,1)S(1)}, bf16[32,4096]{1,0:T(8,128)(2,1)S(1)}, u32[]{:S(2)}, u32[]{:S(2)}) collective-permute-start(bf16[32,4096]{1,0:T(8,128)(2,1)S(1)} %apply_layer.22.before_ref), channel_id=1, source_target_pairs={{1,6},{2,5},{5,10},{6,9},{9,14},{10,13},{13,18},{14,17},{17,22},{1... | collective-permute-start | bytes 786440 | tf_op jit(solution)/shard_map/ppermute | solution.py:108
  88.9 12.7 %collective-permute-start.23 = (bf16[32,4096]{1,0:T(8,128)(2,1)S(1)}, bf16[32,4096]{1,0:T(8,128)(2,1)S(1)}, u32[]{:S(2)}, u32[]{:S(2)}) collective-permute-start(bf16[32,4096]{1,0:T(8,128)(2,1)S(1)} %apply_layer.22.before_ref), channel_id=1, source_target_pairs={{0,5},{1,4},{2,7},{3,6},{4,9},{5,8},{6,11},{7,10},{8,13},{9,12},{1... | collective-permute-start | bytes 786440 | tf_op jit(solution)/shard_map/ppermute | solution.py:108
  94.9 16.5 %collective-permute-start.25 = (bf16[24,4096]{1,0:T(8,128)(2,1)S(1)}, bf16[24,4096]{1,0:T(8,128)(2,1)S(1)}, u32[]{:S(2)}, u32[]{:S(2)}) collective-permute-start(bf16[24,4096]{1,0:T(8,128)(2,1)S(1)} %apply_layer.23.before_ref), channel_id=1, source_target_pairs={{1,6},{2,5},{5,10},{6,9},{9,14},{10,13},{13,18},{14,17},{17,22},{1... | collective-permute-start | bytes 589832 | tf_op jit(solution)/shard_map/ppermute | solution.py:108
  97.7 15.6 %collective-permute-start.26 = (bf16[24,4096]{1,0:T(8,128)(2,1)S(1)}, bf16[24,4096]{1,0:T(8,128)(2,1)S(1)}, u32[]{:S(2)}, u32[]{:S(2)}) collective-permute-start(bf16[24,4096]{1,0:T(8,128)(2,1)S(1)} %apply_layer.23.before_ref), channel_id=1, source_target_pairs={{0,5},{1,4},{2,7},{3,6},{4,9},{5,8},{6,11},{7,10},{8,13},{9,12},{1... | collective-permute-start | bytes 589832 | tf_op jit(solution)/shard_map/ppermute | solution.py:108
  99.7 13.7 %collective-permute-start.27 = (bf16[24,4096]{1,0:T(8,128)(2,1)S(1)}, bf16[24,4096]{1,0:T(8,128)(2,1)S(1)}, u32[]{:S(2)}, u32[]{:S(2)}) collective-permute-start(bf16[24,4096]{1,0:T(8,128)(2,1)S(1)} %apply_layer.23.before_ref), channel_id=1, source_target_pairs={{0,4},{1,5},{2,6},{3,7},{4,8},{5,9},{6,10},{7,11},{8,12},{9,13},{1... | collective-permute-start | bytes 589832 | tf_op jit(solution)/shard_map/ppermute | solution.py:108
  103.8 16.4 %collective-permute-start.28 = (bf16[32,4096]{1,0:T(8,128)(2,1)S(1)}, bf16[32,4096]{1,0:T(8,128)(2,1)S(1)}, u32[]{:S(2)}, u32[]{:S(2)}) collective-permute-start(bf16[32,4096]{1,0:T(8,128)(2,1)S(1)} %apply_layer.24.before_ref), channel_id=1, source_target_pairs={{1,6},{2,5},{5,10},{6,9},{9,14},{10,13},{13,18},{14,17},{17,22},{1... | collective-permute-start | bytes 786440 | tf_op jit(solution)/shard_map/ppermute | solution.py:108
  109.5 12.7 %collective-permute-start.29 = (bf16[32,4096]{1,0:T(8,128)(2,1)S(1)}, bf16[32,4096]{1,0:T(8,128)(2,1)S(1)}, u32[]{:S(2)}, u32[]{:S(2)}) collective-permute-start(bf16[32,4096]{1,0:T(8,128)(2,1)S(1)} %apply_layer.24.before_ref), channel_id=1, source_target_pairs={{0,5},{1,4},{2,7},{3,6},{4,9},{5,8},{6,11},{7,10},{8,13},{9,12},{1... | collective-permute-start | bytes 786440 | tf_op jit(solution)/shard_map/ppermute | solution.py:108
  115.4 16.6 %collective-permute-start.31 = (bf16[24,4096]{1,0:T(8,128)(2,1)S(1)}, bf16[24,4096]{1,0:T(8,128)(2,1)S(1)}, u32[]{:S(2)}, u32[]{:S(2)}) collective-permute-start(bf16[24,4096]{1,0:T(8,128)(2,1)S(1)} %apply_layer.25.before_ref), channel_id=1, source_target_pairs={{1,6},{2,5},{5,10},{6,9},{9,14},{10,13},{13,18},{14,17},{17,22},{1... | collective-permute-start | bytes 589832 | tf_op jit(solution)/shard_map/ppermute | solution.py:108
  118.3 15.6 %collective-permute-start.32 = (bf16[24,4096]{1,0:T(8,128)(2,1)S(1)}, bf16[24,4096]{1,0:T(8,128)(2,1)S(1)}, u32[]{:S(2)}, u32[]{:S(2)}) collective-permute-start(bf16[24,4096]{1,0:T(8,128)(2,1)S(1)} %apply_layer.25.before_ref), channel_id=1, source_target_pairs={{0,5},{1,4},{2,7},{3,6},{4,9},{5,8},{6,11},{7,10},{8,13},{9,12},{1... | collective-permute-start | bytes 589832 | tf_op jit(solution)/shard_map/ppermute | solution.py:108
  120.2 13.7 %collective-permute-start.33 = (bf16[24,4096]{1,0:T(8,128)(2,1)S(1)}, bf16[24,4096]{1,0:T(8,128)(2,1)S(1)}, u32[]{:S(2)}, u32[]{:S(2)}) collective-permute-start(bf16[24,4096]{1,0:T(8,128)(2,1)S(1)} %apply_layer.25.before_ref), channel_id=1, source_target_pairs={{0,4},{1,5},{2,6},{3,7},{4,8},{5,9},{6,10},{7,11},{8,12},{9,13},{1... | collective-permute-start | bytes 589832 | tf_op jit(solution)/shard_map/ppermute | solution.py:108
  124.2 16.5 %collective-permute-start.34 = (bf16[32,4096]{1,0:T(8,128)(2,1)S(1)}, bf16[32,4096]{1,0:T(8,128)(2,1)S(1)}, u32[]{:S(2)}, u32[]{:S(2)}) collective-permute-start(bf16[32,4096]{1,0:T(8,128)(2,1)S(1)} %apply_layer.26.before_ref), channel_id=1, source_target_pairs={{1,6},{2,5},{5,10},{6,9},{9,14},{10,13},{13,18},{14,17},{17,22},{1... | collective-permute-start | bytes 786440 | tf_op jit(solution)/shard_map/ppermute | solution.py:108
  136.0 16.6 %collective-permute-start.37 = (bf16[24,4096]{1,0:T(8,128)(2,1)S(1)}, bf16[24,4096]{1,0:T(8,128)(2,1)S(1)}, u32[]{:S(2)}, u32[]{:S(2)}) collective-permute-start(bf16[24,4096]{1,0:T(8,128)(2,1)S(1)} %apply_layer.27.before_ref), channel_id=1, source_target_pairs={{1,6},{2,5},{5,10},{6,9},{9,14},{10,13},{13,18},{14,17},{17,22},{1... | collective-permute-start | bytes 589832 | tf_op jit(solution)/shard_map/ppermute | solution.py:108
  138.8 15.7 %collective-permute-start.38 = (bf16[24,4096]{1,0:T(8,128)(2,1)S(1)}, bf16[24,4096]{1,0:T(8,128)(2,1)S(1)}, u32[]{:S(2)}, u32[]{:S(2)}) collective-permute-start(bf16[24,4096]{1,0:T(8,128)(2,1)S(1)} %apply_layer.27.before_ref), channel_id=1, source_target_pairs={{0,5},{1,4},{2,7},{3,6},{4,9},{5,8},{6,11},{7,10},{8,13},{9,12},{1... | collective-permute-start | bytes 589832 | tf_op jit(solution)/shard_map/ppermute | solution.py:108
  140.8 13.7 %collective-permute-start.39 = (bf16[24,4096]{1,0:T(8,128)(2,1)S(1)}, bf16[24,4096]{1,0:T(8,128)(2,1)S(1)}, u32[]{:S(2)}, u32[]{:S(2)}) collective-permute-start(bf16[24,4096]{1,0:T(8,128)(2,1)S(1)} %apply_layer.27.before_ref), channel_id=1, source_target_pairs={{0,4},{1,5},{2,6},{3,7},{4,8},{5,9},{6,10},{7,11},{8,12},{9,13},{1... | collective-permute-start | bytes 589832 | tf_op jit(solution)/shard_map/ppermute | solution.py:108
  144.8 16.5 %collective-permute-start.40 = (bf16[32,4096]{1,0:T(8,128)(2,1)S(1)}, bf16[32,4096]{1,0:T(8,128)(2,1)S(1)}, u32[]{:S(2)}, u32[]{:S(2)}) collective-permute-start(bf16[32,4096]{1,0:T(8,128)(2,1)S(1)} %apply_layer.28.before_ref), channel_id=1, source_target_pairs={{1,6},{2,5},{5,10},{6,9},{9,14},{10,13},{13,18},{14,17},{17,22},{1... | collective-permute-start | bytes 786440 | tf_op jit(solution)/shard_map/ppermute | solution.py:108
  (16 other events, 162.5 us)
where the time goes:
time: 176 us; the launch traced here: 173 us
  starting transfers between devices  125 us (71%)
  Pallas kernels  38.8 us (22%)
  local copies, waits for them, and re-layouts  4.62 us (3%)
  waiting for transfers between devices  3.47 us (2%)
    ppermute x46, starting transfers between devices, send(): return lax.ppermute(value, ('layer', 'row'), pairs)  125 us
    pallas_call x16, Pallas kernels, apply_layer(): pl.pallas_call(functools.partial(tick_kernel, tick, first), in_specs=[pl....  32.9 us
    pallas_call x1, Pallas kernels, convert_weights(): pl.pallas_call(convert_kernel, in_specs=[pl.BlockSpec(memory_space=pltpu....  5.89 us
  transfers between devices with their start and end apart: 46, of which 2 were waited for; matrix products, arithmetic and copies ran while one was open for 1% of the time, Pallas kernels for 21%

commit v1 on v0

--- a/solution.py
+++ b/solution.py
@@ -54,7 +54,7 @@
     )(prop)
 
 
-def tick_kernel(tick, first, cols_ref, weights_ref, far_ref, near_ref, own_ref, source_ref, before_ref, out_ref, window):
+def tick_kernel(tick, first, cols_ref, weights_ref, near_ref, far_ref, own_ref, source_ref, before_ref, out_ref, window):
     del before_ref
     shots, width = own_ref.shape
     row_blocks, depth, blk = weights_ref.shape
@@ -73,10 +73,10 @@
         out_ref[:, here] = (mixed + source_ref[tick, 0, first:first + shots, here].astype(jnp.float32)).astype(out_ref.dtype)
         return carry
 
-    lax.fori_loop(0, row_blocks, step, 0, unroll=8)
+    lax.fori_loop(0, row_blocks, step, 0, unroll=min(16, row_blocks))
 
 
-def apply_layer(tick, first, cols, weights, far, near, own, sources, before):
+def apply_layer(tick, first, cols, weights, near, far, own, sources, before):
     shots, width = own.shape
     vmem = pl.BlockSpec(memory_space=pltpu.VMEM)
     return pl.pallas_call(
@@ -90,7 +90,7 @@
             flops=2 * shots * weights.size, bytes_accessed=weights.size * 2, transcendentals=0
         ),
         name="apply_layer",
-    )(cols, weights, far, near, own, sources, before)
+    )(cols, weights, near, far, own, sources, before)
 
 
 def partner(r, rows, far):
@@ -125,8 +125,8 @@
     arriving = []
     for a, b in panels:
         own = incoming[0, a:b]
-        distant = send(own, layers, 0, far)
-        arriving.append((distant, send(own, layers, 0, near), own))
+        beside = send(own, layers, 0, near)
+        arriving.append((beside, send(own, layers, 0, far), own))
     weights = convert_weights(jnp.transpose(propagator[0], (1, 0, 2)))
     before = weights
     history = []
@@ -137,9 +137,9 @@
             before = done
             produced.append(done)
             if tick + 1 < ticks:
+                beside = send(done, layers, 1, near)
                 distant = send(done, layers, 1, far)
-                beside = send(done, layers, 1, near)
-                arriving[i] = (distant, beside, send(done, layers, 1, range(rows)))
+                arriving[i] = (beside, distant, send(done, layers, 1, range(rows)))
         history.append(jnp.concatenate(produced, axis=0))
     return jnp.stack(history)[:, None]
 

time: 176 us -> 170 us (0.966); the launches traced: 173 us -> 169 us
  Pallas kernels: 38.8 us -> 34.4 us
    pallas_call x16, Pallas kernels: 32.9 us -> 28.6 us  [apply_layer(): pl.pallas_call(functools.partial(tick_kernel, tick, first), in_specs=[pl....]
  transfers between devices with their start and end apart: 46 -> 46, of which waited for: 2 -> 2; matrix products, arithmetic and copies ran while one was open for 1% -> 1% of each run, Pallas kernels for 21% -> 19%
where the time goes in v1:
time: 170 us; the launch traced here: 169 us
  starting transfers between devices  124 us (73%)
  Pallas kernels  34.4 us (20%)
  local copies, waits for them, and re-layouts  4.62 us (3%)
  waiting for transfers between devices  3.95 us (2%)
    ppermute x46, starting transfers between devices, send(): return lax.ppermute(value, ('layer', 'row'), pairs)  124 us
    pallas_call x16, Pallas kernels, apply_layer(): pl.pallas_call(functools.partial(tick_kernel, tick, first), in_specs=[pl....  28.6 us
    pallas_call x1, Pallas kernels, convert_weights(): pl.pallas_call(convert_kernel, in_specs=[pl.BlockSpec(memory_space=pltpu....  5.89 us
    ppermute x46, waiting for transfers between devices, send(): return lax.ppermute(value, ('layer', 'row'), pairs)  3.95 us
  transfers between devices with their start and end apart: 46, of which 2 were waited for; matrix products, arithmetic and copies ran while one was open for 1% of the time, Pallas kernels for 19%

profile of v1, /device:TPU:11, one launch (start us, length us, event | category | flops | bytes accessed | tf_op | source)
XLA Modules:
  0.0 168.5 jit_solution(2247207830935916570)
XLA Ops:
  1.3 4.1 %collective-permute-start.1 = (bf16[32,4096]{1,0:T(8,128)(2,1)S(1)}, bf16[32,4096]{1,0:T(8,128)(2,1)S(1)}, u32[]{:S(2)}, u32[]{:S(2)}) collective-permute-start(bf16[32,4096]{1,0:T(8,128)(2,1)S(1)} %slice_bitcast_fusion.own_ref), channel_id=1, source_target_pairs={{1,2},{2,1},{5,6},{6,5},{9,10},{10,9},{13,14},{14,13},{17,18},{18,... | collective-permute-start | bytes 786440 | tf_op jit(solution)/shard_map/ppermute | solution.py:108
  6.4 2.1 %collective-permute-start.3 = (bf16[24,4096]{1,0:T(8,128)(2,1)S(1)}, bf16[24,4096]{1,0:T(8,128)(2,1)S(1)}, u32[]{:S(2)}, u32[]{:S(2)}) collective-permute-start(bf16[24,4096]{1,0:T(8,128)(2,1)S(1)} %slice_bitcast_fusion.1.own_ref), channel_id=1, source_target_pairs={{1,2},{2,1},{5,6},{6,5},{9,10},{10,9},{13,14},{14,13},{17,18},{18,... | collective-permute-start | bytes 589832 | tf_op jit(solution)/shard_map/ppermute | solution.py:108
  9.4 5.9 %convert_weights.1.weights_ref.before_ref = bf16[32,768,128]{2,1,0:T(8,128)(2,1)S(1)} custom-call(f32[6,4096,128]{2,1,0:T(8,128)} %bitcast.42), custom_call_target="tpu_custom_call" | custom-call | bytes 12582912 | tf_op jit(solution)/shard_map/convert_weights/pallas_call | solution.py:42
  17.2 4.3 %collective-permute-start.4 = (bf16[32,4096]{1,0:T(8,128)(2,1)S(1)}, bf16[32,4096]{1,0:T(8,128)(2,1)S(1)}, u32[]{:S(2)}, u32[]{:S(2)}) collective-permute-start(bf16[32,4096]{1,0:T(8,128)(2,1)S(1)} %apply_layer.16.before_ref), channel_id=1, source_target_pairs={{0,5},{1,4},{2,7},{3,6},{4,9},{5,8},{6,11},{7,10},{8,13},{9,12},{1... | collective-permute-start | bytes 786440 | tf_op jit(solution)/shard_map/ppermute | solution.py:108
  21.5 4.1 %collective-permute-start.5 = (bf16[32,4096]{1,0:T(8,128)(2,1)S(1)}, bf16[32,4096]{1,0:T(8,128)(2,1)S(1)}, u32[]{:S(2)}, u32[]{:S(2)}) collective-permute-start(bf16[32,4096]{1,0:T(8,128)(2,1)S(1)} %apply_layer.16.before_ref), channel_id=1, source_target_pairs={{1,6},{2,5},{5,10},{6,9},{9,14},{10,13},{13,18},{14,17},{17,22},{1... | collective-permute-start | bytes 786440 | tf_op jit(solution)/shard_map/ppermute | solution.py:108
  29.3 2.0 %collective-permute-start.7 = (bf16[24,4096]{1,0:T(8,128)(2,1)S(1)}, bf16[24,4096]{1,0:T(8,128)(2,1)S(1)}, u32[]{:S(2)}, u32[]{:S(2)}) collective-permute-start(bf16[24,4096]{1,0:T(8,128)(2,1)S(1)} %apply_layer.17.before_ref), channel_id=1, source_target_pairs={{0,5},{1,4},{2,7},{3,6},{4,9},{5,8},{6,11},{7,10},{8,13},{9,12},{1... | collective-permute-start | bytes 589832 | tf_op jit(solution)/shard_map/ppermute | solution.py:108
  31.3 4.1 %collective-permute-start.8 = (bf16[24,4096]{1,0:T(8,128)(2,1)S(1)}, bf16[24,4096]{1,0:T(8,128)(2,1)S(1)}, u32[]{:S(2)}, u32[]{:S(2)}) collective-permute-start(bf16[24,4096]{1,0:T(8,128)(2,1)S(1)} %apply_layer.17.before_ref), channel_id=1, source_target_pairs={{1,6},{2,5},{5,10},{6,9},{9,14},{10,13},{13,18},{14,17},{17,22},{1... | collective-permute-start | bytes 589832 | tf_op jit(solution)/shard_map/ppermute | solution.py:108
  35.4 2.1 %collective-permute-start.9 = (bf16[24,4096]{1,0:T(8,128)(2,1)S(1)}, bf16[24,4096]{1,0:T(8,128)(2,1)S(1)}, u32[]{:S(2)}, u32[]{:S(2)}) collective-permute-start(bf16[24,4096]{1,0:T(8,128)(2,1)S(1)} %apply_layer.17.before_ref), channel_id=1, source_target_pairs={{0,4},{1,5},{2,6},{3,7},{4,8},{5,9},{6,10},{7,11},{8,12},{9,13},{1... | collective-permute-start | bytes 589832 | tf_op jit(solution)/shard_map/ppermute | solution.py:108
  39.3 2.1 %collective-permute-start.10 = (bf16[32,4096]{1,0:T(8,128)(2,1)S(1)}, bf16[32,4096]{1,0:T(8,128)(2,1)S(1)}, u32[]{:S(2)}, u32[]{:S(2)}) collective-permute-start(bf16[32,4096]{1,0:T(8,128)(2,1)S(1)} %apply_layer.18.before_ref), channel_id=1, source_target_pairs={{0,5},{1,4},{2,7},{3,6},{4,9},{5,8},{6,11},{7,10},{8,13},{9,12},{1... | collective-permute-start | bytes 786440 | tf_op jit(solution)/shard_map/ppermute | solution.py:108
  41.4 4.1 %collective-permute-start.11 = (bf16[32,4096]{1,0:T(8,128)(2,1)S(1)}, bf16[32,4096]{1,0:T(8,128)(2,1)S(1)}, u32[]{:S(2)}, u32[]{:S(2)}) collective-permute-start(bf16[32,4096]{1,0:T(8,128)(2,1)S(1)} %apply_layer.18.before_ref), channel_id=1, source_target_pairs={{1,6},{2,5},{5,10},{6,9},{9,14},{10,13},{13,18},{14,17},{17,22},{1... | collective-permute-start | bytes 786440 | tf_op jit(solution)/shard_map/ppermute | solution.py:108
  45.5 2.1 %collective-permute-start.12 = (bf16[32,4096]{1,0:T(8,128)(2,1)S(1)}, bf16[32,4096]{1,0:T(8,128)(2,1)S(1)}, u32[]{:S(2)}, u32[]{:S(2)}) collective-permute-start(bf16[32,4096]{1,0:T(8,128)(2,1)S(1)} %apply_layer.18.before_ref), channel_id=1, source_target_pairs={{0,4},{1,5},{2,6},{3,7},{4,8},{5,9},{6,10},{7,11},{8,12},{9,13},{1... | collective-permute-start | bytes 786440 | tf_op jit(solution)/shard_map/ppermute | solution.py:108
  49.4 2.2 %collective-permute-start.13 = (bf16[24,4096]{1,0:T(8,128)(2,1)S(1)}, bf16[24,4096]{1,0:T(8,128)(2,1)S(1)}, u32[]{:S(2)}, u32[]{:S(2)}) collective-permute-start(bf16[24,4096]{1,0:T(8,128)(2,1)S(1)} %apply_layer.19.before_ref), channel_id=1, source_target_pairs={{0,5},{1,4},{2,7},{3,6},{4,9},{5,8},{6,11},{7,10},{8,13},{9,12},{1... | collective-permute-start | bytes 589832 | tf_op jit(solution)/shard_map/ppermute | solution.py:108
  51.5 4.9 %collective-permute-start.14 = (bf16[24,4096]{1,0:T(8,128)(2,1)S(1)}, bf16[24,4096]{1,0:T(8,128)(2,1)S(1)}, u32[]{:S(2)}, u32[]{:S(2)}) collective-permute-start(bf16[24,4096]{1,0:T(8,128)(2,1)S(1)} %apply_layer.19.before_ref), channel_id=1, source_target_pairs={{1,6},{2,5},{5,10},{6,9},{9,14},{10,13},{13,18},{14,17},{17,22},{1... | collective-permute-start | bytes 589832 | tf_op jit(solution)/shard_map/ppermute | solution.py:108
  56.4 3.3 %collective-permute-start.15 = (bf16[24,4096]{1,0:T(8,128)(2,1)S(1)}, bf16[24,4096]{1,0:T(8,128)(2,1)S(1)}, u32[]{:S(2)}, u32[]{:S(2)}) collective-permute-start(bf16[24,4096]{1,0:T(8,128)(2,1)S(1)} %apply_layer.19.before_ref), channel_id=1, source_target_pairs={{0,4},{1,5},{2,6},{3,7},{4,8},{5,9},{6,10},{7,11},{8,12},{9,13},{1... | collective-permute-start | bytes 589832 | tf_op jit(solution)/shard_map/ppermute | solution.py:108
  63.5 2.9 %collective-permute-start.17 = (bf16[32,4096]{1,0:T(8,128)(2,1)S(1)}, bf16[32,4096]{1,0:T(8,128)(2,1)S(1)}, u32[]{:S(2)}, u32[]{:S(2)}) collective-permute-start(bf16[32,4096]{1,0:T(8,128)(2,1)S(1)} %apply_layer.20.before_ref), channel_id=1, source_target_pairs={{1,6},{2,5},{5,10},{6,9},{9,14},{10,13},{13,18},{14,17},{17,22},{1... | collective-permute-start | bytes 786440 | tf_op jit(solution)/shard_map/ppermute | solution.py:108
  70.2 1.9 %collective-permute-start.19 = (bf16[24,4096]{1,0:T(8,128)(2,1)S(1)}, bf16[24,4096]{1,0:T(8,128)(2,1)S(1)}, u32[]{:S(2)}, u32[]{:S(2)}) collective-permute-start(bf16[24,4096]{1,0:T(8,128)(2,1)S(1)} %apply_layer.21.before_ref), channel_id=1, source_target_pairs={{0,5},{1,4},{2,7},{3,6},{4,9},{5,8},{6,11},{7,10},{8,13},{9,12},{1... | collective-permute-start | bytes 589832 | tf_op jit(solution)/shard_map/ppermute | solution.py:108
  72.2 2.7 %collective-permute-start.20 = (bf16[24,4096]{1,0:T(8,128)(2,1)S(1)}, bf16[24,4096]{1,0:T(8,128)(2,1)S(1)}, u32[]{:S(2)}, u32[]{:S(2)}) collective-permute-start(bf16[24,4096]{1,0:T(8,128)(2,1)S(1)} %apply_layer.21.before_ref), channel_id=1, source_target_pairs={{1,6},{2,5},{5,10},{6,9},{9,14},{10,13},{13,18},{14,17},{17,22},{1... | collective-permute-start | bytes 589832 | tf_op jit(solution)/shard_map/ppermute | solution.py:108
  74.9 1.9 %collective-permute-start.21 = (bf16[24,4096]{1,0:T(8,128)(2,1)S(1)}, bf16[24,4096]{1,0:T(8,128)(2,1)S(1)}, u32[]{:S(2)}, u32[]{:S(2)}) collective-permute-start(bf16[24,4096]{1,0:T(8,128)(2,1)S(1)} %apply_layer.21.before_ref), channel_id=1, source_target_pairs={{0,4},{1,5},{2,6},{3,7},{4,8},{5,9},{6,10},{7,11},{8,12},{9,13},{1... | collective-permute-start | bytes 589832 | tf_op jit(solution)/shard_map/ppermute | solution.py:108
  80.6 6.1 %collective-permute-start.23 = (bf16[32,4096]{1,0:T(8,128)(2,1)S(1)}, bf16[32,4096]{1,0:T(8,128)(2,1)S(1)}, u32[]{:S(2)}, u32[]{:S(2)}) collective-permute-start(bf16[32,4096]{1,0:T(8,128)(2,1)S(1)} %apply_layer.22.before_ref), channel_id=1, source_target_pairs={{1,6},{2,5},{5,10},{6,9},{9,14},{10,13},{13,18},{14,17},{17,22},{1... | collective-permute-start | bytes 786440 | tf_op jit(solution)/shard_map/ppermute | solution.py:108
  86.8 3.7 %collective-permute-start.24 = (bf16[32,4096]{1,0:T(8,128)(2,1)S(1)}, bf16[32,4096]{1,0:T(8,128)(2,1)S(1)}, u32[]{:S(2)}, u32[]{:S(2)}) collective-permute-start(bf16[32,4096]{1,0:T(8,128)(2,1)S(1)} %apply_layer.22.before_ref), channel_id=1, source_target_pairs={{0,4},{1,5},{2,6},{3,7},{4,8},{5,9},{6,10},{7,11},{8,12},{9,13},{1... | collective-permute-start | bytes 786440 | tf_op jit(solution)/shard_map/ppermute | solution.py:108
  92.3 1.9 %collective-permute-start.25 = (bf16[24,4096]{1,0:T(8,128)(2,1)S(1)}, bf16[24,4096]{1,0:T(8,128)(2,1)S(1)}, u32[]{:S(2)}, u32[]{:S(2)}) collective-permute-start(bf16[24,4096]{1,0:T(8,128)(2,1)S(1)} %apply_layer.23.before_ref), channel_id=1, source_target_pairs={{0,5},{1,4},{2,7},{3,6},{4,9},{5,8},{6,11},{7,10},{8,13},{9,12},{1... | collective-permute-start | bytes 589832 | tf_op jit(solution)/shard_map/ppermute | solution.py:108
  94.2 2.9 %collective-permute-start.26 = (bf16[24,4096]{1,0:T(8,128)(2,1)S(1)}, bf16[24,4096]{1,0:T(8,128)(2,1)S(1)}, u32[]{:S(2)}, u32[]{:S(2)}) collective-permute-start(bf16[24,4096]{1,0:T(8,128)(2,1)S(1)} %apply_layer.23.before_ref), channel_id=1, source_target_pairs={{1,6},{2,5},{5,10},{6,9},{9,14},{10,13},{13,18},{14,17},{17,22},{1... | collective-permute-start | bytes 589832 | tf_op jit(solution)/shard_map/ppermute | solution.py:108
  102.9 2.0 %collective-permute-start.29 = (bf16[32,4096]{1,0:T(8,128)(2,1)S(1)}, bf16[32,4096]{1,0:T(8,128)(2,1)S(1)}, u32[]{:S(2)}, u32[]{:S(2)}) collective-permute-start(bf16[32,4096]{1,0:T(8,128)(2,1)S(1)} %apply_layer.24.before_ref), channel_id=1, source_target_pairs={{1,6},{2,5},{5,10},{6,9},{9,14},{10,13},{13,18},{14,17},{17,22},{1... | collective-permute-start | bytes 786440 | tf_op jit(solution)/shard_map/ppermute | solution.py:108
  110.6 4.5 %collective-permute-start.32 = (bf16[24,4096]{1,0:T(8,128)(2,1)S(1)}, bf16[24,4096]{1,0:T(8,128)(2,1)S(1)}, u32[]{:S(2)}, u32[]{:S(2)}) collective-permute-start(bf16[24,4096]{1,0:T(8,128)(2,1)S(1)} %apply_layer.25.before_ref), channel_id=1, source_target_pairs={{1,6},{2,5},{5,10},{6,9},{9,14},{10,13},{13,18},{14,17},{17,22},{1... | collective-permute-start | bytes 589832 | tf_op jit(solution)/shard_map/ppermute | solution.py:108
  115.2 4.4 %collective-permute-start.33 = (bf16[24,4096]{1,0:T(8,128)(2,1)S(1)}, bf16[24,4096]{1,0:T(8,128)(2,1)S(1)}, u32[]{:S(2)}, u32[]{:S(2)}) collective-permute-start(bf16[24,4096]{1,0:T(8,128)(2,1)S(1)} %apply_layer.25.before_ref), channel_id=1, source_target_pairs={{0,4},{1,5},{2,6},{3,7},{4,8},{5,9},{6,10},{7,11},{8,12},{9,13},{1... | collective-permute-start | bytes 589832 | tf_op jit(solution)/shard_map/ppermute | solution.py:108
  126.9 3.1 %collective-permute-start.36 = (bf16[32,4096]{1,0:T(8,128)(2,1)S(1)}, bf16[32,4096]{1,0:T(8,128)(2,1)S(1)}, u32[]{:S(2)}, u32[]{:S(2)}) collective-permute-start(bf16[32,4096]{1,0:T(8,128)(2,1)S(1)} %apply_layer.26.before_ref), channel_id=1, source_target_pairs={{0,4},{1,5},{2,6},{3,7},{4,8},{5,9},{6,10},{7,11},{8,12},{9,13},{1... | collective-permute-start | bytes 786440 | tf_op jit(solution)/shard_map/ppermute | solution.py:108
  135.6 1.9 %collective-permute-start.39 = (bf16[24,4096]{1,0:T(8,128)(2,1)S(1)}, bf16[24,4096]{1,0:T(8,128)(2,1)S(1)}, u32[]{:S(2)}, u32[]{:S(2)}) collective-permute-start(bf16[24,4096]{1,0:T(8,128)(2,1)S(1)} %apply_layer.27.before_ref), channel_id=1, source_target_pairs={{0,4},{1,5},{2,6},{3,7},{4,8},{5,9},{6,10},{7,11},{8,12},{9,13},{1... | collective-permute-start | bytes 589832 | tf_op jit(solution)/shard_map/ppermute | solution.py:108
  139.4 1.9 %collective-permute-start.40 = (bf16[32,4096]{1,0:T(8,128)(2,1)S(1)}, bf16[32,4096]{1,0:T(8,128)(2,1)S(1)}, u32[]{:S(2)}, u32[]{:S(2)}) collective-permute-start(bf16[32,4096]{1,0:T(8,128)(2,1)S(1)} %apply_layer.28.before_ref), channel_id=1, source_target_pairs={{0,5},{1,4},{2,7},{3,6},{4,9},{5,8},{6,11},{7,10},{8,13},{9,12},{1... | collective-permute-start | bytes 786440 | tf_op jit(solution)/shard_map/ppermute | solution.py:108
  141.4 3.2 %collective-permute-start.41 = (bf16[32,4096]{1,0:T(8,128)(2,1)S(1)}, bf16[32,4096]{1,0:T(8,128)(2,1)S(1)}, u32[]{:S(2)}, u32[]{:S(2)}) collective-permute-start(bf16[32,4096]{1,0:T(8,128)(2,1)S(1)} %apply_layer.28.before_ref), channel_id=1, source_target_pairs={{1,6},{2,5},{5,10},{6,9},{9,14},{10,13},{13,18},{14,17},{17,22},{1... | collective-permute-start | bytes 786440 | tf_op jit(solution)/shard_map/ppermute | solution.py:108
  144.6 6.4 %collective-permute-start.42 = (bf16[32,4096]{1,0:T(8,128)(2,1)S(1)}, bf16[32,4096]{1,0:T(8,128)(2,1)S(1)}, u32[]{:S(2)}, u32[]{:S(2)}) collective-permute-start(bf16[32,4096]{1,0:T(8,128)(2,1)S(1)} %apply_layer.28.before_ref), channel_id=1, source_target_pairs={{0,4},{1,5},{2,6},{3,7},{4,8},{5,9},{6,10},{7,11},{8,12},{9,13},{1... | collective-permute-start | bytes 786440 | tf_op jit(solution)/shard_map/ppermute | solution.py:108
  156.6 4.1 %collective-permute-start.45 = (bf16[24,4096]{1,0:T(8,128)(2,1)S(1)}, bf16[24,4096]{1,0:T(8,128)(2,1)S(1)}, u32[]{:S(2)}, u32[]{:S(2)}) collective-permute-start(bf16[24,4096]{1,0:T(8,128)(2,1)S(1)} %apply_layer.29.before_ref), channel_id=1, source_target_pairs={{0,4},{1,5},{2,6},{3,7},{4,8},{5,9},{6,10},{7,11},{8,12},{9,13},{1... | collective-permute-start | bytes 589832 | tf_op jit(solution)/shard_map/ppermute | solution.py:108
  162.6 2.2 %collective-permute-done.44.far_ref = bf16[24,4096]{1,0:T(8,128)(2,1)S(1)} collective-permute-done((bf16[24,4096]{1,0:T(8,128)(2,1)S(1)}, bf16[24,4096]{1,0:T(8,128)(2,1)S(1)}, u32[]{:S(2)}, u32[]{:S(2)}) %collective-permute-start.44) | collective-permute-done | bytes 196640 | tf_op jit(solution)/shard_map/ppermute | solution.py:108
  (94 shorter events, 62.5 us)
Async XLA Ops:
  1.0 14.3 %collective-permute-start = (bf16[32,4096]{1,0:T(8,128)(2,1)S(1)}, bf16[32,4096]{1,0:T(8,128)(2,1)S(1)}, u32[]{:S(2)}, u32[]{:S(2)}) collective-permute-start(bf16[32,4096]{1,0:T(8,128)(2,1)S(1)} %slice_bitcast_fusion.own_ref), channel_id=1, source_target_pairs={{0,1},{1,0},{2,3},{3,2},{4,5},{5,4},{6,7},{7,6},{8,9},{9,8},{10,11... | collective-permute-start | bytes 786440 | tf_op jit(solution)/shard_map/ppermute | solution.py:108
  1.3 14.0 %collective-permute-start.1 = (bf16[32,4096]{1,0:T(8,128)(2,1)S(1)}, bf16[32,4096]{1,0:T(8,128)(2,1)S(1)}, u32[]{:S(2)}, u32[]{:S(2)}) collective-permute-start(bf16[32,4096]{1,0:T(8,128)(2,1)S(1)} %slice_bitcast_fusion.own_ref), channel_id=1, source_target_pairs={{1,2},{2,1},{5,6},{6,5},{9,10},{10,9},{13,14},{14,13},{17,18},{18,... | collective-permute-start | bytes 786440 | tf_op jit(solution)/shard_map/ppermute | solution.py:108
  6.3 21.2 %collective-permute-start.2 = (bf16[24,4096]{1,0:T(8,128)(2,1)S(1)}, bf16[24,4096]{1,0:T(8,128)(2,1)S(1)}, u32[]{:S(2)}, u32[]{:S(2)}) collective-permute-start(bf16[24,4096]{1,0:T(8,128)(2,1)S(1)} %slice_bitcast_fusion.1.own_ref), channel_id=1, source_target_pairs={{0,1},{1,0},{2,3},{3,2},{4,5},{5,4},{6,7},{7,6},{8,9},{9,8},{10,11... | collective-permute-start | bytes 589832 | tf_op jit(solution)/shard_map/ppermute | solution.py:108
  6.4 21.1 %collective-permute-start.3 = (bf16[24,4096]{1,0:T(8,128)(2,1)S(1)}, bf16[24,4096]{1,0:T(8,128)(2,1)S(1)}, u32[]{:S(2)}, u32[]{:S(2)}) collective-permute-start(bf16[24,4096]{1,0:T(8,128)(2,1)S(1)} %slice_bitcast_fusion.1.own_ref), channel_id=1, source_target_pairs={{1,2},{2,1},{5,6},{6,5},{9,10},{10,9},{13,14},{14,13},{17,18},{18,... | collective-permute-start | bytes 589832 | tf_op jit(solution)/shard_map/ppermute | solution.py:108
  17.2 18.2 %collective-permute-start.4 = (bf16[32,4096]{1,0:T(8,128)(2,1)S(1)}, bf16[32,4096]{1,0:T(8,128)(2,1)S(1)}, u32[]{:S(2)}, u32[]{:S(2)}) collective-permute-start(bf16[32,4096]{1,0:T(8,128)(2,1)S(1)} %apply_layer.16.before_ref), channel_id=1, source_target_pairs={{0,5},{1,4},{2,7},{3,6},{4,9},{5,8},{6,11},{7,10},{8,13},{9,12},{1... | collective-permute-start | bytes 786440 | tf_op jit(solution)/shard_map/ppermute | solution.py:108
  21.5 16.0 %collective-permute-start.5 = (bf16[32,4096]{1,0:T(8,128)(2,1)S(1)}, bf16[32,4096]{1,0:T(8,128)(2,1)S(1)}, u32[]{:S(2)}, u32[]{:S(2)}) collective-permute-start(bf16[32,4096]{1,0:T(8,128)(2,1)S(1)} %apply_layer.16.before_ref), channel_id=1, source_target_pairs={{1,6},{2,5},{5,10},{6,9},{9,14},{10,13},{13,18},{14,17},{17,22},{1... | collective-permute-start | bytes 786440 | tf_op jit(solution)/shard_map/ppermute | solution.py:108
  29.3 16.2 %collective-permute-start.7 = (bf16[24,4096]{1,0:T(8,128)(2,1)S(1)}, bf16[24,4096]{1,0:T(8,128)(2,1)S(1)}, u32[]{:S(2)}, u32[]{:S(2)}) collective-permute-start(bf16[24,4096]{1,0:T(8,128)(2,1)S(1)} %apply_layer.17.before_ref), channel_id=1, source_target_pairs={{0,5},{1,4},{2,7},{3,6},{4,9},{5,8},{6,11},{7,10},{8,13},{9,12},{1... | collective-permute-start | bytes 589832 | tf_op jit(solution)/shard_map/ppermute | solution.py:108
  31.3 16.3 %collective-permute-start.8 = (bf16[24,4096]{1,0:T(8,128)(2,1)S(1)}, bf16[24,4096]{1,0:T(8,128)(2,1)S(1)}, u32[]{:S(2)}, u32[]{:S(2)}) collective-permute-start(bf16[24,4096]{1,0:T(8,128)(2,1)S(1)} %apply_layer.17.before_ref), channel_id=1, source_target_pairs={{1,6},{2,5},{5,10},{6,9},{9,14},{10,13},{13,18},{14,17},{17,22},{1... | collective-permute-start | bytes 589832 | tf_op jit(solution)/shard_map/ppermute | solution.py:108
  39.3 17.1 %collective-permute-start.10 = (bf16[32,4096]{1,0:T(8,128)(2,1)S(1)}, bf16[32,4096]{1,0:T(8,128)(2,1)S(1)}, u32[]{:S(2)}, u32[]{:S(2)}) collective-permute-start(bf16[32,4096]{1,0:T(8,128)(2,1)S(1)} %apply_layer.18.before_ref), channel_id=1, source_target_pairs={{0,5},{1,4},{2,7},{3,6},{4,9},{5,8},{6,11},{7,10},{8,13},{9,12},{1... | collective-permute-start | bytes 786440 | tf_op jit(solution)/shard_map/ppermute | solution.py:108
  41.4 18.4 %collective-permute-start.11 = (bf16[32,4096]{1,0:T(8,128)(2,1)S(1)}, bf16[32,4096]{1,0:T(8,128)(2,1)S(1)}, u32[]{:S(2)}, u32[]{:S(2)}) collective-permute-start(bf16[32,4096]{1,0:T(8,128)(2,1)S(1)} %apply_layer.18.before_ref), channel_id=1, source_target_pairs={{1,6},{2,5},{5,10},{6,9},{9,14},{10,13},{13,18},{14,17},{17,22},{1... | collective-permute-start | bytes 786440 | tf_op jit(solution)/shard_map/ppermute | solution.py:108
  45.5 14.3 %collective-permute-start.12 = (bf16[32,4096]{1,0:T(8,128)(2,1)S(1)}, bf16[32,4096]{1,0:T(8,128)(2,1)S(1)}, u32[]{:S(2)}, u32[]{:S(2)}) collective-permute-start(bf16[32,4096]{1,0:T(8,128)(2,1)S(1)} %apply_layer.18.before_ref), channel_id=1, source_target_pairs={{0,4},{1,5},{2,6},{3,7},{4,8},{5,9},{6,10},{7,11},{8,12},{9,13},{1... | collective-permute-start | bytes 786440 | tf_op jit(solution)/shard_map/ppermute | solution.py:108
  49.4 17.1 %collective-permute-start.13 = (bf16[24,4096]{1,0:T(8,128)(2,1)S(1)}, bf16[24,4096]{1,0:T(8,128)(2,1)S(1)}, u32[]{:S(2)}, u32[]{:S(2)}) collective-permute-start(bf16[24,4096]{1,0:T(8,128)(2,1)S(1)} %apply_layer.19.before_ref), channel_id=1, source_target_pairs={{0,5},{1,4},{2,7},{3,6},{4,9},{5,8},{6,11},{7,10},{8,13},{9,12},{1... | collective-permute-start | bytes 589832 | tf_op jit(solution)/shard_map/ppermute | solution.py:108
  51.5 16.9 %collective-permute-start.14 = (bf16[24,4096]{1,0:T(8,128)(2,1)S(1)}, bf16[24,4096]{1,0:T(8,128)(2,1)S(1)}, u32[]{:S(2)}, u32[]{:S(2)}) collective-permute-start(bf16[24,4096]{1,0:T(8,128)(2,1)S(1)} %apply_layer.19.before_ref), channel_id=1, source_target_pairs={{1,6},{2,5},{5,10},{6,9},{9,14},{10,13},{13,18},{14,17},{17,22},{1... | collective-permute-start | bytes 589832 | tf_op jit(solution)/shard_map/ppermute | solution.py:108
  61.6 13.3 %collective-permute-start.16 = (bf16[32,4096]{1,0:T(8,128)(2,1)S(1)}, bf16[32,4096]{1,0:T(8,128)(2,1)S(1)}, u32[]{:S(2)}, u32[]{:S(2)}) collective-permute-start(bf16[32,4096]{1,0:T(8,128)(2,1)S(1)} %apply_layer.20.before_ref), channel_id=1, source_target_pairs={{0,5},{1,4},{2,7},{3,6},{4,9},{5,8},{6,11},{7,10},{8,13},{9,12},{1... | collective-permute-start | bytes 786440 | tf_op jit(solution)/shard_map/ppermute | solution.py:108
  63.5 13.3 %collective-permute-start.17 = (bf16[32,4096]{1,0:T(8,128)(2,1)S(1)}, bf16[32,4096]{1,0:T(8,128)(2,1)S(1)}, u32[]{:S(2)}, u32[]{:S(2)}) collective-permute-start(bf16[32,4096]{1,0:T(8,128)(2,1)S(1)} %apply_layer.20.before_ref), channel_id=1, source_target_pairs={{1,6},{2,5},{5,10},{6,9},{9,14},{10,13},{13,18},{14,17},{17,22},{1... | collective-permute-start | bytes 786440 | tf_op jit(solution)/shard_map/ppermute | solution.py:108
  70.2 16.5 %collective-permute-start.19 = (bf16[24,4096]{1,0:T(8,128)(2,1)S(1)}, bf16[24,4096]{1,0:T(8,128)(2,1)S(1)}, u32[]{:S(2)}, u32[]{:S(2)}) collective-permute-start(bf16[24,4096]{1,0:T(8,128)(2,1)S(1)} %apply_layer.21.before_ref), channel_id=1, source_target_pairs={{0,5},{1,4},{2,7},{3,6},{4,9},{5,8},{6,11},{7,10},{8,13},{9,12},{1... | collective-permute-start | bytes 589832 | tf_op jit(solution)/shard_map/ppermute | solution.py:108
  72.2 18.3 %collective-permute-start.20 = (bf16[24,4096]{1,0:T(8,128)(2,1)S(1)}, bf16[24,4096]{1,0:T(8,128)(2,1)S(1)}, u32[]{:S(2)}, u32[]{:S(2)}) collective-permute-start(bf16[24,4096]{1,0:T(8,128)(2,1)S(1)} %apply_layer.21.before_ref), channel_id=1, source_target_pairs={{1,6},{2,5},{5,10},{6,9},{9,14},{10,13},{13,18},{14,17},{17,22},{1... | collective-permute-start | bytes 589832 | tf_op jit(solution)/shard_map/ppermute | solution.py:108
  74.9 15.6 %collective-permute-start.21 = (bf16[24,4096]{1,0:T(8,128)(2,1)S(1)}, bf16[24,4096]{1,0:T(8,128)(2,1)S(1)}, u32[]{:S(2)}, u32[]{:S(2)}) collective-permute-start(bf16[24,4096]{1,0:T(8,128)(2,1)S(1)} %apply_layer.21.before_ref), channel_id=1, source_target_pairs={{0,4},{1,5},{2,6},{3,7},{4,8},{5,9},{6,10},{7,11},{8,12},{9,13},{1... | collective-permute-start | bytes 589832 | tf_op jit(solution)/shard_map/ppermute | solution.py:108
  78.7 18.5 %collective-permute-start.22 = (bf16[32,4096]{1,0:T(8,128)(2,1)S(1)}, bf16[32,4096]{1,0:T(8,128)(2,1)S(1)}, u32[]{:S(2)}, u32[]{:S(2)}) collective-permute-start(bf16[32,4096]{1,0:T(8,128)(2,1)S(1)} %apply_layer.22.before_ref), channel_id=1, source_target_pairs={{0,5},{1,4},{2,7},{3,6},{4,9},{5,8},{6,11},{7,10},{8,13},{9,12},{1... | collective-permute-start | bytes 786440 | tf_op jit(solution)/shard_map/ppermute | solution.py:108
  80.6 18.5 %collective-permute-start.23 = (bf16[32,4096]{1,0:T(8,128)(2,1)S(1)}, bf16[32,4096]{1,0:T(8,128)(2,1)S(1)}, u32[]{:S(2)}, u32[]{:S(2)}) collective-permute-start(bf16[32,4096]{1,0:T(8,128)(2,1)S(1)} %apply_layer.22.before_ref), channel_id=1, source_target_pairs={{1,6},{2,5},{5,10},{6,9},{9,14},{10,13},{13,18},{14,17},{17,22},{1... | collective-permute-start | bytes 786440 | tf_op jit(solution)/shard_map/ppermute | solution.py:108
  101.0 14.2 %collective-permute-start.28 = (bf16[32,4096]{1,0:T(8,128)(2,1)S(1)}, bf16[32,4096]{1,0:T(8,128)(2,1)S(1)}, u32[]{:S(2)}, u32[]{:S(2)}) collective-permute-start(bf16[32,4096]{1,0:T(8,128)(2,1)S(1)} %apply_layer.24.before_ref), channel_id=1, source_target_pairs={{0,5},{1,4},{2,7},{3,6},{4,9},{5,8},{6,11},{7,10},{8,13},{9,12},{1... | collective-permute-start | bytes 786440 | tf_op jit(solution)/shard_map/ppermute | solution.py:108
  102.9 18.3 %collective-permute-start.29 = (bf16[32,4096]{1,0:T(8,128)(2,1)S(1)}, bf16[32,4096]{1,0:T(8,128)(2,1)S(1)}, u32[]{:S(2)}, u32[]{:S(2)}) collective-permute-start(bf16[32,4096]{1,0:T(8,128)(2,1)S(1)} %apply_layer.24.before_ref), channel_id=1, source_target_pairs={{1,6},{2,5},{5,10},{6,9},{9,14},{10,13},{13,18},{14,17},{17,22},{1... | collective-permute-start | bytes 786440 | tf_op jit(solution)/shard_map/ppermute | solution.py:108
  105.0 16.2 %collective-permute-start.30 = (bf16[32,4096]{1,0:T(8,128)(2,1)S(1)}, bf16[32,4096]{1,0:T(8,128)(2,1)S(1)}, u32[]{:S(2)}, u32[]{:S(2)}) collective-permute-start(bf16[32,4096]{1,0:T(8,128)(2,1)S(1)} %apply_layer.24.before_ref), channel_id=1, source_target_pairs={{0,4},{1,5},{2,6},{3,7},{4,8},{5,9},{6,10},{7,11},{8,12},{9,13},{1... | collective-permute-start | bytes 786440 | tf_op jit(solution)/shard_map/ppermute | solution.py:108
  108.7 18.2 %collective-permute-start.31 = (bf16[24,4096]{1,0:T(8,128)(2,1)S(1)}, bf16[24,4096]{1,0:T(8,128)(2,1)S(1)}, u32[]{:S(2)}, u32[]{:S(2)}) collective-permute-start(bf16[24,4096]{1,0:T(8,128)(2,1)S(1)} %apply_layer.25.before_ref), channel_id=1, source_target_pairs={{0,5},{1,4},{2,7},{3,6},{4,9},{5,8},{6,11},{7,10},{8,13},{9,12},{1... | collective-permute-start | bytes 589832 | tf_op jit(solution)/shard_map/ppermute | solution.py:108
  110.6 19.3 %collective-permute-start.32 = (bf16[24,4096]{1,0:T(8,128)(2,1)S(1)}, bf16[24,4096]{1,0:T(8,128)(2,1)S(1)}, u32[]{:S(2)}, u32[]{:S(2)}) collective-permute-start(bf16[24,4096]{1,0:T(8,128)(2,1)S(1)} %apply_layer.25.before_ref), channel_id=1, source_target_pairs={{1,6},{2,5},{5,10},{6,9},{9,14},{10,13},{13,18},{14,17},{17,22},{1... | collective-permute-start | bytes 589832 | tf_op jit(solution)/shard_map/ppermute | solution.py:108
  115.2 14.8 %collective-permute-start.33 = (bf16[24,4096]{1,0:T(8,128)(2,1)S(1)}, bf16[24,4096]{1,0:T(8,128)(2,1)S(1)}, u32[]{:S(2)}, u32[]{:S(2)}) collective-permute-start(bf16[24,4096]{1,0:T(8,128)(2,1)S(1)} %apply_layer.25.before_ref), channel_id=1, source_target_pairs={{0,4},{1,5},{2,6},{3,7},{4,8},{5,9},{6,10},{7,11},{8,12},{9,13},{1... | collective-permute-start | bytes 589832 | tf_op jit(solution)/shard_map/ppermute | solution.py:108
  131.8 12.8 %collective-permute-start.37 = (bf16[24,4096]{1,0:T(8,128)(2,1)S(1)}, bf16[24,4096]{1,0:T(8,128)(2,1)S(1)}, u32[]{:S(2)}, u32[]{:S(2)}) collective-permute-start(bf16[24,4096]{1,0:T(8,128)(2,1)S(1)} %apply_layer.27.before_ref), channel_id=1, source_target_pairs={{0,5},{1,4},{2,7},{3,6},{4,9},{5,8},{6,11},{7,10},{8,13},{9,12},{1... | collective-permute-start | bytes 589832 | tf_op jit(solution)/shard_map/ppermute | solution.py:108
  133.7 17.3 %collective-permute-start.38 = (bf16[24,4096]{1,0:T(8,128)(2,1)S(1)}, bf16[24,4096]{1,0:T(8,128)(2,1)S(1)}, u32[]{:S(2)}, u32[]{:S(2)}) collective-permute-start(bf16[24,4096]{1,0:T(8,128)(2,1)S(1)} %apply_layer.27.before_ref), channel_id=1, source_target_pairs={{1,6},{2,5},{5,10},{6,9},{9,14},{10,13},{13,18},{14,17},{17,22},{1... | collective-permute-start | bytes 589832 | tf_op jit(solution)/shard_map/ppermute | solution.py:108
  135.6 15.3 %collective-permute-start.39 = (bf16[24,4096]{1,0:T(8,128)(2,1)S(1)}, bf16[24,4096]{1,0:T(8,128)(2,1)S(1)}, u32[]{:S(2)}, u32[]{:S(2)}) collective-permute-start(bf16[24,4096]{1,0:T(8,128)(2,1)S(1)} %apply_layer.27.before_ref), channel_id=1, source_target_pairs={{0,4},{1,5},{2,6},{3,7},{4,8},{5,9},{6,10},{7,11},{8,12},{9,13},{1... | collective-permute-start | bytes 589832 | tf_op jit(solution)/shard_map/ppermute | solution.py:108
  139.4 17.2 %collective-permute-start.40 = (bf16[32,4096]{1,0:T(8,128)(2,1)S(1)}, bf16[32,4096]{1,0:T(8,128)(2,1)S(1)}, u32[]{:S(2)}, u32[]{:S(2)}) collective-permute-start(bf16[32,4096]{1,0:T(8,128)(2,1)S(1)} %apply_layer.28.before_ref), channel_id=1, source_target_pairs={{0,5},{1,4},{2,7},{3,6},{4,9},{5,8},{6,11},{7,10},{8,13},{9,12},{1... | collective-permute-start | bytes 786440 | tf_op jit(solution)/shard_map/ppermute | solution.py:108
  141.4 19.4 %collective-permute-start.41 = (bf16[32,4096]{1,0:T(8,128)(2,1)S(1)}, bf16[32,4096]{1,0:T(8,128)(2,1)S(1)}, u32[]{:S(2)}, u32[]{:S(2)}) collective-permute-start(bf16[32,4096]{1,0:T(8,128)(2,1)S(1)} %apply_layer.28.before_ref), channel_id=1, source_target_pairs={{1,6},{2,5},{5,10},{6,9},{9,14},{10,13},{13,18},{14,17},{17,22},{1... | collective-permute-start | bytes 786440 | tf_op jit(solution)/shard_map/ppermute | solution.py:108
  144.6 16.2 %collective-permute-start.42 = (bf16[32,4096]{1,0:T(8,128)(2,1)S(1)}, bf16[32,4096]{1,0:T(8,128)(2,1)S(1)}, u32[]{:S(2)}, u32[]{:S(2)}) collective-permute-start(bf16[32,4096]{1,0:T(8,128)(2,1)S(1)} %apply_layer.28.before_ref), channel_id=1, source_target_pairs={{0,4},{1,5},{2,6},{3,7},{4,8},{5,9},{6,10},{7,11},{8,12},{9,13},{1... | collective-permute-start | bytes 786440 | tf_op jit(solution)/shard_map/ppermute | solution.py:108
  (16 other events, 166.0 us)

commit v2 on v1

--- a/solution.py
+++ b/solution.py
@@ -54,7 +54,7 @@
     )(prop)
 
 
-def tick_kernel(tick, first, cols_ref, weights_ref, near_ref, far_ref, own_ref, source_ref, before_ref, out_ref, window):
+def tick_kernel(tick, first, cols_ref, weights_ref, near_ref, own_ref, far_ref, source_ref, before_ref, out_ref, window):
     del before_ref
     shots, width = own_ref.shape
     row_blocks, depth, blk = weights_ref.shape
@@ -76,7 +76,7 @@
     lax.fori_loop(0, row_blocks, step, 0, unroll=min(16, row_blocks))
 
 
-def apply_layer(tick, first, cols, weights, near, far, own, sources, before):
+def apply_layer(tick, first, cols, weights, near, own, far, sources, before):
     shots, width = own.shape
     vmem = pl.BlockSpec(memory_space=pltpu.VMEM)
     return pl.pallas_call(
@@ -90,7 +90,7 @@
             flops=2 * shots * weights.size, bytes_accessed=weights.size * 2, transcendentals=0
         ),
         name="apply_layer",
-    )(cols, weights, near, far, own, sources, before)
+    )(cols, weights, near, own, far, sources, before)
 
 
 def partner(r, rows, far):
@@ -126,7 +126,7 @@
     for a, b in panels:
         own = incoming[0, a:b]
         beside = send(own, layers, 0, near)
-        arriving.append((beside, send(own, layers, 0, far), own))
+        arriving.append((beside, own, send(own, layers, 0, far)))
     weights = convert_weights(jnp.transpose(propagator[0], (1, 0, 2)))
     before = weights
     history = []
@@ -138,8 +138,9 @@
             produced.append(done)
             if tick + 1 < ticks:
                 beside = send(done, layers, 1, near)
+                same = send(done, layers, 1, range(rows))
                 distant = send(done, layers, 1, far)
-                arriving[i] = (beside, distant, send(done, layers, 1, range(rows)))
+                arriving[i] = (beside, same, distant)
         history.append(jnp.concatenate(produced, axis=0))
     return jnp.stack(history)[:, None]
 

time: 170 us -> 168 us (0.988)
  starting transfers between devices: 124 us -> 118 us
  waiting for transfers between devices: 3.95 us -> 7.62 us
    ppermute x46, starting transfers between devices: 124 us -> 118 us  [send(): return lax.ppermute(value, ('layer', 'row'), pairs)]
    ppermute x46, waiting for transfers between devices: 3.95 us -> 7.62 us  [send(): return lax.ppermute(value, ('layer', 'row'), pairs)]
  transfers between devices with their start and end apart: 46 -> 46, of which waited for: 2 -> 8; matrix products, arithmetic and copies ran while one was open for 1% -> 1% of each run, Pallas kernels for 19% -> 20%
where the time goes in v2:
time: 168 us; the launch traced here: 166 us
  starting transfers between devices  118 us (70%)
  Pallas kernels  34.6 us (21%)
  waiting for transfers between devices  7.62 us (5%)
  local copies, waits for them, and re-layouts  4.62 us (3%)
    ppermute x46, starting transfers between devices, send(): return lax.ppermute(value, ('layer', 'row'), pairs)  118 us
    pallas_call x16, Pallas kernels, apply_layer(): pl.pallas_call(functools.partial(tick_kernel, tick, first), in_specs=[pl....  28.7 us
    ppermute x46, waiting for transfers between devices, send(): return lax.ppermute(value, ('layer', 'row'), pairs)  7.62 us
    pallas_call x1, Pallas kernels, convert_weights(): pl.pallas_call(convert_kernel, in_specs=[pl.BlockSpec(memory_space=pltpu....  5.89 us
  transfers between devices with their start and end apart: 46, of which 8 were waited for; matrix products, arithmetic and copies ran while one was open for 1% of the time, Pallas kernels for 20%

profile of v2, /device:TPU:11, one launch (start us, length us, event | category | flops | bytes accessed | tf_op | source)
XLA Modules:
  0.0 166.0 jit_solution(13464461231085405008)
XLA Ops:
  1.3 4.1 %collective-permute-start.1 = (bf16[32,4096]{1,0:T(8,128)(2,1)S(1)}, bf16[32,4096]{1,0:T(8,128)(2,1)S(1)}, u32[]{:S(2)}, u32[]{:S(2)}) collective-permute-start(bf16[32,4096]{1,0:T(8,128)(2,1)S(1)} %slice_bitcast_fusion.own_ref), channel_id=1, source_target_pairs={{1,2},{2,1},{5,6},{6,5},{9,10},{10,9},{13,14},{14,13},{17,18},{18,... | collective-permute-start | bytes 786440 | tf_op jit(solution)/shard_map/ppermute | solution.py:108
  6.4 2.1 %collective-permute-start.3 = (bf16[24,4096]{1,0:T(8,128)(2,1)S(1)}, bf16[24,4096]{1,0:T(8,128)(2,1)S(1)}, u32[]{:S(2)}, u32[]{:S(2)}) collective-permute-start(bf16[24,4096]{1,0:T(8,128)(2,1)S(1)} %slice_bitcast_fusion.1.own_ref), channel_id=1, source_target_pairs={{1,2},{2,1},{5,6},{6,5},{9,10},{10,9},{13,14},{14,13},{17,18},{18,... | collective-permute-start | bytes 589832 | tf_op jit(solution)/shard_map/ppermute | solution.py:108
  9.4 5.9 %convert_weights.1.weights_ref.before_ref = bf16[32,768,128]{2,1,0:T(8,128)(2,1)S(1)} custom-call(f32[6,4096,128]{2,1,0:T(8,128)} %bitcast.42), custom_call_target="tpu_custom_call" | custom-call | bytes 12582912 | tf_op jit(solution)/shard_map/convert_weights/pallas_call | solution.py:42
  17.2 4.3 %collective-permute-start.4 = (bf16[32,4096]{1,0:T(8,128)(2,1)S(1)}, bf16[32,4096]{1,0:T(8,128)(2,1)S(1)}, u32[]{:S(2)}, u32[]{:S(2)}) collective-permute-start(bf16[32,4096]{1,0:T(8,128)(2,1)S(1)} %apply_layer.16.before_ref), channel_id=1, source_target_pairs={{0,5},{1,4},{2,7},{3,6},{4,9},{5,8},{6,11},{7,10},{8,13},{9,12},{1... | collective-permute-start | bytes 786440 | tf_op jit(solution)/shard_map/ppermute | solution.py:108
  21.5 2.8 %collective-permute-start.5 = (bf16[32,4096]{1,0:T(8,128)(2,1)S(1)}, bf16[32,4096]{1,0:T(8,128)(2,1)S(1)}, u32[]{:S(2)}, u32[]{:S(2)}) collective-permute-start(bf16[32,4096]{1,0:T(8,128)(2,1)S(1)} %apply_layer.16.before_ref), channel_id=1, source_target_pairs={{0,4},{1,5},{2,6},{3,7},{4,8},{5,9},{6,10},{7,11},{8,12},{9,13},{1... | collective-permute-start | bytes 786440 | tf_op jit(solution)/shard_map/ppermute | solution.py:108
  24.3 3.2 %collective-permute-start.6 = (bf16[32,4096]{1,0:T(8,128)(2,1)S(1)}, bf16[32,4096]{1,0:T(8,128)(2,1)S(1)}, u32[]{:S(2)}, u32[]{:S(2)}) collective-permute-start(bf16[32,4096]{1,0:T(8,128)(2,1)S(1)} %apply_layer.16.before_ref), channel_id=1, source_target_pairs={{1,6},{2,5},{5,10},{6,9},{9,14},{10,13},{13,18},{14,17},{17,22},{1... | collective-permute-start | bytes 786440 | tf_op jit(solution)/shard_map/ppermute | solution.py:108
  29.3 2.0 %collective-permute-start.7 = (bf16[24,4096]{1,0:T(8,128)(2,1)S(1)}, bf16[24,4096]{1,0:T(8,128)(2,1)S(1)}, u32[]{:S(2)}, u32[]{:S(2)}) collective-permute-start(bf16[24,4096]{1,0:T(8,128)(2,1)S(1)} %apply_layer.17.before_ref), channel_id=1, source_target_pairs={{0,5},{1,4},{2,7},{3,6},{4,9},{5,8},{6,11},{7,10},{8,13},{9,12},{1... | collective-permute-start | bytes 589832 | tf_op jit(solution)/shard_map/ppermute | solution.py:108
  31.3 3.7 %collective-permute-start.8 = (bf16[24,4096]{1,0:T(8,128)(2,1)S(1)}, bf16[24,4096]{1,0:T(8,128)(2,1)S(1)}, u32[]{:S(2)}, u32[]{:S(2)}) collective-permute-start(bf16[24,4096]{1,0:T(8,128)(2,1)S(1)} %apply_layer.17.before_ref), channel_id=1, source_target_pairs={{0,4},{1,5},{2,6},{3,7},{4,8},{5,9},{6,10},{7,11},{8,12},{9,13},{1... | collective-permute-start | bytes 589832 | tf_op jit(solution)/shard_map/ppermute | solution.py:108
  35.0 2.5 %collective-permute-start.9 = (bf16[24,4096]{1,0:T(8,128)(2,1)S(1)}, bf16[24,4096]{1,0:T(8,128)(2,1)S(1)}, u32[]{:S(2)}, u32[]{:S(2)}) collective-permute-start(bf16[24,4096]{1,0:T(8,128)(2,1)S(1)} %apply_layer.17.before_ref), channel_id=1, source_target_pairs={{1,6},{2,5},{5,10},{6,9},{9,14},{10,13},{13,18},{14,17},{17,22},{1... | collective-permute-start | bytes 589832 | tf_op jit(solution)/shard_map/ppermute | solution.py:108
  39.5 1.9 %collective-permute-start.10 = (bf16[32,4096]{1,0:T(8,128)(2,1)S(1)}, bf16[32,4096]{1,0:T(8,128)(2,1)S(1)}, u32[]{:S(2)}, u32[]{:S(2)}) collective-permute-start(bf16[32,4096]{1,0:T(8,128)(2,1)S(1)} %apply_layer.18.before_ref), channel_id=1, source_target_pairs={{0,5},{1,4},{2,7},{3,6},{4,9},{5,8},{6,11},{7,10},{8,13},{9,12},{1... | collective-permute-start | bytes 786440 | tf_op jit(solution)/shard_map/ppermute | solution.py:108
  41.4 2.1 %collective-permute-start.11 = (bf16[32,4096]{1,0:T(8,128)(2,1)S(1)}, bf16[32,4096]{1,0:T(8,128)(2,1)S(1)}, u32[]{:S(2)}, u32[]{:S(2)}) collective-permute-start(bf16[32,4096]{1,0:T(8,128)(2,1)S(1)} %apply_layer.18.before_ref), channel_id=1, source_target_pairs={{0,4},{1,5},{2,6},{3,7},{4,8},{5,9},{6,10},{7,11},{8,12},{9,13},{1... | collective-permute-start | bytes 786440 | tf_op jit(solution)/shard_map/ppermute | solution.py:108
  43.5 4.1 %collective-permute-start.12 = (bf16[32,4096]{1,0:T(8,128)(2,1)S(1)}, bf16[32,4096]{1,0:T(8,128)(2,1)S(1)}, u32[]{:S(2)}, u32[]{:S(2)}) collective-permute-start(bf16[32,4096]{1,0:T(8,128)(2,1)S(1)} %apply_layer.18.before_ref), channel_id=1, source_target_pairs={{1,6},{2,5},{5,10},{6,9},{9,14},{10,13},{13,18},{14,17},{17,22},{1... | collective-permute-start | bytes 786440 | tf_op jit(solution)/shard_map/ppermute | solution.py:108
  51.3 2.7 %collective-permute-start.14 = (bf16[24,4096]{1,0:T(8,128)(2,1)S(1)}, bf16[24,4096]{1,0:T(8,128)(2,1)S(1)}, u32[]{:S(2)}, u32[]{:S(2)}) collective-permute-start(bf16[24,4096]{1,0:T(8,128)(2,1)S(1)} %apply_layer.19.before_ref), channel_id=1, source_target_pairs={{0,4},{1,5},{2,6},{3,7},{4,8},{5,9},{6,10},{7,11},{8,12},{9,13},{1... | collective-permute-start | bytes 589832 | tf_op jit(solution)/shard_map/ppermute | solution.py:108
  54.0 3.1 %collective-permute-start.15 = (bf16[24,4096]{1,0:T(8,128)(2,1)S(1)}, bf16[24,4096]{1,0:T(8,128)(2,1)S(1)}, u32[]{:S(2)}, u32[]{:S(2)}) collective-permute-start(bf16[24,4096]{1,0:T(8,128)(2,1)S(1)} %apply_layer.19.before_ref), channel_id=1, source_target_pairs={{1,6},{2,5},{5,10},{6,9},{9,14},{10,13},{13,18},{14,17},{17,22},{1... | collective-permute-start | bytes 589832 | tf_op jit(solution)/shard_map/ppermute | solution.py:108
  63.3 3.8 %collective-permute-start.18 = (bf16[32,4096]{1,0:T(8,128)(2,1)S(1)}, bf16[32,4096]{1,0:T(8,128)(2,1)S(1)}, u32[]{:S(2)}, u32[]{:S(2)}) collective-permute-start(bf16[32,4096]{1,0:T(8,128)(2,1)S(1)} %apply_layer.20.before_ref), channel_id=1, source_target_pairs={{1,6},{2,5},{5,10},{6,9},{9,14},{10,13},{13,18},{14,17},{17,22},{1... | collective-permute-start | bytes 786440 | tf_op jit(solution)/shard_map/ppermute | solution.py:108
  68.9 1.9 %collective-permute-start.19 = (bf16[24,4096]{1,0:T(8,128)(2,1)S(1)}, bf16[24,4096]{1,0:T(8,128)(2,1)S(1)}, u32[]{:S(2)}, u32[]{:S(2)}) collective-permute-start(bf16[24,4096]{1,0:T(8,128)(2,1)S(1)} %apply_layer.21.before_ref), channel_id=1, source_target_pairs={{0,5},{1,4},{2,7},{3,6},{4,9},{5,8},{6,11},{7,10},{8,13},{9,12},{1... | collective-permute-start | bytes 589832 | tf_op jit(solution)/shard_map/ppermute | solution.py:108
  70.8 2.8 %collective-permute-start.20 = (bf16[24,4096]{1,0:T(8,128)(2,1)S(1)}, bf16[24,4096]{1,0:T(8,128)(2,1)S(1)}, u32[]{:S(2)}, u32[]{:S(2)}) collective-permute-start(bf16[24,4096]{1,0:T(8,128)(2,1)S(1)} %apply_layer.21.before_ref), channel_id=1, source_target_pairs={{0,4},{1,5},{2,6},{3,7},{4,8},{5,9},{6,10},{7,11},{8,12},{9,13},{1... | collective-permute-start | bytes 589832 | tf_op jit(solution)/shard_map/ppermute | solution.py:108
  73.7 3.1 %collective-permute-start.21 = (bf16[24,4096]{1,0:T(8,128)(2,1)S(1)}, bf16[24,4096]{1,0:T(8,128)(2,1)S(1)}, u32[]{:S(2)}, u32[]{:S(2)}) collective-permute-start(bf16[24,4096]{1,0:T(8,128)(2,1)S(1)} %apply_layer.21.before_ref), channel_id=1, source_target_pairs={{1,6},{2,5},{5,10},{6,9},{9,14},{10,13},{13,18},{14,17},{17,22},{1... | collective-permute-start | bytes 589832 | tf_op jit(solution)/shard_map/ppermute | solution.py:108
  79.2 1.9 %collective-permute-start.22 = (bf16[32,4096]{1,0:T(8,128)(2,1)S(1)}, bf16[32,4096]{1,0:T(8,128)(2,1)S(1)}, u32[]{:S(2)}, u32[]{:S(2)}) collective-permute-start(bf16[32,4096]{1,0:T(8,128)(2,1)S(1)} %apply_layer.22.before_ref), channel_id=1, source_target_pairs={{0,5},{1,4},{2,7},{3,6},{4,9},{5,8},{6,11},{7,10},{8,13},{9,12},{1... | collective-permute-start | bytes 786440 | tf_op jit(solution)/shard_map/ppermute | solution.py:108
  83.1 3.7 %collective-permute-start.24 = (bf16[32,4096]{1,0:T(8,128)(2,1)S(1)}, bf16[32,4096]{1,0:T(8,128)(2,1)S(1)}, u32[]{:S(2)}, u32[]{:S(2)}) collective-permute-start(bf16[32,4096]{1,0:T(8,128)(2,1)S(1)} %apply_layer.22.before_ref), channel_id=1, source_target_pairs={{1,6},{2,5},{5,10},{6,9},{9,14},{10,13},{13,18},{14,17},{17,22},{1... | collective-permute-start | bytes 786440 | tf_op jit(solution)/shard_map/ppermute | solution.py:108
  90.5 2.8 %collective-permute-start.26 = (bf16[24,4096]{1,0:T(8,128)(2,1)S(1)}, bf16[24,4096]{1,0:T(8,128)(2,1)S(1)}, u32[]{:S(2)}, u32[]{:S(2)}) collective-permute-start(bf16[24,4096]{1,0:T(8,128)(2,1)S(1)} %apply_layer.23.before_ref), channel_id=1, source_target_pairs={{0,4},{1,5},{2,6},{3,7},{4,8},{5,9},{6,10},{7,11},{8,12},{9,13},{1... | collective-permute-start | bytes 589832 | tf_op jit(solution)/shard_map/ppermute | solution.py:108
  93.4 3.1 %collective-permute-start.27 = (bf16[24,4096]{1,0:T(8,128)(2,1)S(1)}, bf16[24,4096]{1,0:T(8,128)(2,1)S(1)}, u32[]{:S(2)}, u32[]{:S(2)}) collective-permute-start(bf16[24,4096]{1,0:T(8,128)(2,1)S(1)} %apply_layer.23.before_ref), channel_id=1, source_target_pairs={{1,6},{2,5},{5,10},{6,9},{9,14},{10,13},{13,18},{14,17},{17,22},{1... | collective-permute-start | bytes 589832 | tf_op jit(solution)/shard_map/ppermute | solution.py:108
  102.7 3.7 %collective-permute-start.30 = (bf16[32,4096]{1,0:T(8,128)(2,1)S(1)}, bf16[32,4096]{1,0:T(8,128)(2,1)S(1)}, u32[]{:S(2)}, u32[]{:S(2)}) collective-permute-start(bf16[32,4096]{1,0:T(8,128)(2,1)S(1)} %apply_layer.24.before_ref), channel_id=1, source_target_pairs={{1,6},{2,5},{5,10},{6,9},{9,14},{10,13},{13,18},{14,17},{17,22},{1... | collective-permute-start | bytes 786440 | tf_op jit(solution)/shard_map/ppermute | solution.py:108
  110.2 2.8 %collective-permute-start.32 = (bf16[24,4096]{1,0:T(8,128)(2,1)S(1)}, bf16[24,4096]{1,0:T(8,128)(2,1)S(1)}, u32[]{:S(2)}, u32[]{:S(2)}) collective-permute-start(bf16[24,4096]{1,0:T(8,128)(2,1)S(1)} %apply_layer.25.before_ref), channel_id=1, source_target_pairs={{0,4},{1,5},{2,6},{3,7},{4,8},{5,9},{6,10},{7,11},{8,12},{9,13},{1... | collective-permute-start | bytes 589832 | tf_op jit(solution)/shard_map/ppermute | solution.py:108
  113.0 3.1 %collective-permute-start.33 = (bf16[24,4096]{1,0:T(8,128)(2,1)S(1)}, bf16[24,4096]{1,0:T(8,128)(2,1)S(1)}, u32[]{:S(2)}, u32[]{:S(2)}) collective-permute-start(bf16[24,4096]{1,0:T(8,128)(2,1)S(1)} %apply_layer.25.before_ref), channel_id=1, source_target_pairs={{1,6},{2,5},{5,10},{6,9},{9,14},{10,13},{13,18},{14,17},{17,22},{1... | collective-permute-start | bytes 589832 | tf_op jit(solution)/shard_map/ppermute | solution.py:108
  122.3 3.7 %collective-permute-start.36 = (bf16[32,4096]{1,0:T(8,128)(2,1)S(1)}, bf16[32,4096]{1,0:T(8,128)(2,1)S(1)}, u32[]{:S(2)}, u32[]{:S(2)}) collective-permute-start(bf16[32,4096]{1,0:T(8,128)(2,1)S(1)} %apply_layer.26.before_ref), channel_id=1, source_target_pairs={{1,6},{2,5},{5,10},{6,9},{9,14},{10,13},{13,18},{14,17},{17,22},{1... | collective-permute-start | bytes 786440 | tf_op jit(solution)/shard_map/ppermute | solution.py:108
  129.8 2.8 %collective-permute-start.38 = (bf16[24,4096]{1,0:T(8,128)(2,1)S(1)}, bf16[24,4096]{1,0:T(8,128)(2,1)S(1)}, u32[]{:S(2)}, u32[]{:S(2)}) collective-permute-start(bf16[24,4096]{1,0:T(8,128)(2,1)S(1)} %apply_layer.27.before_ref), channel_id=1, source_target_pairs={{0,4},{1,5},{2,6},{3,7},{4,8},{5,9},{6,10},{7,11},{8,12},{9,13},{1... | collective-permute-start | bytes 589832 | tf_op jit(solution)/shard_map/ppermute | solution.py:108
  132.7 3.1 %collective-permute-start.39 = (bf16[24,4096]{1,0:T(8,128)(2,1)S(1)}, bf16[24,4096]{1,0:T(8,128)(2,1)S(1)}, u32[]{:S(2)}, u32[]{:S(2)}) collective-permute-start(bf16[24,4096]{1,0:T(8,128)(2,1)S(1)} %apply_layer.27.before_ref), channel_id=1, source_target_pairs={{1,6},{2,5},{5,10},{6,9},{9,14},{10,13},{13,18},{14,17},{17,22},{1... | collective-permute-start | bytes 589832 | tf_op jit(solution)/shard_map/ppermute | solution.py:108
  142.0 3.7 %collective-permute-start.42 = (bf16[32,4096]{1,0:T(8,128)(2,1)S(1)}, bf16[32,4096]{1,0:T(8,128)(2,1)S(1)}, u32[]{:S(2)}, u32[]{:S(2)}) collective-permute-start(bf16[32,4096]{1,0:T(8,128)(2,1)S(1)} %apply_layer.28.before_ref), channel_id=1, source_target_pairs={{1,6},{2,5},{5,10},{6,9},{9,14},{10,13},{13,18},{14,17},{17,22},{1... | collective-permute-start | bytes 786440 | tf_op jit(solution)/shard_map/ppermute | solution.py:108
  149.5 2.8 %collective-permute-start.44 = (bf16[24,4096]{1,0:T(8,128)(2,1)S(1)}, bf16[24,4096]{1,0:T(8,128)(2,1)S(1)}, u32[]{:S(2)}, u32[]{:S(2)}) collective-permute-start(bf16[24,4096]{1,0:T(8,128)(2,1)S(1)} %apply_layer.29.before_ref), channel_id=1, source_target_pairs={{0,4},{1,5},{2,6},{3,7},{4,8},{5,9},{6,10},{7,11},{8,12},{9,13},{1... | collective-permute-start | bytes 589832 | tf_op jit(solution)/shard_map/ppermute | solution.py:108
  152.3 3.1 %collective-permute-start.45 = (bf16[24,4096]{1,0:T(8,128)(2,1)S(1)}, bf16[24,4096]{1,0:T(8,128)(2,1)S(1)}, u32[]{:S(2)}, u32[]{:S(2)}) collective-permute-start(bf16[24,4096]{1,0:T(8,128)(2,1)S(1)} %apply_layer.29.before_ref), channel_id=1, source_target_pairs={{1,6},{2,5},{5,10},{6,9},{9,14},{10,13},{13,18},{14,17},{17,22},{1... | collective-permute-start | bytes 589832 | tf_op jit(solution)/shard_map/ppermute | solution.py:108
  157.8 4.5 %collective-permute-done.45.far_ref = bf16[24,4096]{1,0:T(8,128)(2,1)S(1)} collective-permute-done((bf16[24,4096]{1,0:T(8,128)(2,1)S(1)}, bf16[24,4096]{1,0:T(8,128)(2,1)S(1)}, u32[]{:S(2)}, u32[]{:S(2)}) %collective-permute-start.45) | collective-permute-done | bytes 196640 | tf_op jit(solution)/shard_map/ppermute | solution.py:108
  (94 shorter events, 64.0 us)
Async XLA Ops:
  1.0 14.3 %collective-permute-start = (bf16[32,4096]{1,0:T(8,128)(2,1)S(1)}, bf16[32,4096]{1,0:T(8,128)(2,1)S(1)}, u32[]{:S(2)}, u32[]{:S(2)}) collective-permute-start(bf16[32,4096]{1,0:T(8,128)(2,1)S(1)} %slice_bitcast_fusion.own_ref), channel_id=1, source_target_pairs={{0,1},{1,0},{2,3},{3,2},{4,5},{5,4},{6,7},{7,6},{8,9},{9,8},{10,11... | collective-permute-start | bytes 786440 | tf_op jit(solution)/shard_map/ppermute | solution.py:108
  1.3 14.0 %collective-permute-start.1 = (bf16[32,4096]{1,0:T(8,128)(2,1)S(1)}, bf16[32,4096]{1,0:T(8,128)(2,1)S(1)}, u32[]{:S(2)}, u32[]{:S(2)}) collective-permute-start(bf16[32,4096]{1,0:T(8,128)(2,1)S(1)} %slice_bitcast_fusion.own_ref), channel_id=1, source_target_pairs={{1,2},{2,1},{5,6},{6,5},{9,10},{10,9},{13,14},{14,13},{17,18},{18,... | collective-permute-start | bytes 786440 | tf_op jit(solution)/shard_map/ppermute | solution.py:108
  6.3 21.2 %collective-permute-start.2 = (bf16[24,4096]{1,0:T(8,128)(2,1)S(1)}, bf16[24,4096]{1,0:T(8,128)(2,1)S(1)}, u32[]{:S(2)}, u32[]{:S(2)}) collective-permute-start(bf16[24,4096]{1,0:T(8,128)(2,1)S(1)} %slice_bitcast_fusion.1.own_ref), channel_id=1, source_target_pairs={{0,1},{1,0},{2,3},{3,2},{4,5},{5,4},{6,7},{7,6},{8,9},{9,8},{10,11... | collective-permute-start | bytes 589832 | tf_op jit(solution)/shard_map/ppermute | solution.py:108
  6.4 21.1 %collective-permute-start.3 = (bf16[24,4096]{1,0:T(8,128)(2,1)S(1)}, bf16[24,4096]{1,0:T(8,128)(2,1)S(1)}, u32[]{:S(2)}, u32[]{:S(2)}) collective-permute-start(bf16[24,4096]{1,0:T(8,128)(2,1)S(1)} %slice_bitcast_fusion.1.own_ref), channel_id=1, source_target_pairs={{1,2},{2,1},{5,6},{6,5},{9,10},{10,9},{13,14},{14,13},{17,18},{18,... | collective-permute-start | bytes 589832 | tf_op jit(solution)/shard_map/ppermute | solution.py:108
  17.2 17.8 %collective-permute-start.4 = (bf16[32,4096]{1,0:T(8,128)(2,1)S(1)}, bf16[32,4096]{1,0:T(8,128)(2,1)S(1)}, u32[]{:S(2)}, u32[]{:S(2)}) collective-permute-start(bf16[32,4096]{1,0:T(8,128)(2,1)S(1)} %apply_layer.16.before_ref), channel_id=1, source_target_pairs={{0,5},{1,4},{2,7},{3,6},{4,9},{5,8},{6,11},{7,10},{8,13},{9,12},{1... | collective-permute-start | bytes 786440 | tf_op jit(solution)/shard_map/ppermute | solution.py:108
  21.5 16.0 %collective-permute-start.5 = (bf16[32,4096]{1,0:T(8,128)(2,1)S(1)}, bf16[32,4096]{1,0:T(8,128)(2,1)S(1)}, u32[]{:S(2)}, u32[]{:S(2)}) collective-permute-start(bf16[32,4096]{1,0:T(8,128)(2,1)S(1)} %apply_layer.16.before_ref), channel_id=1, source_target_pairs={{0,4},{1,5},{2,6},{3,7},{4,8},{5,9},{6,10},{7,11},{8,12},{9,13},{1... | collective-permute-start | bytes 786440 | tf_op jit(solution)/shard_map/ppermute | solution.py:108
  29.3 14.2 %collective-permute-start.7 = (bf16[24,4096]{1,0:T(8,128)(2,1)S(1)}, bf16[24,4096]{1,0:T(8,128)(2,1)S(1)}, u32[]{:S(2)}, u32[]{:S(2)}) collective-permute-start(bf16[24,4096]{1,0:T(8,128)(2,1)S(1)} %apply_layer.17.before_ref), channel_id=1, source_target_pairs={{0,5},{1,4},{2,7},{3,6},{4,9},{5,8},{6,11},{7,10},{8,13},{9,12},{1... | collective-permute-start | bytes 589832 | tf_op jit(solution)/shard_map/ppermute | solution.py:108
  31.3 16.3 %collective-permute-start.8 = (bf16[24,4096]{1,0:T(8,128)(2,1)S(1)}, bf16[24,4096]{1,0:T(8,128)(2,1)S(1)}, u32[]{:S(2)}, u32[]{:S(2)}) collective-permute-start(bf16[24,4096]{1,0:T(8,128)(2,1)S(1)} %apply_layer.17.before_ref), channel_id=1, source_target_pairs={{0,4},{1,5},{2,6},{3,7},{4,8},{5,9},{6,10},{7,11},{8,12},{9,13},{1... | collective-permute-start | bytes 589832 | tf_op jit(solution)/shard_map/ppermute | solution.py:108
  39.5 14.5 %collective-permute-start.10 = (bf16[32,4096]{1,0:T(8,128)(2,1)S(1)}, bf16[32,4096]{1,0:T(8,128)(2,1)S(1)}, u32[]{:S(2)}, u32[]{:S(2)}) collective-permute-start(bf16[32,4096]{1,0:T(8,128)(2,1)S(1)} %apply_layer.18.before_ref), channel_id=1, source_target_pairs={{0,5},{1,4},{2,7},{3,6},{4,9},{5,8},{6,11},{7,10},{8,13},{9,12},{1... | collective-permute-start | bytes 786440 | tf_op jit(solution)/shard_map/ppermute | solution.py:108
  41.4 15.7 %collective-permute-start.11 = (bf16[32,4096]{1,0:T(8,128)(2,1)S(1)}, bf16[32,4096]{1,0:T(8,128)(2,1)S(1)}, u32[]{:S(2)}, u32[]{:S(2)}) collective-permute-start(bf16[32,4096]{1,0:T(8,128)(2,1)S(1)} %apply_layer.18.before_ref), channel_id=1, source_target_pairs={{0,4},{1,5},{2,6},{3,7},{4,8},{5,9},{6,10},{7,11},{8,12},{9,13},{1... | collective-permute-start | bytes 786440 | tf_op jit(solution)/shard_map/ppermute | solution.py:108
  43.5 14.1 %collective-permute-start.12 = (bf16[32,4096]{1,0:T(8,128)(2,1)S(1)}, bf16[32,4096]{1,0:T(8,128)(2,1)S(1)}, u32[]{:S(2)}, u32[]{:S(2)}) collective-permute-start(bf16[32,4096]{1,0:T(8,128)(2,1)S(1)} %apply_layer.18.before_ref), channel_id=1, source_target_pairs={{1,6},{2,5},{5,10},{6,9},{9,14},{10,13},{13,18},{14,17},{17,22},{1... | collective-permute-start | bytes 786440 | tf_op jit(solution)/shard_map/ppermute | solution.py:108
  51.3 15.8 %collective-permute-start.14 = (bf16[24,4096]{1,0:T(8,128)(2,1)S(1)}, bf16[24,4096]{1,0:T(8,128)(2,1)S(1)}, u32[]{:S(2)}, u32[]{:S(2)}) collective-permute-start(bf16[24,4096]{1,0:T(8,128)(2,1)S(1)} %apply_layer.19.before_ref), channel_id=1, source_target_pairs={{0,4},{1,5},{2,6},{3,7},{4,8},{5,9},{6,10},{7,11},{8,12},{9,13},{1... | collective-permute-start | bytes 589832 | tf_op jit(solution)/shard_map/ppermute | solution.py:108
  59.4 14.3 %collective-permute-start.16 = (bf16[32,4096]{1,0:T(8,128)(2,1)S(1)}, bf16[32,4096]{1,0:T(8,128)(2,1)S(1)}, u32[]{:S(2)}, u32[]{:S(2)}) collective-permute-start(bf16[32,4096]{1,0:T(8,128)(2,1)S(1)} %apply_layer.20.before_ref), channel_id=1, source_target_pairs={{0,5},{1,4},{2,7},{3,6},{4,9},{5,8},{6,11},{7,10},{8,13},{9,12},{1... | collective-permute-start | bytes 786440 | tf_op jit(solution)/shard_map/ppermute | solution.py:108
  61.3 15.5 %collective-permute-start.17 = (bf16[32,4096]{1,0:T(8,128)(2,1)S(1)}, bf16[32,4096]{1,0:T(8,128)(2,1)S(1)}, u32[]{:S(2)}, u32[]{:S(2)}) collective-permute-start(bf16[32,4096]{1,0:T(8,128)(2,1)S(1)} %apply_layer.20.before_ref), channel_id=1, source_target_pairs={{0,4},{1,5},{2,6},{3,7},{4,8},{5,9},{6,10},{7,11},{8,12},{9,13},{1... | collective-permute-start | bytes 786440 | tf_op jit(solution)/shard_map/ppermute | solution.py:108
  63.3 14.1 %collective-permute-start.18 = (bf16[32,4096]{1,0:T(8,128)(2,1)S(1)}, bf16[32,4096]{1,0:T(8,128)(2,1)S(1)}, u32[]{:S(2)}, u32[]{:S(2)}) collective-permute-start(bf16[32,4096]{1,0:T(8,128)(2,1)S(1)} %apply_layer.20.before_ref), channel_id=1, source_target_pairs={{1,6},{2,5},{5,10},{6,9},{9,14},{10,13},{13,18},{14,17},{17,22},{1... | collective-permute-start | bytes 786440 | tf_op jit(solution)/shard_map/ppermute | solution.py:108
  68.9 14.1 %collective-permute-start.19 = (bf16[24,4096]{1,0:T(8,128)(2,1)S(1)}, bf16[24,4096]{1,0:T(8,128)(2,1)S(1)}, u32[]{:S(2)}, u32[]{:S(2)}) collective-permute-start(bf16[24,4096]{1,0:T(8,128)(2,1)S(1)} %apply_layer.21.before_ref), channel_id=1, source_target_pairs={{0,5},{1,4},{2,7},{3,6},{4,9},{5,8},{6,11},{7,10},{8,13},{9,12},{1... | collective-permute-start | bytes 589832 | tf_op jit(solution)/shard_map/ppermute | solution.py:108
  70.8 15.9 %collective-permute-start.20 = (bf16[24,4096]{1,0:T(8,128)(2,1)S(1)}, bf16[24,4096]{1,0:T(8,128)(2,1)S(1)}, u32[]{:S(2)}, u32[]{:S(2)}) collective-permute-start(bf16[24,4096]{1,0:T(8,128)(2,1)S(1)} %apply_layer.21.before_ref), channel_id=1, source_target_pairs={{0,4},{1,5},{2,6},{3,7},{4,8},{5,9},{6,10},{7,11},{8,12},{9,13},{1... | collective-permute-start | bytes 589832 | tf_op jit(solution)/shard_map/ppermute | solution.py:108
  79.2 14.2 %collective-permute-start.22 = (bf16[32,4096]{1,0:T(8,128)(2,1)S(1)}, bf16[32,4096]{1,0:T(8,128)(2,1)S(1)}, u32[]{:S(2)}, u32[]{:S(2)}) collective-permute-start(bf16[32,4096]{1,0:T(8,128)(2,1)S(1)} %apply_layer.22.before_ref), channel_id=1, source_target_pairs={{0,5},{1,4},{2,7},{3,6},{4,9},{5,8},{6,11},{7,10},{8,13},{9,12},{1... | collective-permute-start | bytes 786440 | tf_op jit(solution)/shard_map/ppermute | solution.py:108
  81.1 15.4 %collective-permute-start.23 = (bf16[32,4096]{1,0:T(8,128)(2,1)S(1)}, bf16[32,4096]{1,0:T(8,128)(2,1)S(1)}, u32[]{:S(2)}, u32[]{:S(2)}) collective-permute-start(bf16[32,4096]{1,0:T(8,128)(2,1)S(1)} %apply_layer.22.before_ref), channel_id=1, source_target_pairs={{0,4},{1,5},{2,6},{3,7},{4,8},{5,9},{6,10},{7,11},{8,12},{9,13},{1... | collective-permute-start | bytes 786440 | tf_op jit(solution)/shard_map/ppermute | solution.py:108
  88.6 14.1 %collective-permute-start.25 = (bf16[24,4096]{1,0:T(8,128)(2,1)S(1)}, bf16[24,4096]{1,0:T(8,128)(2,1)S(1)}, u32[]{:S(2)}, u32[]{:S(2)}) collective-permute-start(bf16[24,4096]{1,0:T(8,128)(2,1)S(1)} %apply_layer.23.before_ref), channel_id=1, source_target_pairs={{0,5},{1,4},{2,7},{3,6},{4,9},{5,8},{6,11},{7,10},{8,13},{9,12},{1... | collective-permute-start | bytes 589832 | tf_op jit(solution)/shard_map/ppermute | solution.py:108
  90.5 15.9 %collective-permute-start.26 = (bf16[24,4096]{1,0:T(8,128)(2,1)S(1)}, bf16[24,4096]{1,0:T(8,128)(2,1)S(1)}, u32[]{:S(2)}, u32[]{:S(2)}) collective-permute-start(bf16[24,4096]{1,0:T(8,128)(2,1)S(1)} %apply_layer.23.before_ref), channel_id=1, source_target_pairs={{0,4},{1,5},{2,6},{3,7},{4,8},{5,9},{6,10},{7,11},{8,12},{9,13},{1... | collective-permute-start | bytes 589832 | tf_op jit(solution)/shard_map/ppermute | solution.py:108
  98.8 14.2 %collective-permute-start.28 = (bf16[32,4096]{1,0:T(8,128)(2,1)S(1)}, bf16[32,4096]{1,0:T(8,128)(2,1)S(1)}, u32[]{:S(2)}, u32[]{:S(2)}) collective-permute-start(bf16[32,4096]{1,0:T(8,128)(2,1)S(1)} %apply_layer.24.before_ref), channel_id=1, source_target_pairs={{0,5},{1,4},{2,7},{3,6},{4,9},{5,8},{6,11},{7,10},{8,13},{9,12},{1... | collective-permute-start | bytes 786440 | tf_op jit(solution)/shard_map/ppermute | solution.py:108
  100.7 15.4 %collective-permute-start.29 = (bf16[32,4096]{1,0:T(8,128)(2,1)S(1)}, bf16[32,4096]{1,0:T(8,128)(2,1)S(1)}, u32[]{:S(2)}, u32[]{:S(2)}) collective-permute-start(bf16[32,4096]{1,0:T(8,128)(2,1)S(1)} %apply_layer.24.before_ref), channel_id=1, source_target_pairs={{0,4},{1,5},{2,6},{3,7},{4,8},{5,9},{6,10},{7,11},{8,12},{9,13},{1... | collective-permute-start | bytes 786440 | tf_op jit(solution)/shard_map/ppermute | solution.py:108
  108.2 14.1 %collective-permute-start.31 = (bf16[24,4096]{1,0:T(8,128)(2,1)S(1)}, bf16[24,4096]{1,0:T(8,128)(2,1)S(1)}, u32[]{:S(2)}, u32[]{:S(2)}) collective-permute-start(bf16[24,4096]{1,0:T(8,128)(2,1)S(1)} %apply_layer.25.before_ref), channel_id=1, source_target_pairs={{0,5},{1,4},{2,7},{3,6},{4,9},{5,8},{6,11},{7,10},{8,13},{9,12},{1... | collective-permute-start | bytes 589832 | tf_op jit(solution)/shard_map/ppermute | solution.py:108
  110.2 15.9 %collective-permute-start.32 = (bf16[24,4096]{1,0:T(8,128)(2,1)S(1)}, bf16[24,4096]{1,0:T(8,128)(2,1)S(1)}, u32[]{:S(2)}, u32[]{:S(2)}) collective-permute-start(bf16[24,4096]{1,0:T(8,128)(2,1)S(1)} %apply_layer.25.before_ref), channel_id=1, source_target_pairs={{0,4},{1,5},{2,6},{3,7},{4,8},{5,9},{6,10},{7,11},{8,12},{9,13},{1... | collective-permute-start | bytes 589832 | tf_op jit(solution)/shard_map/ppermute | solution.py:108
  118.5 14.2 %collective-permute-start.34 = (bf16[32,4096]{1,0:T(8,128)(2,1)S(1)}, bf16[32,4096]{1,0:T(8,128)(2,1)S(1)}, u32[]{:S(2)}, u32[]{:S(2)}) collective-permute-start(bf16[32,4096]{1,0:T(8,128)(2,1)S(1)} %apply_layer.26.before_ref), channel_id=1, source_target_pairs={{0,5},{1,4},{2,7},{3,6},{4,9},{5,8},{6,11},{7,10},{8,13},{9,12},{1... | collective-permute-start | bytes 786440 | tf_op jit(solution)/shard_map/ppermute | solution.py:108
  120.4 15.4 %collective-permute-start.35 = (bf16[32,4096]{1,0:T(8,128)(2,1)S(1)}, bf16[32,4096]{1,0:T(8,128)(2,1)S(1)}, u32[]{:S(2)}, u32[]{:S(2)}) collective-permute-start(bf16[32,4096]{1,0:T(8,128)(2,1)S(1)} %apply_layer.26.before_ref), channel_id=1, source_target_pairs={{0,4},{1,5},{2,6},{3,7},{4,8},{5,9},{6,10},{7,11},{8,12},{9,13},{1... | collective-permute-start | bytes 786440 | tf_op jit(solution)/shard_map/ppermute | solution.py:108
  122.3 14.0 %collective-permute-start.36 = (bf16[32,4096]{1,0:T(8,128)(2,1)S(1)}, bf16[32,4096]{1,0:T(8,128)(2,1)S(1)}, u32[]{:S(2)}, u32[]{:S(2)}) collective-permute-start(bf16[32,4096]{1,0:T(8,128)(2,1)S(1)} %apply_layer.26.before_ref), channel_id=1, source_target_pairs={{1,6},{2,5},{5,10},{6,9},{9,14},{10,13},{13,18},{14,17},{17,22},{1... | collective-permute-start | bytes 786440 | tf_op jit(solution)/shard_map/ppermute | solution.py:108
  127.9 14.1 %collective-permute-start.37 = (bf16[24,4096]{1,0:T(8,128)(2,1)S(1)}, bf16[24,4096]{1,0:T(8,128)(2,1)S(1)}, u32[]{:S(2)}, u32[]{:S(2)}) collective-permute-start(bf16[24,4096]{1,0:T(8,128)(2,1)S(1)} %apply_layer.27.before_ref), channel_id=1, source_target_pairs={{0,5},{1,4},{2,7},{3,6},{4,9},{5,8},{6,11},{7,10},{8,13},{9,12},{1... | collective-permute-start | bytes 589832 | tf_op jit(solution)/shard_map/ppermute | solution.py:108
  129.8 15.9 %collective-permute-start.38 = (bf16[24,4096]{1,0:T(8,128)(2,1)S(1)}, bf16[24,4096]{1,0:T(8,128)(2,1)S(1)}, u32[]{:S(2)}, u32[]{:S(2)}) collective-permute-start(bf16[24,4096]{1,0:T(8,128)(2,1)S(1)} %apply_layer.27.before_ref), channel_id=1, source_target_pairs={{0,4},{1,5},{2,6},{3,7},{4,8},{5,9},{6,10},{7,11},{8,12},{9,13},{1... | collective-permute-start | bytes 589832 | tf_op jit(solution)/shard_map/ppermute | solution.py:108
  138.1 14.2 %collective-permute-start.40 = (bf16[32,4096]{1,0:T(8,128)(2,1)S(1)}, bf16[32,4096]{1,0:T(8,128)(2,1)S(1)}, u32[]{:S(2)}, u32[]{:S(2)}) collective-permute-start(bf16[32,4096]{1,0:T(8,128)(2,1)S(1)} %apply_layer.28.before_ref), channel_id=1, source_target_pairs={{0,5},{1,4},{2,7},{3,6},{4,9},{5,8},{6,11},{7,10},{8,13},{9,12},{1... | collective-permute-start | bytes 786440 | tf_op jit(solution)/shard_map/ppermute | solution.py:108
  140.1 15.4 %collective-permute-start.41 = (bf16[32,4096]{1,0:T(8,128)(2,1)S(1)}, bf16[32,4096]{1,0:T(8,128)(2,1)S(1)}, u32[]{:S(2)}, u32[]{:S(2)}) collective-permute-start(bf16[32,4096]{1,0:T(8,128)(2,1)S(1)} %apply_layer.28.before_ref), channel_id=1, source_target_pairs={{0,4},{1,5},{2,6},{3,7},{4,8},{5,9},{6,10},{7,11},{8,12},{9,13},{1... | collective-permute-start | bytes 786440 | tf_op jit(solution)/shard_map/ppermute | solution.py:108
  (16 other events, 183.3 us)

commit v3 on v2

--- a/solution.py
+++ b/solution.py
@@ -54,14 +54,13 @@
     )(prop)
 
 
-def tick_kernel(tick, first, cols_ref, weights_ref, near_ref, own_ref, far_ref, source_ref, before_ref, out_ref, window):
-    del before_ref
-    shots, width = own_ref.shape
+def tick_kernel(tick, first, places, cols_ref, weights_ref, *refs):
+    thirds, (source_ref, _, out_ref, window) = refs[:len(places)], refs[len(places):]
+    shots, width = out_ref.shape
     row_blocks, depth, blk = weights_ref.shape
     slots = depth // blk
-    window[:, :width] = near_ref[...]
-    window[:, width:2 * width] = own_ref[...]
-    window[:, 2 * width:] = far_ref[...]
+    for place, third_ref in zip(places, thirds):
+        window[:, place * width:(place + 1) * width] = third_ref[...]
 
     def step(r, carry):
         picked = []
@@ -73,14 +72,14 @@
         out_ref[:, here] = (mixed + source_ref[tick, 0, first:first + shots, here].astype(jnp.float32)).astype(out_ref.dtype)
         return carry
 
-    lax.fori_loop(0, row_blocks, step, 0, unroll=min(16, row_blocks))
+    lax.fori_loop(0, row_blocks, step, 0, unroll=True)
 
 
-def apply_layer(tick, first, cols, weights, near, own, far, sources, before):
-    shots, width = own.shape
+def apply_layer(tick, first, places, cols, weights, thirds, sources, before):
+    shots, width = thirds[0].shape
     vmem = pl.BlockSpec(memory_space=pltpu.VMEM)
     return pl.pallas_call(
-        functools.partial(tick_kernel, tick, first),
+        functools.partial(tick_kernel, tick, first, places),
         in_specs=[pl.BlockSpec(memory_space=pltpu.SMEM)] + [vmem] * 5 + [pl.BlockSpec(memory_space=pl.ANY)],
         out_specs=vmem,
         out_shape=jax.ShapeDtypeStruct((shots, width), jnp.bfloat16),
@@ -90,7 +89,7 @@
             flops=2 * shots * weights.size, bytes_accessed=weights.size * 2, transcendentals=0
         ),
         name="apply_layer",
-    )(cols, weights, near, own, far, sources, before)
+    )(cols, weights, *thirds, sources, before)
 
 
 def partner(r, rows, far):
@@ -122,6 +121,7 @@
     cols = (third * block_count + lax.rem(col_blocks[0], block_count)).reshape(-1)
     cut = (shots // 16 + 1) // 2 * 16
     panels = [(0, cut), (cut, shots)]
+    orders = [(0, 2, 1), (0, 1, 2)]
     arriving = []
     for a, b in panels:
         own = incoming[0, a:b]
@@ -133,7 +133,8 @@
     for tick in range(ticks):
         produced = []
         for i in range(len(panels)):
-            done = apply_layer(tick, panels[i][0], cols, weights, *arriving[i], sources, before)
+            thirds = [arriving[i][place] for place in orders[i]]
+            done = apply_layer(tick, panels[i][0], orders[i], cols, weights, thirds, sources, before)
             before = done
             produced.append(done)
             if tick + 1 < ticks:

time: 168 us -> 172 us (1.024)
  starting transfers between devices: 118 us -> 123 us
  Pallas kernels: 34.6 us -> 32.3 us
    ppermute x46, starting transfers between devices: 118 us -> 123 us  [send(): return lax.ppermute(value, ('layer', 'row'), pairs)]
    pallas_call x16, Pallas kernels: 28.7 us -> 26.4 us  [apply_layer(): pl.pallas_call(functools.partial(tick_kernel, tick, first, places), in_sp...]
  transfers between devices with their start and end apart: 46 -> 46, of which waited for: 8 -> 5; matrix products, arithmetic and copies ran while one was open for 1% -> 1% of each run, Pallas kernels for 20% -> 18%
where the time goes in v3:
time: 172 us; the launch traced here: 169 us
  starting transfers between devices  123 us (72%)
  Pallas kernels  32.3 us (19%)
  waiting for transfers between devices  8.33 us (5%)
  local copies, waits for them, and re-layouts  4.62 us (3%)
    ppermute x46, starting transfers between devices, send(): return lax.ppermute(value, ('layer', 'row'), pairs)  123 us
    pallas_call x16, Pallas kernels, apply_layer(): pl.pallas_call(functools.partial(tick_kernel, tick, first, places), in_sp...  26.4 us
    ppermute x46, waiting for transfers between devices, send(): return lax.ppermute(value, ('layer', 'row'), pairs)  8.33 us
    pallas_call x1, Pallas kernels, convert_weights(): pl.pallas_call(convert_kernel, in_specs=[pl.BlockSpec(memory_space=pltpu....  5.89 us
  transfers between devices with their start and end apart: 46, of which 5 were waited for; matrix products, arithmetic and copies ran while one was open for 1% of the time, Pallas kernels for 18%

profile of v3, /device:TPU:11, one launch (start us, length us, event | category | flops | bytes accessed | tf_op | source)
XLA Modules:
  0.0 169.4 jit_solution(16946883254821560853)
XLA Ops:
  1.3 4.1 %collective-permute-start.1 = (bf16[32,4096]{1,0:T(8,128)(2,1)S(1)}, bf16[32,4096]{1,0:T(8,128)(2,1)S(1)}, u32[]{:S(2)}, u32[]{:S(2)}) collective-permute-start(bf16[32,4096]{1,0:T(8,128)(2,1)S(1)} %slice_bitcast_fusion.refs_2_), channel_id=1, source_target_pairs={{1,2},{2,1},{5,6},{6,5},{9,10},{10,9},{13,14},{14,13},{17,18},{18,... | collective-permute-start | bytes 786440 | tf_op jit(solution)/shard_map/ppermute | solution.py:107
  6.4 2.1 %collective-permute-start.3 = (bf16[24,4096]{1,0:T(8,128)(2,1)S(1)}, bf16[24,4096]{1,0:T(8,128)(2,1)S(1)}, u32[]{:S(2)}, u32[]{:S(2)}) collective-permute-start(bf16[24,4096]{1,0:T(8,128)(2,1)S(1)} %slice_bitcast_fusion.1.refs_1_), channel_id=1, source_target_pairs={{1,2},{2,1},{5,6},{6,5},{9,10},{10,9},{13,14},{14,13},{17,18},{18,... | collective-permute-start | bytes 589832 | tf_op jit(solution)/shard_map/ppermute | solution.py:107
  9.4 5.9 %convert_weights.1.weights_ref.refs_4_ = bf16[32,768,128]{2,1,0:T(8,128)(2,1)S(1)} custom-call(f32[6,4096,128]{2,1,0:T(8,128)} %bitcast.42), custom_call_target="tpu_custom_call" | custom-call | bytes 12582912 | tf_op jit(solution)/shard_map/convert_weights/pallas_call | solution.py:42
  17.0 4.3 %collective-permute-start.4 = (bf16[32,4096]{1,0:T(8,128)(2,1)S(1)}, bf16[32,4096]{1,0:T(8,128)(2,1)S(1)}, u32[]{:S(2)}, u32[]{:S(2)}) collective-permute-start(bf16[32,4096]{1,0:T(8,128)(2,1)S(1)} %apply_layer.16.refs_4_), channel_id=1, source_target_pairs={{0,5},{1,4},{2,7},{3,6},{4,9},{5,8},{6,11},{7,10},{8,13},{9,12},{1... | collective-permute-start | bytes 786440 | tf_op jit(solution)/shard_map/ppermute | solution.py:107
  21.4 4.1 %collective-permute-start.5 = (bf16[32,4096]{1,0:T(8,128)(2,1)S(1)}, bf16[32,4096]{1,0:T(8,128)(2,1)S(1)}, u32[]{:S(2)}, u32[]{:S(2)}) collective-permute-start(bf16[32,4096]{1,0:T(8,128)(2,1)S(1)} %apply_layer.16.refs_4_), channel_id=1, source_target_pairs={{1,6},{2,5},{5,10},{6,9},{9,14},{10,13},{13,18},{14,17},{17,22},{1... | collective-permute-start | bytes 786440 | tf_op jit(solution)/shard_map/ppermute | solution.py:107
  25.4 1.9 %collective-permute-start.6 = (bf16[32,4096]{1,0:T(8,128)(2,1)S(1)}, bf16[32,4096]{1,0:T(8,128)(2,1)S(1)}, u32[]{:S(2)}, u32[]{:S(2)}) collective-permute-start(bf16[32,4096]{1,0:T(8,128)(2,1)S(1)} %apply_layer.16.refs_4_), channel_id=1, source_target_pairs={{0,4},{1,5},{2,6},{3,7},{4,8},{5,9},{6,10},{7,11},{8,12},{9,13},{1... | collective-permute-start | bytes 786440 | tf_op jit(solution)/shard_map/ppermute | solution.py:107
  29.0 2.0 %collective-permute-start.7 = (bf16[24,4096]{1,0:T(8,128)(2,1)S(1)}, bf16[24,4096]{1,0:T(8,128)(2,1)S(1)}, u32[]{:S(2)}, u32[]{:S(2)}) collective-permute-start(bf16[24,4096]{1,0:T(8,128)(2,1)S(1)} %apply_layer.17.refs_4_), channel_id=1, source_target_pairs={{0,5},{1,4},{2,7},{3,6},{4,9},{5,8},{6,11},{7,10},{8,13},{9,12},{1... | collective-permute-start | bytes 589832 | tf_op jit(solution)/shard_map/ppermute | solution.py:107
  31.0 3.5 %collective-permute-start.8 = (bf16[24,4096]{1,0:T(8,128)(2,1)S(1)}, bf16[24,4096]{1,0:T(8,128)(2,1)S(1)}, u32[]{:S(2)}, u32[]{:S(2)}) collective-permute-start(bf16[24,4096]{1,0:T(8,128)(2,1)S(1)} %apply_layer.17.refs_4_), channel_id=1, source_target_pairs={{0,4},{1,5},{2,6},{3,7},{4,8},{5,9},{6,10},{7,11},{8,12},{9,13},{1... | collective-permute-start | bytes 589832 | tf_op jit(solution)/shard_map/ppermute | solution.py:107
  34.6 2.5 %collective-permute-start.9 = (bf16[24,4096]{1,0:T(8,128)(2,1)S(1)}, bf16[24,4096]{1,0:T(8,128)(2,1)S(1)}, u32[]{:S(2)}, u32[]{:S(2)}) collective-permute-start(bf16[24,4096]{1,0:T(8,128)(2,1)S(1)} %apply_layer.17.refs_4_), channel_id=1, source_target_pairs={{1,6},{2,5},{5,10},{6,9},{9,14},{10,13},{13,18},{14,17},{17,22},{1... | collective-permute-start | bytes 589832 | tf_op jit(solution)/shard_map/ppermute | solution.py:107
  39.1 2.0 %collective-permute-start.10 = (bf16[32,4096]{1,0:T(8,128)(2,1)S(1)}, bf16[32,4096]{1,0:T(8,128)(2,1)S(1)}, u32[]{:S(2)}, u32[]{:S(2)}) collective-permute-start(bf16[32,4096]{1,0:T(8,128)(2,1)S(1)} %apply_layer.18.refs_4_), channel_id=1, source_target_pairs={{0,5},{1,4},{2,7},{3,6},{4,9},{5,8},{6,11},{7,10},{8,13},{9,12},{1... | collective-permute-start | bytes 786440 | tf_op jit(solution)/shard_map/ppermute | solution.py:107
  41.1 4.2 %collective-permute-start.11 = (bf16[32,4096]{1,0:T(8,128)(2,1)S(1)}, bf16[32,4096]{1,0:T(8,128)(2,1)S(1)}, u32[]{:S(2)}, u32[]{:S(2)}) collective-permute-start(bf16[32,4096]{1,0:T(8,128)(2,1)S(1)} %apply_layer.18.refs_4_), channel_id=1, source_target_pairs={{1,6},{2,5},{5,10},{6,9},{9,14},{10,13},{13,18},{14,17},{17,22},{1... | collective-permute-start | bytes 786440 | tf_op jit(solution)/shard_map/ppermute | solution.py:107
  50.9 2.8 %collective-permute-start.14 = (bf16[24,4096]{1,0:T(8,128)(2,1)S(1)}, bf16[24,4096]{1,0:T(8,128)(2,1)S(1)}, u32[]{:S(2)}, u32[]{:S(2)}) collective-permute-start(bf16[24,4096]{1,0:T(8,128)(2,1)S(1)} %apply_layer.19.refs_4_), channel_id=1, source_target_pairs={{0,4},{1,5},{2,6},{3,7},{4,8},{5,9},{6,10},{7,11},{8,12},{9,13},{1... | collective-permute-start | bytes 589832 | tf_op jit(solution)/shard_map/ppermute | solution.py:107
  53.7 3.9 %collective-permute-start.15 = (bf16[24,4096]{1,0:T(8,128)(2,1)S(1)}, bf16[24,4096]{1,0:T(8,128)(2,1)S(1)}, u32[]{:S(2)}, u32[]{:S(2)}) collective-permute-start(bf16[24,4096]{1,0:T(8,128)(2,1)S(1)} %apply_layer.19.refs_4_), channel_id=1, source_target_pairs={{1,6},{2,5},{5,10},{6,9},{9,14},{10,13},{13,18},{14,17},{17,22},{1... | collective-permute-start | bytes 589832 | tf_op jit(solution)/shard_map/ppermute | solution.py:107
  59.4 2.5 %collective-permute-start.16 = (bf16[32,4096]{1,0:T(8,128)(2,1)S(1)}, bf16[32,4096]{1,0:T(8,128)(2,1)S(1)}, u32[]{:S(2)}, u32[]{:S(2)}) collective-permute-start(bf16[32,4096]{1,0:T(8,128)(2,1)S(1)} %apply_layer.20.refs_4_), channel_id=1, source_target_pairs={{0,5},{1,4},{2,7},{3,6},{4,9},{5,8},{6,11},{7,10},{8,13},{9,12},{1... | collective-permute-start | bytes 786440 | tf_op jit(solution)/shard_map/ppermute | solution.py:107
  61.9 4.1 %collective-permute-start.17 = (bf16[32,4096]{1,0:T(8,128)(2,1)S(1)}, bf16[32,4096]{1,0:T(8,128)(2,1)S(1)}, u32[]{:S(2)}, u32[]{:S(2)}) collective-permute-start(bf16[32,4096]{1,0:T(8,128)(2,1)S(1)} %apply_layer.20.refs_4_), channel_id=1, source_target_pairs={{1,6},{2,5},{5,10},{6,9},{9,14},{10,13},{13,18},{14,17},{17,22},{1... | collective-permute-start | bytes 786440 | tf_op jit(solution)/shard_map/ppermute | solution.py:107
  66.0 3.0 %collective-permute-start.18 = (bf16[32,4096]{1,0:T(8,128)(2,1)S(1)}, bf16[32,4096]{1,0:T(8,128)(2,1)S(1)}, u32[]{:S(2)}, u32[]{:S(2)}) collective-permute-start(bf16[32,4096]{1,0:T(8,128)(2,1)S(1)} %apply_layer.20.refs_4_), channel_id=1, source_target_pairs={{0,4},{1,5},{2,6},{3,7},{4,8},{5,9},{6,10},{7,11},{8,12},{9,13},{1... | collective-permute-start | bytes 786440 | tf_op jit(solution)/shard_map/ppermute | solution.py:107
  74.5 2.4 %collective-permute-start.21 = (bf16[24,4096]{1,0:T(8,128)(2,1)S(1)}, bf16[24,4096]{1,0:T(8,128)(2,1)S(1)}, u32[]{:S(2)}, u32[]{:S(2)}) collective-permute-start(bf16[24,4096]{1,0:T(8,128)(2,1)S(1)} %apply_layer.21.refs_4_), channel_id=1, source_target_pairs={{1,6},{2,5},{5,10},{6,9},{9,14},{10,13},{13,18},{14,17},{17,22},{1... | collective-permute-start | bytes 589832 | tf_op jit(solution)/shard_map/ppermute | solution.py:107
  80.8 3.8 %collective-permute-start.23 = (bf16[32,4096]{1,0:T(8,128)(2,1)S(1)}, bf16[32,4096]{1,0:T(8,128)(2,1)S(1)}, u32[]{:S(2)}, u32[]{:S(2)}) collective-permute-start(bf16[32,4096]{1,0:T(8,128)(2,1)S(1)} %apply_layer.22.refs_4_), channel_id=1, source_target_pairs={{1,6},{2,5},{5,10},{6,9},{9,14},{10,13},{13,18},{14,17},{17,22},{1... | collective-permute-start | bytes 786440 | tf_op jit(solution)/shard_map/ppermute | solution.py:107
  84.6 2.8 %collective-permute-start.24 = (bf16[32,4096]{1,0:T(8,128)(2,1)S(1)}, bf16[32,4096]{1,0:T(8,128)(2,1)S(1)}, u32[]{:S(2)}, u32[]{:S(2)}) collective-permute-start(bf16[32,4096]{1,0:T(8,128)(2,1)S(1)} %apply_layer.22.refs_4_), channel_id=1, source_target_pairs={{0,4},{1,5},{2,6},{3,7},{4,8},{5,9},{6,10},{7,11},{8,12},{9,13},{1... | collective-permute-start | bytes 786440 | tf_op jit(solution)/shard_map/ppermute | solution.py:107
  91.1 2.2 %collective-permute-start.26 = (bf16[24,4096]{1,0:T(8,128)(2,1)S(1)}, bf16[24,4096]{1,0:T(8,128)(2,1)S(1)}, u32[]{:S(2)}, u32[]{:S(2)}) collective-permute-start(bf16[24,4096]{1,0:T(8,128)(2,1)S(1)} %apply_layer.23.refs_4_), channel_id=1, source_target_pairs={{0,4},{1,5},{2,6},{3,7},{4,8},{5,9},{6,10},{7,11},{8,12},{9,13},{1... | collective-permute-start | bytes 589832 | tf_op jit(solution)/shard_map/ppermute | solution.py:107
  93.3 5.3 %collective-permute-start.27 = (bf16[24,4096]{1,0:T(8,128)(2,1)S(1)}, bf16[24,4096]{1,0:T(8,128)(2,1)S(1)}, u32[]{:S(2)}, u32[]{:S(2)}) collective-permute-start(bf16[24,4096]{1,0:T(8,128)(2,1)S(1)} %apply_layer.23.refs_4_), channel_id=1, source_target_pairs={{1,6},{2,5},{5,10},{6,9},{9,14},{10,13},{13,18},{14,17},{17,22},{1... | collective-permute-start | bytes 589832 | tf_op jit(solution)/shard_map/ppermute | solution.py:107
  100.3 2.6 %collective-permute-start.28 = (bf16[32,4096]{1,0:T(8,128)(2,1)S(1)}, bf16[32,4096]{1,0:T(8,128)(2,1)S(1)}, u32[]{:S(2)}, u32[]{:S(2)}) collective-permute-start(bf16[32,4096]{1,0:T(8,128)(2,1)S(1)} %apply_layer.24.refs_4_), channel_id=1, source_target_pairs={{0,5},{1,4},{2,7},{3,6},{4,9},{5,8},{6,11},{7,10},{8,13},{9,12},{1... | collective-permute-start | bytes 786440 | tf_op jit(solution)/shard_map/ppermute | solution.py:107
  102.9 4.1 %collective-permute-start.29 = (bf16[32,4096]{1,0:T(8,128)(2,1)S(1)}, bf16[32,4096]{1,0:T(8,128)(2,1)S(1)}, u32[]{:S(2)}, u32[]{:S(2)}) collective-permute-start(bf16[32,4096]{1,0:T(8,128)(2,1)S(1)} %apply_layer.24.refs_4_), channel_id=1, source_target_pairs={{1,6},{2,5},{5,10},{6,9},{9,14},{10,13},{13,18},{14,17},{17,22},{1... | collective-permute-start | bytes 786440 | tf_op jit(solution)/shard_map/ppermute | solution.py:107
  114.5 2.3 %collective-permute-start.33 = (bf16[24,4096]{1,0:T(8,128)(2,1)S(1)}, bf16[24,4096]{1,0:T(8,128)(2,1)S(1)}, u32[]{:S(2)}, u32[]{:S(2)}) collective-permute-start(bf16[24,4096]{1,0:T(8,128)(2,1)S(1)} %apply_layer.25.refs_4_), channel_id=1, source_target_pairs={{1,6},{2,5},{5,10},{6,9},{9,14},{10,13},{13,18},{14,17},{17,22},{1... | collective-permute-start | bytes 589832 | tf_op jit(solution)/shard_map/ppermute | solution.py:107
  121.4 3.9 %collective-permute-start.35 = (bf16[32,4096]{1,0:T(8,128)(2,1)S(1)}, bf16[32,4096]{1,0:T(8,128)(2,1)S(1)}, u32[]{:S(2)}, u32[]{:S(2)}) collective-permute-start(bf16[32,4096]{1,0:T(8,128)(2,1)S(1)} %apply_layer.26.refs_4_), channel_id=1, source_target_pairs={{1,6},{2,5},{5,10},{6,9},{9,14},{10,13},{13,18},{14,17},{17,22},{1... | collective-permute-start | bytes 786440 | tf_op jit(solution)/shard_map/ppermute | solution.py:107
  125.3 2.8 %collective-permute-start.36 = (bf16[32,4096]{1,0:T(8,128)(2,1)S(1)}, bf16[32,4096]{1,0:T(8,128)(2,1)S(1)}, u32[]{:S(2)}, u32[]{:S(2)}) collective-permute-start(bf16[32,4096]{1,0:T(8,128)(2,1)S(1)} %apply_layer.26.refs_4_), channel_id=1, source_target_pairs={{0,4},{1,5},{2,6},{3,7},{4,8},{5,9},{6,10},{7,11},{8,12},{9,13},{1... | collective-permute-start | bytes 786440 | tf_op jit(solution)/shard_map/ppermute | solution.py:107
  131.8 1.9 %collective-permute-start.38 = (bf16[24,4096]{1,0:T(8,128)(2,1)S(1)}, bf16[24,4096]{1,0:T(8,128)(2,1)S(1)}, u32[]{:S(2)}, u32[]{:S(2)}) collective-permute-start(bf16[24,4096]{1,0:T(8,128)(2,1)S(1)} %apply_layer.27.refs_4_), channel_id=1, source_target_pairs={{0,4},{1,5},{2,6},{3,7},{4,8},{5,9},{6,10},{7,11},{8,12},{9,13},{1... | collective-permute-start | bytes 589832 | tf_op jit(solution)/shard_map/ppermute | solution.py:107
  133.7 5.5 %collective-permute-start.39 = (bf16[24,4096]{1,0:T(8,128)(2,1)S(1)}, bf16[24,4096]{1,0:T(8,128)(2,1)S(1)}, u32[]{:S(2)}, u32[]{:S(2)}) collective-permute-start(bf16[24,4096]{1,0:T(8,128)(2,1)S(1)} %apply_layer.27.refs_4_), channel_id=1, source_target_pairs={{1,6},{2,5},{5,10},{6,9},{9,14},{10,13},{13,18},{14,17},{17,22},{1... | collective-permute-start | bytes 589832 | tf_op jit(solution)/shard_map/ppermute | solution.py:107
  140.9 2.6 %collective-permute-start.40 = (bf16[32,4096]{1,0:T(8,128)(2,1)S(1)}, bf16[32,4096]{1,0:T(8,128)(2,1)S(1)}, u32[]{:S(2)}, u32[]{:S(2)}) collective-permute-start(bf16[32,4096]{1,0:T(8,128)(2,1)S(1)} %apply_layer.28.refs_4_), channel_id=1, source_target_pairs={{0,5},{1,4},{2,7},{3,6},{4,9},{5,8},{6,11},{7,10},{8,13},{9,12},{1... | collective-permute-start | bytes 786440 | tf_op jit(solution)/shard_map/ppermute | solution.py:107
  143.5 4.1 %collective-permute-start.41 = (bf16[32,4096]{1,0:T(8,128)(2,1)S(1)}, bf16[32,4096]{1,0:T(8,128)(2,1)S(1)}, u32[]{:S(2)}, u32[]{:S(2)}) collective-permute-start(bf16[32,4096]{1,0:T(8,128)(2,1)S(1)} %apply_layer.28.refs_4_), channel_id=1, source_target_pairs={{1,6},{2,5},{5,10},{6,9},{9,14},{10,13},{13,18},{14,17},{17,22},{1... | collective-permute-start | bytes 786440 | tf_op jit(solution)/shard_map/ppermute | solution.py:107
  155.0 2.5 %collective-permute-start.45 = (bf16[24,4096]{1,0:T(8,128)(2,1)S(1)}, bf16[24,4096]{1,0:T(8,128)(2,1)S(1)}, u32[]{:S(2)}, u32[]{:S(2)}) collective-permute-start(bf16[24,4096]{1,0:T(8,128)(2,1)S(1)} %apply_layer.29.refs_4_), channel_id=1, source_target_pairs={{1,6},{2,5},{5,10},{6,9},{9,14},{10,13},{13,18},{14,17},{17,22},{1... | collective-permute-start | bytes 589832 | tf_op jit(solution)/shard_map/ppermute | solution.py:107
  160.4 5.5 %collective-permute-done.45.refs_2_ = bf16[24,4096]{1,0:T(8,128)(2,1)S(1)} collective-permute-done((bf16[24,4096]{1,0:T(8,128)(2,1)S(1)}, bf16[24,4096]{1,0:T(8,128)(2,1)S(1)}, u32[]{:S(2)}, u32[]{:S(2)}) %collective-permute-start.45) | collective-permute-done | bytes 196640 | tf_op jit(solution)/shard_map/ppermute | solution.py:107
  (94 shorter events, 61.5 us)
Async XLA Ops:
  1.0 14.3 %collective-permute-start = (bf16[32,4096]{1,0:T(8,128)(2,1)S(1)}, bf16[32,4096]{1,0:T(8,128)(2,1)S(1)}, u32[]{:S(2)}, u32[]{:S(2)}) collective-permute-start(bf16[32,4096]{1,0:T(8,128)(2,1)S(1)} %slice_bitcast_fusion.refs_2_), channel_id=1, source_target_pairs={{0,1},{1,0},{2,3},{3,2},{4,5},{5,4},{6,7},{7,6},{8,9},{9,8},{10,11... | collective-permute-start | bytes 786440 | tf_op jit(solution)/shard_map/ppermute | solution.py:107
  1.3 14.0 %collective-permute-start.1 = (bf16[32,4096]{1,0:T(8,128)(2,1)S(1)}, bf16[32,4096]{1,0:T(8,128)(2,1)S(1)}, u32[]{:S(2)}, u32[]{:S(2)}) collective-permute-start(bf16[32,4096]{1,0:T(8,128)(2,1)S(1)} %slice_bitcast_fusion.refs_2_), channel_id=1, source_target_pairs={{1,2},{2,1},{5,6},{6,5},{9,10},{10,9},{13,14},{14,13},{17,18},{18,... | collective-permute-start | bytes 786440 | tf_op jit(solution)/shard_map/ppermute | solution.py:107
  6.3 21.1 %collective-permute-start.2 = (bf16[24,4096]{1,0:T(8,128)(2,1)S(1)}, bf16[24,4096]{1,0:T(8,128)(2,1)S(1)}, u32[]{:S(2)}, u32[]{:S(2)}) collective-permute-start(bf16[24,4096]{1,0:T(8,128)(2,1)S(1)} %slice_bitcast_fusion.1.refs_1_), channel_id=1, source_target_pairs={{0,1},{1,0},{2,3},{3,2},{4,5},{5,4},{6,7},{7,6},{8,9},{9,8},{10,11... | collective-permute-start | bytes 589832 | tf_op jit(solution)/shard_map/ppermute | solution.py:107
  6.4 21.0 %collective-permute-start.3 = (bf16[24,4096]{1,0:T(8,128)(2,1)S(1)}, bf16[24,4096]{1,0:T(8,128)(2,1)S(1)}, u32[]{:S(2)}, u32[]{:S(2)}) collective-permute-start(bf16[24,4096]{1,0:T(8,128)(2,1)S(1)} %slice_bitcast_fusion.1.refs_1_), channel_id=1, source_target_pairs={{1,2},{2,1},{5,6},{6,5},{9,10},{10,9},{13,14},{14,13},{17,18},{18,... | collective-permute-start | bytes 589832 | tf_op jit(solution)/shard_map/ppermute | solution.py:107
  17.0 17.5 %collective-permute-start.4 = (bf16[32,4096]{1,0:T(8,128)(2,1)S(1)}, bf16[32,4096]{1,0:T(8,128)(2,1)S(1)}, u32[]{:S(2)}, u32[]{:S(2)}) collective-permute-start(bf16[32,4096]{1,0:T(8,128)(2,1)S(1)} %apply_layer.16.refs_4_), channel_id=1, source_target_pairs={{0,5},{1,4},{2,7},{3,6},{4,9},{5,8},{6,11},{7,10},{8,13},{9,12},{1... | collective-permute-start | bytes 786440 | tf_op jit(solution)/shard_map/ppermute | solution.py:107
  21.4 16.1 %collective-permute-start.5 = (bf16[32,4096]{1,0:T(8,128)(2,1)S(1)}, bf16[32,4096]{1,0:T(8,128)(2,1)S(1)}, u32[]{:S(2)}, u32[]{:S(2)}) collective-permute-start(bf16[32,4096]{1,0:T(8,128)(2,1)S(1)} %apply_layer.16.refs_4_), channel_id=1, source_target_pairs={{1,6},{2,5},{5,10},{6,9},{9,14},{10,13},{13,18},{14,17},{17,22},{1... | collective-permute-start | bytes 786440 | tf_op jit(solution)/shard_map/ppermute | solution.py:107
  29.0 16.3 %collective-permute-start.7 = (bf16[24,4096]{1,0:T(8,128)(2,1)S(1)}, bf16[24,4096]{1,0:T(8,128)(2,1)S(1)}, u32[]{:S(2)}, u32[]{:S(2)}) collective-permute-start(bf16[24,4096]{1,0:T(8,128)(2,1)S(1)} %apply_layer.17.refs_4_), channel_id=1, source_target_pairs={{0,5},{1,4},{2,7},{3,6},{4,9},{5,8},{6,11},{7,10},{8,13},{9,12},{1... | collective-permute-start | bytes 589832 | tf_op jit(solution)/shard_map/ppermute | solution.py:107
  31.0 16.3 %collective-permute-start.8 = (bf16[24,4096]{1,0:T(8,128)(2,1)S(1)}, bf16[24,4096]{1,0:T(8,128)(2,1)S(1)}, u32[]{:S(2)}, u32[]{:S(2)}) collective-permute-start(bf16[24,4096]{1,0:T(8,128)(2,1)S(1)} %apply_layer.17.refs_4_), channel_id=1, source_target_pairs={{0,4},{1,5},{2,6},{3,7},{4,8},{5,9},{6,10},{7,11},{8,12},{9,13},{1... | collective-permute-start | bytes 589832 | tf_op jit(solution)/shard_map/ppermute | solution.py:107
  39.1 14.6 %collective-permute-start.10 = (bf16[32,4096]{1,0:T(8,128)(2,1)S(1)}, bf16[32,4096]{1,0:T(8,128)(2,1)S(1)}, u32[]{:S(2)}, u32[]{:S(2)}) collective-permute-start(bf16[32,4096]{1,0:T(8,128)(2,1)S(1)} %apply_layer.18.refs_4_), channel_id=1, source_target_pairs={{0,5},{1,4},{2,7},{3,6},{4,9},{5,8},{6,11},{7,10},{8,13},{9,12},{1... | collective-permute-start | bytes 786440 | tf_op jit(solution)/shard_map/ppermute | solution.py:107
  41.1 16.5 %collective-permute-start.11 = (bf16[32,4096]{1,0:T(8,128)(2,1)S(1)}, bf16[32,4096]{1,0:T(8,128)(2,1)S(1)}, u32[]{:S(2)}, u32[]{:S(2)}) collective-permute-start(bf16[32,4096]{1,0:T(8,128)(2,1)S(1)} %apply_layer.18.refs_4_), channel_id=1, source_target_pairs={{1,6},{2,5},{5,10},{6,9},{9,14},{10,13},{13,18},{14,17},{17,22},{1... | collective-permute-start | bytes 786440 | tf_op jit(solution)/shard_map/ppermute | solution.py:107
  49.0 17.0 %collective-permute-start.13 = (bf16[24,4096]{1,0:T(8,128)(2,1)S(1)}, bf16[24,4096]{1,0:T(8,128)(2,1)S(1)}, u32[]{:S(2)}, u32[]{:S(2)}) collective-permute-start(bf16[24,4096]{1,0:T(8,128)(2,1)S(1)} %apply_layer.19.refs_4_), channel_id=1, source_target_pairs={{0,5},{1,4},{2,7},{3,6},{4,9},{5,8},{6,11},{7,10},{8,13},{9,12},{1... | collective-permute-start | bytes 589832 | tf_op jit(solution)/shard_map/ppermute | solution.py:107
  50.9 18.1 %collective-permute-start.14 = (bf16[24,4096]{1,0:T(8,128)(2,1)S(1)}, bf16[24,4096]{1,0:T(8,128)(2,1)S(1)}, u32[]{:S(2)}, u32[]{:S(2)}) collective-permute-start(bf16[24,4096]{1,0:T(8,128)(2,1)S(1)} %apply_layer.19.refs_4_), channel_id=1, source_target_pairs={{0,4},{1,5},{2,6},{3,7},{4,8},{5,9},{6,10},{7,11},{8,12},{9,13},{1... | collective-permute-start | bytes 589832 | tf_op jit(solution)/shard_map/ppermute | solution.py:107
  53.7 15.3 %collective-permute-start.15 = (bf16[24,4096]{1,0:T(8,128)(2,1)S(1)}, bf16[24,4096]{1,0:T(8,128)(2,1)S(1)}, u32[]{:S(2)}, u32[]{:S(2)}) collective-permute-start(bf16[24,4096]{1,0:T(8,128)(2,1)S(1)} %apply_layer.19.refs_4_), channel_id=1, source_target_pairs={{1,6},{2,5},{5,10},{6,9},{9,14},{10,13},{13,18},{14,17},{17,22},{1... | collective-permute-start | bytes 589832 | tf_op jit(solution)/shard_map/ppermute | solution.py:107
  59.4 15.1 %collective-permute-start.16 = (bf16[32,4096]{1,0:T(8,128)(2,1)S(1)}, bf16[32,4096]{1,0:T(8,128)(2,1)S(1)}, u32[]{:S(2)}, u32[]{:S(2)}) collective-permute-start(bf16[32,4096]{1,0:T(8,128)(2,1)S(1)} %apply_layer.20.refs_4_), channel_id=1, source_target_pairs={{0,5},{1,4},{2,7},{3,6},{4,9},{5,8},{6,11},{7,10},{8,13},{9,12},{1... | collective-permute-start | bytes 786440 | tf_op jit(solution)/shard_map/ppermute | solution.py:107
  61.9 15.3 %collective-permute-start.17 = (bf16[32,4096]{1,0:T(8,128)(2,1)S(1)}, bf16[32,4096]{1,0:T(8,128)(2,1)S(1)}, u32[]{:S(2)}, u32[]{:S(2)}) collective-permute-start(bf16[32,4096]{1,0:T(8,128)(2,1)S(1)} %apply_layer.20.refs_4_), channel_id=1, source_target_pairs={{1,6},{2,5},{5,10},{6,9},{9,14},{10,13},{13,18},{14,17},{17,22},{1... | collective-permute-start | bytes 786440 | tf_op jit(solution)/shard_map/ppermute | solution.py:107
  72.6 14.9 %collective-permute-start.20 = (bf16[24,4096]{1,0:T(8,128)(2,1)S(1)}, bf16[24,4096]{1,0:T(8,128)(2,1)S(1)}, u32[]{:S(2)}, u32[]{:S(2)}) collective-permute-start(bf16[24,4096]{1,0:T(8,128)(2,1)S(1)} %apply_layer.21.refs_4_), channel_id=1, source_target_pairs={{0,4},{1,5},{2,6},{3,7},{4,8},{5,9},{6,10},{7,11},{8,12},{9,13},{1... | collective-permute-start | bytes 589832 | tf_op jit(solution)/shard_map/ppermute | solution.py:107
  78.8 14.4 %collective-permute-start.22 = (bf16[32,4096]{1,0:T(8,128)(2,1)S(1)}, bf16[32,4096]{1,0:T(8,128)(2,1)S(1)}, u32[]{:S(2)}, u32[]{:S(2)}) collective-permute-start(bf16[32,4096]{1,0:T(8,128)(2,1)S(1)} %apply_layer.22.refs_4_), channel_id=1, source_target_pairs={{0,5},{1,4},{2,7},{3,6},{4,9},{5,8},{6,11},{7,10},{8,13},{9,12},{1... | collective-permute-start | bytes 786440 | tf_op jit(solution)/shard_map/ppermute | solution.py:107
  80.8 17.8 %collective-permute-start.23 = (bf16[32,4096]{1,0:T(8,128)(2,1)S(1)}, bf16[32,4096]{1,0:T(8,128)(2,1)S(1)}, u32[]{:S(2)}, u32[]{:S(2)}) collective-permute-start(bf16[32,4096]{1,0:T(8,128)(2,1)S(1)} %apply_layer.22.refs_4_), channel_id=1, source_target_pairs={{1,6},{2,5},{5,10},{6,9},{9,14},{10,13},{13,18},{14,17},{17,22},{1... | collective-permute-start | bytes 786440 | tf_op jit(solution)/shard_map/ppermute | solution.py:107
  89.1 17.8 %collective-permute-start.25 = (bf16[24,4096]{1,0:T(8,128)(2,1)S(1)}, bf16[24,4096]{1,0:T(8,128)(2,1)S(1)}, u32[]{:S(2)}, u32[]{:S(2)}) collective-permute-start(bf16[24,4096]{1,0:T(8,128)(2,1)S(1)} %apply_layer.23.refs_4_), channel_id=1, source_target_pairs={{0,5},{1,4},{2,7},{3,6},{4,9},{5,8},{6,11},{7,10},{8,13},{9,12},{1... | collective-permute-start | bytes 589832 | tf_op jit(solution)/shard_map/ppermute | solution.py:107
  91.1 17.9 %collective-permute-start.26 = (bf16[24,4096]{1,0:T(8,128)(2,1)S(1)}, bf16[24,4096]{1,0:T(8,128)(2,1)S(1)}, u32[]{:S(2)}, u32[]{:S(2)}) collective-permute-start(bf16[24,4096]{1,0:T(8,128)(2,1)S(1)} %apply_layer.23.refs_4_), channel_id=1, source_target_pairs={{0,4},{1,5},{2,6},{3,7},{4,8},{5,9},{6,10},{7,11},{8,12},{9,13},{1... | collective-permute-start | bytes 589832 | tf_op jit(solution)/shard_map/ppermute | solution.py:107
  93.3 15.6 %collective-permute-start.27 = (bf16[24,4096]{1,0:T(8,128)(2,1)S(1)}, bf16[24,4096]{1,0:T(8,128)(2,1)S(1)}, u32[]{:S(2)}, u32[]{:S(2)}) collective-permute-start(bf16[24,4096]{1,0:T(8,128)(2,1)S(1)} %apply_layer.23.refs_4_), channel_id=1, source_target_pairs={{1,6},{2,5},{5,10},{6,9},{9,14},{10,13},{13,18},{14,17},{17,22},{1... | collective-permute-start | bytes 589832 | tf_op jit(solution)/shard_map/ppermute | solution.py:107
  100.3 14.1 %collective-permute-start.28 = (bf16[32,4096]{1,0:T(8,128)(2,1)S(1)}, bf16[32,4096]{1,0:T(8,128)(2,1)S(1)}, u32[]{:S(2)}, u32[]{:S(2)}) collective-permute-start(bf16[32,4096]{1,0:T(8,128)(2,1)S(1)} %apply_layer.24.refs_4_), channel_id=1, source_target_pairs={{0,5},{1,4},{2,7},{3,6},{4,9},{5,8},{6,11},{7,10},{8,13},{9,12},{1... | collective-permute-start | bytes 786440 | tf_op jit(solution)/shard_map/ppermute | solution.py:107
  102.9 14.9 %collective-permute-start.29 = (bf16[32,4096]{1,0:T(8,128)(2,1)S(1)}, bf16[32,4096]{1,0:T(8,128)(2,1)S(1)}, u32[]{:S(2)}, u32[]{:S(2)}) collective-permute-start(bf16[32,4096]{1,0:T(8,128)(2,1)S(1)} %apply_layer.24.refs_4_), channel_id=1, source_target_pairs={{1,6},{2,5},{5,10},{6,9},{9,14},{10,13},{13,18},{14,17},{17,22},{1... | collective-permute-start | bytes 786440 | tf_op jit(solution)/shard_map/ppermute | solution.py:107
  110.6 14.8 %collective-permute-start.31 = (bf16[24,4096]{1,0:T(8,128)(2,1)S(1)}, bf16[24,4096]{1,0:T(8,128)(2,1)S(1)}, u32[]{:S(2)}, u32[]{:S(2)}) collective-permute-start(bf16[24,4096]{1,0:T(8,128)(2,1)S(1)} %apply_layer.25.refs_4_), channel_id=1, source_target_pairs={{0,5},{1,4},{2,7},{3,6},{4,9},{5,8},{6,11},{7,10},{8,13},{9,12},{1... | collective-permute-start | bytes 589832 | tf_op jit(solution)/shard_map/ppermute | solution.py:107
  112.5 15.6 %collective-permute-start.32 = (bf16[24,4096]{1,0:T(8,128)(2,1)S(1)}, bf16[24,4096]{1,0:T(8,128)(2,1)S(1)}, u32[]{:S(2)}, u32[]{:S(2)}) collective-permute-start(bf16[24,4096]{1,0:T(8,128)(2,1)S(1)} %apply_layer.25.refs_4_), channel_id=1, source_target_pairs={{0,4},{1,5},{2,6},{3,7},{4,8},{5,9},{6,10},{7,11},{8,12},{9,13},{1... | collective-permute-start | bytes 589832 | tf_op jit(solution)/shard_map/ppermute | solution.py:107
  119.5 14.2 %collective-permute-start.34 = (bf16[32,4096]{1,0:T(8,128)(2,1)S(1)}, bf16[32,4096]{1,0:T(8,128)(2,1)S(1)}, u32[]{:S(2)}, u32[]{:S(2)}) collective-permute-start(bf16[32,4096]{1,0:T(8,128)(2,1)S(1)} %apply_layer.26.refs_4_), channel_id=1, source_target_pairs={{0,5},{1,4},{2,7},{3,6},{4,9},{5,8},{6,11},{7,10},{8,13},{9,12},{1... | collective-permute-start | bytes 786440 | tf_op jit(solution)/shard_map/ppermute | solution.py:107
  121.4 17.7 %collective-permute-start.35 = (bf16[32,4096]{1,0:T(8,128)(2,1)S(1)}, bf16[32,4096]{1,0:T(8,128)(2,1)S(1)}, u32[]{:S(2)}, u32[]{:S(2)}) collective-permute-start(bf16[32,4096]{1,0:T(8,128)(2,1)S(1)} %apply_layer.26.refs_4_), channel_id=1, source_target_pairs={{1,6},{2,5},{5,10},{6,9},{9,14},{10,13},{13,18},{14,17},{17,22},{1... | collective-permute-start | bytes 786440 | tf_op jit(solution)/shard_map/ppermute | solution.py:107
  129.8 17.7 %collective-permute-start.37 = (bf16[24,4096]{1,0:T(8,128)(2,1)S(1)}, bf16[24,4096]{1,0:T(8,128)(2,1)S(1)}, u32[]{:S(2)}, u32[]{:S(2)}) collective-permute-start(bf16[24,4096]{1,0:T(8,128)(2,1)S(1)} %apply_layer.27.refs_4_), channel_id=1, source_target_pairs={{0,5},{1,4},{2,7},{3,6},{4,9},{5,8},{6,11},{7,10},{8,13},{9,12},{1... | collective-permute-start | bytes 589832 | tf_op jit(solution)/shard_map/ppermute | solution.py:107
  131.8 17.7 %collective-permute-start.38 = (bf16[24,4096]{1,0:T(8,128)(2,1)S(1)}, bf16[24,4096]{1,0:T(8,128)(2,1)S(1)}, u32[]{:S(2)}, u32[]{:S(2)}) collective-permute-start(bf16[24,4096]{1,0:T(8,128)(2,1)S(1)} %apply_layer.27.refs_4_), channel_id=1, source_target_pairs={{0,4},{1,5},{2,6},{3,7},{4,8},{5,9},{6,10},{7,11},{8,12},{9,13},{1... | collective-permute-start | bytes 589832 | tf_op jit(solution)/shard_map/ppermute | solution.py:107
  133.7 15.8 %collective-permute-start.39 = (bf16[24,4096]{1,0:T(8,128)(2,1)S(1)}, bf16[24,4096]{1,0:T(8,128)(2,1)S(1)}, u32[]{:S(2)}, u32[]{:S(2)}) collective-permute-start(bf16[24,4096]{1,0:T(8,128)(2,1)S(1)} %apply_layer.27.refs_4_), channel_id=1, source_target_pairs={{1,6},{2,5},{5,10},{6,9},{9,14},{10,13},{13,18},{14,17},{17,22},{1... | collective-permute-start | bytes 589832 | tf_op jit(solution)/shard_map/ppermute | solution.py:107
  140.9 14.1 %collective-permute-start.40 = (bf16[32,4096]{1,0:T(8,128)(2,1)S(1)}, bf16[32,4096]{1,0:T(8,128)(2,1)S(1)}, u32[]{:S(2)}, u32[]{:S(2)}) collective-permute-start(bf16[32,4096]{1,0:T(8,128)(2,1)S(1)} %apply_layer.28.refs_4_), channel_id=1, source_target_pairs={{0,5},{1,4},{2,7},{3,6},{4,9},{5,8},{6,11},{7,10},{8,13},{9,12},{1... | collective-permute-start | bytes 786440 | tf_op jit(solution)/shard_map/ppermute | solution.py:107
  143.5 14.1 %collective-permute-start.41 = (bf16[32,4096]{1,0:T(8,128)(2,1)S(1)}, bf16[32,4096]{1,0:T(8,128)(2,1)S(1)}, u32[]{:S(2)}, u32[]{:S(2)}) collective-permute-start(bf16[32,4096]{1,0:T(8,128)(2,1)S(1)} %apply_layer.28.refs_4_), channel_id=1, source_target_pairs={{1,6},{2,5},{5,10},{6,9},{9,14},{10,13},{13,18},{14,17},{17,22},{1... | collective-permute-start | bytes 786440 | tf_op jit(solution)/shard_map/ppermute | solution.py:107
  (16 other events, 172.8 us)

commit v4 on v3

--- a/solution.py
+++ b/solution.py
@@ -11,41 +11,46 @@
 
 
 def convert_kernel(prop_ref, weights_ref, blocks, arrived):
-    row_blocks = weights_ref.shape[0]
-    flight, slots, blk, _ = blocks.shape
+    row_blocks, _, blk = weights_ref.shape
+    flight, slots, rows, _ = blocks.shape
+    group = rows // blk
+    steps = row_blocks // group
 
-    def fetch(r, slot):
-        rows = pl.ds(pl.multiple_of(r * blk, blk), blk)
-        return pltpu.make_async_copy(prop_ref.at[:, rows, :], blocks.at[slot], arrived.at[slot])
+    def fetch(i, slot):
+        here = pl.ds(pl.multiple_of(i * rows, rows), rows)
+        return pltpu.make_async_copy(prop_ref.at[:, here, :], blocks.at[slot], arrived.at[slot])
 
-    for r in range(flight):
-        fetch(r, r).start()
+    for i in range(flight):
+        fetch(i, i).start()
 
-    def step(r, carry):
-        slot = lax.rem(r, flight)
-        fetch(r, slot).wait()
-        for k in range(slots):
-            weights_ref[r, k * blk:(k + 1) * blk, :] = blocks[slot, k].astype(jnp.bfloat16).T
+    def step(i, carry):
+        slot = lax.rem(i, flight)
+        fetch(i, slot).wait()
+        for g in range(group):
+            for k in range(slots):
+                block = blocks[slot, k, g * blk:(g + 1) * blk, :].astype(jnp.bfloat16)
+                weights_ref[i * group + g, k * blk:(k + 1) * blk, :] = block.T
 
-        @pl.when(r + flight < row_blocks)
+        @pl.when(i + flight < steps)
         def _():
-            fetch(r + flight, slot).start()
+            fetch(i + flight, slot).start()
 
         return carry
 
-    lax.fori_loop(0, row_blocks, step, 0)
+    lax.fori_loop(0, steps, step, 0)
 
 
 def convert_weights(prop):
     slots, rows, blk = prop.shape
-    flight = min(8, rows // blk)
+    group = 1 if rows // blk % 2 else 2
+    flight = min(6, rows // blk // group)
     return pl.pallas_call(
         convert_kernel,
         in_specs=[pl.BlockSpec(memory_space=pltpu.HBM)],
         out_specs=pl.BlockSpec(memory_space=pltpu.VMEM),
         out_shape=jax.ShapeDtypeStruct((rows // blk, slots * blk, blk), jnp.bfloat16),
         scratch_shapes=[
-            pltpu.VMEM((flight, slots, blk, blk), jnp.float32),
+            pltpu.VMEM((flight, slots, group * blk, blk), jnp.float32),
             pltpu.SemaphoreType.DMA((flight,)),
         ],
         compiler_params=pltpu.CompilerParams(vmem_limit_bytes=44 * MIB),
@@ -54,18 +59,18 @@
     )(prop)
 
 
-def tick_kernel(tick, first, places, cols_ref, weights_ref, *refs):
-    thirds, (source_ref, _, out_ref, window) = refs[:len(places)], refs[len(places):]
+def tick_kernel(tick, first, cols_ref, weights_ref, *refs):
+    thirds, (source_ref, _, out_ref, window) = refs[:3], refs[3:]
     shots, width = out_ref.shape
     row_blocks, depth, blk = weights_ref.shape
     slots = depth // blk
-    for place, third_ref in zip(places, thirds):
+    for place, third_ref in enumerate(thirds):
         window[:, place * width:(place + 1) * width] = third_ref[...]
 
     def step(r, carry):
         picked = []
         for k in range(slots):
-            start = pl.multiple_of(cols_ref[r * slots + k] * blk, blk)
+            start = pl.multiple_of(cols_ref[k, r] * blk, blk)
             picked.append(window[:, pl.ds(start, blk)])
         mixed = jnp.dot(jnp.concatenate(picked, axis=1), weights_ref[r], preferred_element_type=jnp.float32)
         here = pl.ds(pl.multiple_of(r * blk, blk), blk)
@@ -75,11 +80,11 @@
     lax.fori_loop(0, row_blocks, step, 0, unroll=True)
 
 
-def apply_layer(tick, first, places, cols, weights, thirds, sources, before):
+def apply_layer(tick, first, cols, weights, thirds, sources, before):
     shots, width = thirds[0].shape
     vmem = pl.BlockSpec(memory_space=pltpu.VMEM)
     return pl.pallas_call(
-        functools.partial(tick_kernel, tick, first, places),
+        functools.partial(tick_kernel, tick, first),
         in_specs=[pl.BlockSpec(memory_space=pltpu.SMEM)] + [vmem] * 5 + [pl.BlockSpec(memory_space=pl.ANY)],
         out_specs=vmem,
         out_shape=jax.ShapeDtypeStruct((shots, width), jnp.bfloat16),
@@ -116,12 +121,12 @@
     far = [partner(r, rows, True) for r in range(rows)]
     block_count = row_count // blk
     place = lax.axis_index("row")
-    side = lax.div(col_blocks[0], block_count) - place
+    absolute = jnp.transpose(col_blocks[0])
+    side = lax.div(absolute, block_count) - place
     third = 1 + side * (2 * lax.rem(place, 2) - 1)
-    cols = (third * block_count + lax.rem(col_blocks[0], block_count)).reshape(-1)
+    cols = third * block_count + lax.rem(absolute, block_count)
     cut = (shots // 16 + 1) // 2 * 16
     panels = [(0, cut), (cut, shots)]
-    orders = [(0, 2, 1), (0, 1, 2)]
     arriving = []
     for a, b in panels:
         own = incoming[0, a:b]
@@ -133,8 +138,7 @@
     for tick in range(ticks):
         produced = []
         for i in range(len(panels)):
-            thirds = [arriving[i][place] for place in orders[i]]
-            done = apply_layer(tick, panels[i][0], orders[i], cols, weights, thirds, sources, before)
+            done = apply_layer(tick, panels[i][0], cols, weights, arriving[i], sources, before)
             before = done
             produced.append(done)
             if tick + 1 < ticks:

time: 172 us -> 167 us (0.971)
  starting transfers between devices: 123 us -> 119 us
    ppermute x46, starting transfers between devices: 123 us -> 119 us  [send(): return lax.ppermute(value, ('layer', 'row'), pairs)]
  transfers between devices with their start and end apart: 46 -> 46, of which waited for: 5 -> 14; matrix products, arithmetic and copies ran while one was open for 1% -> 1% of each run, Pallas kernels for 18% -> 19%
where the time goes in v4:
time: 167 us; the launch traced here: 166 us
  starting transfers between devices  119 us (71%)
  Pallas kernels  32.5 us (19%)
  waiting for transfers between devices  8.56 us (5%)
  local copies, waits for them, and re-layouts  3.98 us (2%)
    ppermute x46, starting transfers between devices, send(): return lax.ppermute(value, ('layer', 'row'), pairs)  119 us
    pallas_call x16, Pallas kernels, apply_layer(): pl.pallas_call(functools.partial(tick_kernel, tick, first), in_specs=[pl....  27.2 us
    ppermute x46, waiting for transfers between devices, send(): return lax.ppermute(value, ('layer', 'row'), pairs)  8.56 us
    pallas_call x1, Pallas kernels, convert_weights(): pl.pallas_call(convert_kernel, in_specs=[pl.BlockSpec(memory_space=pltpu....  5.27 us
  transfers between devices with their start and end apart: 46, of which 14 were waited for; matrix products, arithmetic and copies ran while one was open for 1% of the time, Pallas kernels for 19%

profile of v4, /device:TPU:11, one launch (start us, length us, event | category | flops | bytes accessed | tf_op | source)
XLA Modules:
  0.0 165.7 jit_solution(637041503354574778)
XLA Ops:
  1.3 4.1 %collective-permute-start.1 = (bf16[32,4096]{1,0:T(8,128)(2,1)S(1)}, bf16[32,4096]{1,0:T(8,128)(2,1)S(1)}, u32[]{:S(2)}, u32[]{:S(2)}) collective-permute-start(bf16[32,4096]{1,0:T(8,128)(2,1)S(1)} %slice_bitcast_fusion.refs_1_), channel_id=1, source_target_pairs={{1,2},{2,1},{5,6},{6,5},{9,10},{10,9},{13,14},{14,13},{17,18},{18,... | collective-permute-start | bytes 786440 | tf_op jit(solution)/shard_map/ppermute | solution.py:112
  6.4 2.1 %collective-permute-start.3 = (bf16[24,4096]{1,0:T(8,128)(2,1)S(1)}, bf16[24,4096]{1,0:T(8,128)(2,1)S(1)}, u32[]{:S(2)}, u32[]{:S(2)}) collective-permute-start(bf16[24,4096]{1,0:T(8,128)(2,1)S(1)} %slice_bitcast_fusion.1.refs_1_), channel_id=1, source_target_pairs={{1,2},{2,1},{5,6},{6,5},{9,10},{10,9},{13,14},{14,13},{17,18},{18,... | collective-permute-start | bytes 589832 | tf_op jit(solution)/shard_map/ppermute | solution.py:112
  9.2 5.3 %convert_weights.1.weights_ref.refs_4_ = bf16[32,768,128]{2,1,0:T(8,128)(2,1)S(1)} custom-call(f32[6,4096,128]{2,1,0:T(8,128)} %bitcast.49), custom_call_target="tpu_custom_call" | custom-call | bytes 12582912 | tf_op jit(solution)/shard_map/convert_weights/pallas_call | solution.py:47
  16.8 4.3 %collective-permute-start.4 = (bf16[32,4096]{1,0:T(8,128)(2,1)S(1)}, bf16[32,4096]{1,0:T(8,128)(2,1)S(1)}, u32[]{:S(2)}, u32[]{:S(2)}) collective-permute-start(bf16[32,4096]{1,0:T(8,128)(2,1)S(1)} %apply_layer.16.refs_4_), channel_id=1, source_target_pairs={{0,5},{1,4},{2,7},{3,6},{4,9},{5,8},{6,11},{7,10},{8,13},{9,12},{1... | collective-permute-start | bytes 786440 | tf_op jit(solution)/shard_map/ppermute | solution.py:112
  21.1 3.1 %collective-permute-start.5 = (bf16[32,4096]{1,0:T(8,128)(2,1)S(1)}, bf16[32,4096]{1,0:T(8,128)(2,1)S(1)}, u32[]{:S(2)}, u32[]{:S(2)}) collective-permute-start(bf16[32,4096]{1,0:T(8,128)(2,1)S(1)} %apply_layer.16.refs_4_), channel_id=1, source_target_pairs={{0,4},{1,5},{2,6},{3,7},{4,8},{5,9},{6,10},{7,11},{8,12},{9,13},{1... | collective-permute-start | bytes 786440 | tf_op jit(solution)/shard_map/ppermute | solution.py:112
  24.2 2.9 %collective-permute-start.6 = (bf16[32,4096]{1,0:T(8,128)(2,1)S(1)}, bf16[32,4096]{1,0:T(8,128)(2,1)S(1)}, u32[]{:S(2)}, u32[]{:S(2)}) collective-permute-start(bf16[32,4096]{1,0:T(8,128)(2,1)S(1)} %apply_layer.16.refs_4_), channel_id=1, source_target_pairs={{1,6},{2,5},{5,10},{6,9},{9,14},{10,13},{13,18},{14,17},{17,22},{1... | collective-permute-start | bytes 786440 | tf_op jit(solution)/shard_map/ppermute | solution.py:112
  28.8 2.3 %collective-permute-start.7 = (bf16[24,4096]{1,0:T(8,128)(2,1)S(1)}, bf16[24,4096]{1,0:T(8,128)(2,1)S(1)}, u32[]{:S(2)}, u32[]{:S(2)}) collective-permute-start(bf16[24,4096]{1,0:T(8,128)(2,1)S(1)} %apply_layer.17.refs_4_), channel_id=1, source_target_pairs={{0,5},{1,4},{2,7},{3,6},{4,9},{5,8},{6,11},{7,10},{8,13},{9,12},{1... | collective-permute-start | bytes 589832 | tf_op jit(solution)/shard_map/ppermute | solution.py:112
  31.1 3.4 %collective-permute-start.8 = (bf16[24,4096]{1,0:T(8,128)(2,1)S(1)}, bf16[24,4096]{1,0:T(8,128)(2,1)S(1)}, u32[]{:S(2)}, u32[]{:S(2)}) collective-permute-start(bf16[24,4096]{1,0:T(8,128)(2,1)S(1)} %apply_layer.17.refs_4_), channel_id=1, source_target_pairs={{0,4},{1,5},{2,6},{3,7},{4,8},{5,9},{6,10},{7,11},{8,12},{9,13},{1... | collective-permute-start | bytes 589832 | tf_op jit(solution)/shard_map/ppermute | solution.py:112
  34.5 2.8 %collective-permute-start.9 = (bf16[24,4096]{1,0:T(8,128)(2,1)S(1)}, bf16[24,4096]{1,0:T(8,128)(2,1)S(1)}, u32[]{:S(2)}, u32[]{:S(2)}) collective-permute-start(bf16[24,4096]{1,0:T(8,128)(2,1)S(1)} %apply_layer.17.refs_4_), channel_id=1, source_target_pairs={{1,6},{2,5},{5,10},{6,9},{9,14},{10,13},{13,18},{14,17},{17,22},{1... | collective-permute-start | bytes 589832 | tf_op jit(solution)/shard_map/ppermute | solution.py:112
  39.1 2.1 %collective-permute-start.10 = (bf16[32,4096]{1,0:T(8,128)(2,1)S(1)}, bf16[32,4096]{1,0:T(8,128)(2,1)S(1)}, u32[]{:S(2)}, u32[]{:S(2)}) collective-permute-start(bf16[32,4096]{1,0:T(8,128)(2,1)S(1)} %apply_layer.18.refs_4_), channel_id=1, source_target_pairs={{0,5},{1,4},{2,7},{3,6},{4,9},{5,8},{6,11},{7,10},{8,13},{9,12},{1... | collective-permute-start | bytes 786440 | tf_op jit(solution)/shard_map/ppermute | solution.py:112
  41.2 2.1 %collective-permute-start.11 = (bf16[32,4096]{1,0:T(8,128)(2,1)S(1)}, bf16[32,4096]{1,0:T(8,128)(2,1)S(1)}, u32[]{:S(2)}, u32[]{:S(2)}) collective-permute-start(bf16[32,4096]{1,0:T(8,128)(2,1)S(1)} %apply_layer.18.refs_4_), channel_id=1, source_target_pairs={{0,4},{1,5},{2,6},{3,7},{4,8},{5,9},{6,10},{7,11},{8,12},{9,13},{1... | collective-permute-start | bytes 786440 | tf_op jit(solution)/shard_map/ppermute | solution.py:112
  43.3 4.1 %collective-permute-start.12 = (bf16[32,4096]{1,0:T(8,128)(2,1)S(1)}, bf16[32,4096]{1,0:T(8,128)(2,1)S(1)}, u32[]{:S(2)}, u32[]{:S(2)}) collective-permute-start(bf16[32,4096]{1,0:T(8,128)(2,1)S(1)} %apply_layer.18.refs_4_), channel_id=1, source_target_pairs={{1,6},{2,5},{5,10},{6,9},{9,14},{10,13},{13,18},{14,17},{17,22},{1... | collective-permute-start | bytes 786440 | tf_op jit(solution)/shard_map/ppermute | solution.py:112
  51.0 2.8 %collective-permute-start.14 = (bf16[24,4096]{1,0:T(8,128)(2,1)S(1)}, bf16[24,4096]{1,0:T(8,128)(2,1)S(1)}, u32[]{:S(2)}, u32[]{:S(2)}) collective-permute-start(bf16[24,4096]{1,0:T(8,128)(2,1)S(1)} %apply_layer.19.refs_4_), channel_id=1, source_target_pairs={{0,4},{1,5},{2,6},{3,7},{4,8},{5,9},{6,10},{7,11},{8,12},{9,13},{1... | collective-permute-start | bytes 589832 | tf_op jit(solution)/shard_map/ppermute | solution.py:112
  53.8 3.1 %collective-permute-start.15 = (bf16[24,4096]{1,0:T(8,128)(2,1)S(1)}, bf16[24,4096]{1,0:T(8,128)(2,1)S(1)}, u32[]{:S(2)}, u32[]{:S(2)}) collective-permute-start(bf16[24,4096]{1,0:T(8,128)(2,1)S(1)} %apply_layer.19.refs_4_), channel_id=1, source_target_pairs={{1,6},{2,5},{5,10},{6,9},{9,14},{10,13},{13,18},{14,17},{17,22},{1... | collective-permute-start | bytes 589832 | tf_op jit(solution)/shard_map/ppermute | solution.py:112
  61.0 2.0 %collective-permute-start.17 = (bf16[32,4096]{1,0:T(8,128)(2,1)S(1)}, bf16[32,4096]{1,0:T(8,128)(2,1)S(1)}, u32[]{:S(2)}, u32[]{:S(2)}) collective-permute-start(bf16[32,4096]{1,0:T(8,128)(2,1)S(1)} %apply_layer.20.refs_4_), channel_id=1, source_target_pairs={{0,4},{1,5},{2,6},{3,7},{4,8},{5,9},{6,10},{7,11},{8,12},{9,13},{1... | collective-permute-start | bytes 786440 | tf_op jit(solution)/shard_map/ppermute | solution.py:112
  63.0 3.6 %collective-permute-start.18 = (bf16[32,4096]{1,0:T(8,128)(2,1)S(1)}, bf16[32,4096]{1,0:T(8,128)(2,1)S(1)}, u32[]{:S(2)}, u32[]{:S(2)}) collective-permute-start(bf16[32,4096]{1,0:T(8,128)(2,1)S(1)} %apply_layer.20.refs_4_), channel_id=1, source_target_pairs={{1,6},{2,5},{5,10},{6,9},{9,14},{10,13},{13,18},{14,17},{17,22},{1... | collective-permute-start | bytes 786440 | tf_op jit(solution)/shard_map/ppermute | solution.py:112
  70.4 3.2 %collective-permute-start.20 = (bf16[24,4096]{1,0:T(8,128)(2,1)S(1)}, bf16[24,4096]{1,0:T(8,128)(2,1)S(1)}, u32[]{:S(2)}, u32[]{:S(2)}) collective-permute-start(bf16[24,4096]{1,0:T(8,128)(2,1)S(1)} %apply_layer.21.refs_4_), channel_id=1, source_target_pairs={{0,4},{1,5},{2,6},{3,7},{4,8},{5,9},{6,10},{7,11},{8,12},{9,13},{1... | collective-permute-start | bytes 589832 | tf_op jit(solution)/shard_map/ppermute | solution.py:112
  73.5 3.1 %collective-permute-start.21 = (bf16[24,4096]{1,0:T(8,128)(2,1)S(1)}, bf16[24,4096]{1,0:T(8,128)(2,1)S(1)}, u32[]{:S(2)}, u32[]{:S(2)}) collective-permute-start(bf16[24,4096]{1,0:T(8,128)(2,1)S(1)} %apply_layer.21.refs_4_), channel_id=1, source_target_pairs={{1,6},{2,5},{5,10},{6,9},{9,14},{10,13},{13,18},{14,17},{17,22},{1... | collective-permute-start | bytes 589832 | tf_op jit(solution)/shard_map/ppermute | solution.py:112
  82.8 3.5 %collective-permute-start.24 = (bf16[32,4096]{1,0:T(8,128)(2,1)S(1)}, bf16[32,4096]{1,0:T(8,128)(2,1)S(1)}, u32[]{:S(2)}, u32[]{:S(2)}) collective-permute-start(bf16[32,4096]{1,0:T(8,128)(2,1)S(1)} %apply_layer.22.refs_4_), channel_id=1, source_target_pairs={{1,6},{2,5},{5,10},{6,9},{9,14},{10,13},{13,18},{14,17},{17,22},{1... | collective-permute-start | bytes 786440 | tf_op jit(solution)/shard_map/ppermute | solution.py:112
  90.1 3.1 %collective-permute-start.26 = (bf16[24,4096]{1,0:T(8,128)(2,1)S(1)}, bf16[24,4096]{1,0:T(8,128)(2,1)S(1)}, u32[]{:S(2)}, u32[]{:S(2)}) collective-permute-start(bf16[24,4096]{1,0:T(8,128)(2,1)S(1)} %apply_layer.23.refs_4_), channel_id=1, source_target_pairs={{0,4},{1,5},{2,6},{3,7},{4,8},{5,9},{6,10},{7,11},{8,12},{9,13},{1... | collective-permute-start | bytes 589832 | tf_op jit(solution)/shard_map/ppermute | solution.py:112
  93.2 3.3 %collective-permute-start.27 = (bf16[24,4096]{1,0:T(8,128)(2,1)S(1)}, bf16[24,4096]{1,0:T(8,128)(2,1)S(1)}, u32[]{:S(2)}, u32[]{:S(2)}) collective-permute-start(bf16[24,4096]{1,0:T(8,128)(2,1)S(1)} %apply_layer.23.refs_4_), channel_id=1, source_target_pairs={{1,6},{2,5},{5,10},{6,9},{9,14},{10,13},{13,18},{14,17},{17,22},{1... | collective-permute-start | bytes 589832 | tf_op jit(solution)/shard_map/ppermute | solution.py:112
  100.5 2.0 %collective-permute-start.29 = (bf16[32,4096]{1,0:T(8,128)(2,1)S(1)}, bf16[32,4096]{1,0:T(8,128)(2,1)S(1)}, u32[]{:S(2)}, u32[]{:S(2)}) collective-permute-start(bf16[32,4096]{1,0:T(8,128)(2,1)S(1)} %apply_layer.24.refs_4_), channel_id=1, source_target_pairs={{0,4},{1,5},{2,6},{3,7},{4,8},{5,9},{6,10},{7,11},{8,12},{9,13},{1... | collective-permute-start | bytes 786440 | tf_op jit(solution)/shard_map/ppermute | solution.py:112
  102.5 3.4 %collective-permute-start.30 = (bf16[32,4096]{1,0:T(8,128)(2,1)S(1)}, bf16[32,4096]{1,0:T(8,128)(2,1)S(1)}, u32[]{:S(2)}, u32[]{:S(2)}) collective-permute-start(bf16[32,4096]{1,0:T(8,128)(2,1)S(1)} %apply_layer.24.refs_4_), channel_id=1, source_target_pairs={{1,6},{2,5},{5,10},{6,9},{9,14},{10,13},{13,18},{14,17},{17,22},{1... | collective-permute-start | bytes 786440 | tf_op jit(solution)/shard_map/ppermute | solution.py:112
  109.9 2.9 %collective-permute-start.32 = (bf16[24,4096]{1,0:T(8,128)(2,1)S(1)}, bf16[24,4096]{1,0:T(8,128)(2,1)S(1)}, u32[]{:S(2)}, u32[]{:S(2)}) collective-permute-start(bf16[24,4096]{1,0:T(8,128)(2,1)S(1)} %apply_layer.25.refs_4_), channel_id=1, source_target_pairs={{0,4},{1,5},{2,6},{3,7},{4,8},{5,9},{6,10},{7,11},{8,12},{9,13},{1... | collective-permute-start | bytes 589832 | tf_op jit(solution)/shard_map/ppermute | solution.py:112
  112.9 3.1 %collective-permute-start.33 = (bf16[24,4096]{1,0:T(8,128)(2,1)S(1)}, bf16[24,4096]{1,0:T(8,128)(2,1)S(1)}, u32[]{:S(2)}, u32[]{:S(2)}) collective-permute-start(bf16[24,4096]{1,0:T(8,128)(2,1)S(1)} %apply_layer.25.refs_4_), channel_id=1, source_target_pairs={{1,6},{2,5},{5,10},{6,9},{9,14},{10,13},{13,18},{14,17},{17,22},{1... | collective-permute-start | bytes 589832 | tf_op jit(solution)/shard_map/ppermute | solution.py:112
  122.1 3.5 %collective-permute-start.36 = (bf16[32,4096]{1,0:T(8,128)(2,1)S(1)}, bf16[32,4096]{1,0:T(8,128)(2,1)S(1)}, u32[]{:S(2)}, u32[]{:S(2)}) collective-permute-start(bf16[32,4096]{1,0:T(8,128)(2,1)S(1)} %apply_layer.26.refs_4_), channel_id=1, source_target_pairs={{1,6},{2,5},{5,10},{6,9},{9,14},{10,13},{13,18},{14,17},{17,22},{1... | collective-permute-start | bytes 786440 | tf_op jit(solution)/shard_map/ppermute | solution.py:112
  129.4 3.1 %collective-permute-start.38 = (bf16[24,4096]{1,0:T(8,128)(2,1)S(1)}, bf16[24,4096]{1,0:T(8,128)(2,1)S(1)}, u32[]{:S(2)}, u32[]{:S(2)}) collective-permute-start(bf16[24,4096]{1,0:T(8,128)(2,1)S(1)} %apply_layer.27.refs_4_), channel_id=1, source_target_pairs={{0,4},{1,5},{2,6},{3,7},{4,8},{5,9},{6,10},{7,11},{8,12},{9,13},{1... | collective-permute-start | bytes 589832 | tf_op jit(solution)/shard_map/ppermute | solution.py:112
  132.5 3.1 %collective-permute-start.39 = (bf16[24,4096]{1,0:T(8,128)(2,1)S(1)}, bf16[24,4096]{1,0:T(8,128)(2,1)S(1)}, u32[]{:S(2)}, u32[]{:S(2)}) collective-permute-start(bf16[24,4096]{1,0:T(8,128)(2,1)S(1)} %apply_layer.27.refs_4_), channel_id=1, source_target_pairs={{1,6},{2,5},{5,10},{6,9},{9,14},{10,13},{13,18},{14,17},{17,22},{1... | collective-permute-start | bytes 589832 | tf_op jit(solution)/shard_map/ppermute | solution.py:112
  141.8 3.5 %collective-permute-start.42 = (bf16[32,4096]{1,0:T(8,128)(2,1)S(1)}, bf16[32,4096]{1,0:T(8,128)(2,1)S(1)}, u32[]{:S(2)}, u32[]{:S(2)}) collective-permute-start(bf16[32,4096]{1,0:T(8,128)(2,1)S(1)} %apply_layer.28.refs_4_), channel_id=1, source_target_pairs={{1,6},{2,5},{5,10},{6,9},{9,14},{10,13},{13,18},{14,17},{17,22},{1... | collective-permute-start | bytes 786440 | tf_op jit(solution)/shard_map/ppermute | solution.py:112
  149.0 3.1 %collective-permute-start.44 = (bf16[24,4096]{1,0:T(8,128)(2,1)S(1)}, bf16[24,4096]{1,0:T(8,128)(2,1)S(1)}, u32[]{:S(2)}, u32[]{:S(2)}) collective-permute-start(bf16[24,4096]{1,0:T(8,128)(2,1)S(1)} %apply_layer.29.refs_4_), channel_id=1, source_target_pairs={{0,4},{1,5},{2,6},{3,7},{4,8},{5,9},{6,10},{7,11},{8,12},{9,13},{1... | collective-permute-start | bytes 589832 | tf_op jit(solution)/shard_map/ppermute | solution.py:112
  152.2 3.1 %collective-permute-start.45 = (bf16[24,4096]{1,0:T(8,128)(2,1)S(1)}, bf16[24,4096]{1,0:T(8,128)(2,1)S(1)}, u32[]{:S(2)}, u32[]{:S(2)}) collective-permute-start(bf16[24,4096]{1,0:T(8,128)(2,1)S(1)} %apply_layer.29.refs_4_), channel_id=1, source_target_pairs={{1,6},{2,5},{5,10},{6,9},{9,14},{10,13},{13,18},{14,17},{17,22},{1... | collective-permute-start | bytes 589832 | tf_op jit(solution)/shard_map/ppermute | solution.py:112
  157.6 4.6 %collective-permute-done.45.refs_2_ = bf16[24,4096]{1,0:T(8,128)(2,1)S(1)} collective-permute-done((bf16[24,4096]{1,0:T(8,128)(2,1)S(1)}, bf16[24,4096]{1,0:T(8,128)(2,1)S(1)}, u32[]{:S(2)}, u32[]{:S(2)}) %collective-permute-start.45) | collective-permute-done | bytes 196640 | tf_op jit(solution)/shard_map/ppermute | solution.py:112
  (92 shorter events, 63.4 us)
Async XLA Ops:
  6.3 20.8 %collective-permute-start.2 = (bf16[24,4096]{1,0:T(8,128)(2,1)S(1)}, bf16[24,4096]{1,0:T(8,128)(2,1)S(1)}, u32[]{:S(2)}, u32[]{:S(2)}) collective-permute-start(bf16[24,4096]{1,0:T(8,128)(2,1)S(1)} %slice_bitcast_fusion.1.refs_1_), channel_id=1, source_target_pairs={{0,1},{1,0},{2,3},{3,2},{4,5},{5,4},{6,7},{7,6},{8,9},{9,8},{10,11... | collective-permute-start | bytes 589832 | tf_op jit(solution)/shard_map/ppermute | solution.py:112
  6.4 20.7 %collective-permute-start.3 = (bf16[24,4096]{1,0:T(8,128)(2,1)S(1)}, bf16[24,4096]{1,0:T(8,128)(2,1)S(1)}, u32[]{:S(2)}, u32[]{:S(2)}) collective-permute-start(bf16[24,4096]{1,0:T(8,128)(2,1)S(1)} %slice_bitcast_fusion.1.refs_1_), channel_id=1, source_target_pairs={{1,2},{2,1},{5,6},{6,5},{9,10},{10,9},{13,14},{14,13},{17,18},{18,... | collective-permute-start | bytes 589832 | tf_op jit(solution)/shard_map/ppermute | solution.py:112
  16.8 17.8 %collective-permute-start.4 = (bf16[32,4096]{1,0:T(8,128)(2,1)S(1)}, bf16[32,4096]{1,0:T(8,128)(2,1)S(1)}, u32[]{:S(2)}, u32[]{:S(2)}) collective-permute-start(bf16[32,4096]{1,0:T(8,128)(2,1)S(1)} %apply_layer.16.refs_4_), channel_id=1, source_target_pairs={{0,5},{1,4},{2,7},{3,6},{4,9},{5,8},{6,11},{7,10},{8,13},{9,12},{1... | collective-permute-start | bytes 786440 | tf_op jit(solution)/shard_map/ppermute | solution.py:112
  21.1 16.2 %collective-permute-start.5 = (bf16[32,4096]{1,0:T(8,128)(2,1)S(1)}, bf16[32,4096]{1,0:T(8,128)(2,1)S(1)}, u32[]{:S(2)}, u32[]{:S(2)}) collective-permute-start(bf16[32,4096]{1,0:T(8,128)(2,1)S(1)} %apply_layer.16.refs_4_), channel_id=1, source_target_pairs={{0,4},{1,5},{2,6},{3,7},{4,8},{5,9},{6,10},{7,11},{8,12},{9,13},{1... | collective-permute-start | bytes 786440 | tf_op jit(solution)/shard_map/ppermute | solution.py:112
  28.8 14.5 %collective-permute-start.7 = (bf16[24,4096]{1,0:T(8,128)(2,1)S(1)}, bf16[24,4096]{1,0:T(8,128)(2,1)S(1)}, u32[]{:S(2)}, u32[]{:S(2)}) collective-permute-start(bf16[24,4096]{1,0:T(8,128)(2,1)S(1)} %apply_layer.17.refs_4_), channel_id=1, source_target_pairs={{0,5},{1,4},{2,7},{3,6},{4,9},{5,8},{6,11},{7,10},{8,13},{9,12},{1... | collective-permute-start | bytes 589832 | tf_op jit(solution)/shard_map/ppermute | solution.py:112
  31.1 16.3 %collective-permute-start.8 = (bf16[24,4096]{1,0:T(8,128)(2,1)S(1)}, bf16[24,4096]{1,0:T(8,128)(2,1)S(1)}, u32[]{:S(2)}, u32[]{:S(2)}) collective-permute-start(bf16[24,4096]{1,0:T(8,128)(2,1)S(1)} %apply_layer.17.refs_4_), channel_id=1, source_target_pairs={{0,4},{1,5},{2,6},{3,7},{4,8},{5,9},{6,10},{7,11},{8,12},{9,13},{1... | collective-permute-start | bytes 589832 | tf_op jit(solution)/shard_map/ppermute | solution.py:112
  39.1 14.7 %collective-permute-start.10 = (bf16[32,4096]{1,0:T(8,128)(2,1)S(1)}, bf16[32,4096]{1,0:T(8,128)(2,1)S(1)}, u32[]{:S(2)}, u32[]{:S(2)}) collective-permute-start(bf16[32,4096]{1,0:T(8,128)(2,1)S(1)} %apply_layer.18.refs_4_), channel_id=1, source_target_pairs={{0,5},{1,4},{2,7},{3,6},{4,9},{5,8},{6,11},{7,10},{8,13},{9,12},{1... | collective-permute-start | bytes 786440 | tf_op jit(solution)/shard_map/ppermute | solution.py:112
  41.2 15.7 %collective-permute-start.11 = (bf16[32,4096]{1,0:T(8,128)(2,1)S(1)}, bf16[32,4096]{1,0:T(8,128)(2,1)S(1)}, u32[]{:S(2)}, u32[]{:S(2)}) collective-permute-start(bf16[32,4096]{1,0:T(8,128)(2,1)S(1)} %apply_layer.18.refs_4_), channel_id=1, source_target_pairs={{0,4},{1,5},{2,6},{3,7},{4,8},{5,9},{6,10},{7,11},{8,12},{9,13},{1... | collective-permute-start | bytes 786440 | tf_op jit(solution)/shard_map/ppermute | solution.py:112
  43.3 14.0 %collective-permute-start.12 = (bf16[32,4096]{1,0:T(8,128)(2,1)S(1)}, bf16[32,4096]{1,0:T(8,128)(2,1)S(1)}, u32[]{:S(2)}, u32[]{:S(2)}) collective-permute-start(bf16[32,4096]{1,0:T(8,128)(2,1)S(1)} %apply_layer.18.refs_4_), channel_id=1, source_target_pairs={{1,6},{2,5},{5,10},{6,9},{9,14},{10,13},{13,18},{14,17},{17,22},{1... | collective-permute-start | bytes 786440 | tf_op jit(solution)/shard_map/ppermute | solution.py:112
  51.0 15.6 %collective-permute-start.14 = (bf16[24,4096]{1,0:T(8,128)(2,1)S(1)}, bf16[24,4096]{1,0:T(8,128)(2,1)S(1)}, u32[]{:S(2)}, u32[]{:S(2)}) collective-permute-start(bf16[24,4096]{1,0:T(8,128)(2,1)S(1)} %apply_layer.19.refs_4_), channel_id=1, source_target_pairs={{0,4},{1,5},{2,6},{3,7},{4,8},{5,9},{6,10},{7,11},{8,12},{9,13},{1... | collective-permute-start | bytes 589832 | tf_op jit(solution)/shard_map/ppermute | solution.py:112
  59.1 14.5 %collective-permute-start.16 = (bf16[32,4096]{1,0:T(8,128)(2,1)S(1)}, bf16[32,4096]{1,0:T(8,128)(2,1)S(1)}, u32[]{:S(2)}, u32[]{:S(2)}) collective-permute-start(bf16[32,4096]{1,0:T(8,128)(2,1)S(1)} %apply_layer.20.refs_4_), channel_id=1, source_target_pairs={{0,5},{1,4},{2,7},{3,6},{4,9},{5,8},{6,11},{7,10},{8,13},{9,12},{1... | collective-permute-start | bytes 786440 | tf_op jit(solution)/shard_map/ppermute | solution.py:112
  61.0 15.7 %collective-permute-start.17 = (bf16[32,4096]{1,0:T(8,128)(2,1)S(1)}, bf16[32,4096]{1,0:T(8,128)(2,1)S(1)}, u32[]{:S(2)}, u32[]{:S(2)}) collective-permute-start(bf16[32,4096]{1,0:T(8,128)(2,1)S(1)} %apply_layer.20.refs_4_), channel_id=1, source_target_pairs={{0,4},{1,5},{2,6},{3,7},{4,8},{5,9},{6,10},{7,11},{8,12},{9,13},{1... | collective-permute-start | bytes 786440 | tf_op jit(solution)/shard_map/ppermute | solution.py:112
  63.0 14.2 %collective-permute-start.18 = (bf16[32,4096]{1,0:T(8,128)(2,1)S(1)}, bf16[32,4096]{1,0:T(8,128)(2,1)S(1)}, u32[]{:S(2)}, u32[]{:S(2)}) collective-permute-start(bf16[32,4096]{1,0:T(8,128)(2,1)S(1)} %apply_layer.20.refs_4_), channel_id=1, source_target_pairs={{1,6},{2,5},{5,10},{6,9},{9,14},{10,13},{13,18},{14,17},{17,22},{1... | collective-permute-start | bytes 786440 | tf_op jit(solution)/shard_map/ppermute | solution.py:112
  68.4 14.4 %collective-permute-start.19 = (bf16[24,4096]{1,0:T(8,128)(2,1)S(1)}, bf16[24,4096]{1,0:T(8,128)(2,1)S(1)}, u32[]{:S(2)}, u32[]{:S(2)}) collective-permute-start(bf16[24,4096]{1,0:T(8,128)(2,1)S(1)} %apply_layer.21.refs_4_), channel_id=1, source_target_pairs={{0,5},{1,4},{2,7},{3,6},{4,9},{5,8},{6,11},{7,10},{8,13},{9,12},{1... | collective-permute-start | bytes 589832 | tf_op jit(solution)/shard_map/ppermute | solution.py:112
  70.4 15.9 %collective-permute-start.20 = (bf16[24,4096]{1,0:T(8,128)(2,1)S(1)}, bf16[24,4096]{1,0:T(8,128)(2,1)S(1)}, u32[]{:S(2)}, u32[]{:S(2)}) collective-permute-start(bf16[24,4096]{1,0:T(8,128)(2,1)S(1)} %apply_layer.21.refs_4_), channel_id=1, source_target_pairs={{0,4},{1,5},{2,6},{3,7},{4,8},{5,9},{6,10},{7,11},{8,12},{9,13},{1... | collective-permute-start | bytes 589832 | tf_op jit(solution)/shard_map/ppermute | solution.py:112
  78.9 14.3 %collective-permute-start.22 = (bf16[32,4096]{1,0:T(8,128)(2,1)S(1)}, bf16[32,4096]{1,0:T(8,128)(2,1)S(1)}, u32[]{:S(2)}, u32[]{:S(2)}) collective-permute-start(bf16[32,4096]{1,0:T(8,128)(2,1)S(1)} %apply_layer.22.refs_4_), channel_id=1, source_target_pairs={{0,5},{1,4},{2,7},{3,6},{4,9},{5,8},{6,11},{7,10},{8,13},{9,12},{1... | collective-permute-start | bytes 786440 | tf_op jit(solution)/shard_map/ppermute | solution.py:112
  80.9 15.7 %collective-permute-start.23 = (bf16[32,4096]{1,0:T(8,128)(2,1)S(1)}, bf16[32,4096]{1,0:T(8,128)(2,1)S(1)}, u32[]{:S(2)}, u32[]{:S(2)}) collective-permute-start(bf16[32,4096]{1,0:T(8,128)(2,1)S(1)} %apply_layer.22.refs_4_), channel_id=1, source_target_pairs={{0,4},{1,5},{2,6},{3,7},{4,8},{5,9},{6,10},{7,11},{8,12},{9,13},{1... | collective-permute-start | bytes 786440 | tf_op jit(solution)/shard_map/ppermute | solution.py:112
  82.8 14.0 %collective-permute-start.24 = (bf16[32,4096]{1,0:T(8,128)(2,1)S(1)}, bf16[32,4096]{1,0:T(8,128)(2,1)S(1)}, u32[]{:S(2)}, u32[]{:S(2)}) collective-permute-start(bf16[32,4096]{1,0:T(8,128)(2,1)S(1)} %apply_layer.22.refs_4_), channel_id=1, source_target_pairs={{1,6},{2,5},{5,10},{6,9},{9,14},{10,13},{13,18},{14,17},{17,22},{1... | collective-permute-start | bytes 786440 | tf_op jit(solution)/shard_map/ppermute | solution.py:112
  88.1 14.4 %collective-permute-start.25 = (bf16[24,4096]{1,0:T(8,128)(2,1)S(1)}, bf16[24,4096]{1,0:T(8,128)(2,1)S(1)}, u32[]{:S(2)}, u32[]{:S(2)}) collective-permute-start(bf16[24,4096]{1,0:T(8,128)(2,1)S(1)} %apply_layer.23.refs_4_), channel_id=1, source_target_pairs={{0,5},{1,4},{2,7},{3,6},{4,9},{5,8},{6,11},{7,10},{8,13},{9,12},{1... | collective-permute-start | bytes 589832 | tf_op jit(solution)/shard_map/ppermute | solution.py:112
  90.1 15.9 %collective-permute-start.26 = (bf16[24,4096]{1,0:T(8,128)(2,1)S(1)}, bf16[24,4096]{1,0:T(8,128)(2,1)S(1)}, u32[]{:S(2)}, u32[]{:S(2)}) collective-permute-start(bf16[24,4096]{1,0:T(8,128)(2,1)S(1)} %apply_layer.23.refs_4_), channel_id=1, source_target_pairs={{0,4},{1,5},{2,6},{3,7},{4,8},{5,9},{6,10},{7,11},{8,12},{9,13},{1... | collective-permute-start | bytes 589832 | tf_op jit(solution)/shard_map/ppermute | solution.py:112
  98.6 14.3 %collective-permute-start.28 = (bf16[32,4096]{1,0:T(8,128)(2,1)S(1)}, bf16[32,4096]{1,0:T(8,128)(2,1)S(1)}, u32[]{:S(2)}, u32[]{:S(2)}) collective-permute-start(bf16[32,4096]{1,0:T(8,128)(2,1)S(1)} %apply_layer.24.refs_4_), channel_id=1, source_target_pairs={{0,5},{1,4},{2,7},{3,6},{4,9},{5,8},{6,11},{7,10},{8,13},{9,12},{1... | collective-permute-start | bytes 786440 | tf_op jit(solution)/shard_map/ppermute | solution.py:112
  100.5 15.5 %collective-permute-start.29 = (bf16[32,4096]{1,0:T(8,128)(2,1)S(1)}, bf16[32,4096]{1,0:T(8,128)(2,1)S(1)}, u32[]{:S(2)}, u32[]{:S(2)}) collective-permute-start(bf16[32,4096]{1,0:T(8,128)(2,1)S(1)} %apply_layer.24.refs_4_), channel_id=1, source_target_pairs={{0,4},{1,5},{2,6},{3,7},{4,8},{5,9},{6,10},{7,11},{8,12},{9,13},{1... | collective-permute-start | bytes 786440 | tf_op jit(solution)/shard_map/ppermute | solution.py:112
  107.9 14.1 %collective-permute-start.31 = (bf16[24,4096]{1,0:T(8,128)(2,1)S(1)}, bf16[24,4096]{1,0:T(8,128)(2,1)S(1)}, u32[]{:S(2)}, u32[]{:S(2)}) collective-permute-start(bf16[24,4096]{1,0:T(8,128)(2,1)S(1)} %apply_layer.25.refs_4_), channel_id=1, source_target_pairs={{0,5},{1,4},{2,7},{3,6},{4,9},{5,8},{6,11},{7,10},{8,13},{9,12},{1... | collective-permute-start | bytes 589832 | tf_op jit(solution)/shard_map/ppermute | solution.py:112
  109.9 15.7 %collective-permute-start.32 = (bf16[24,4096]{1,0:T(8,128)(2,1)S(1)}, bf16[24,4096]{1,0:T(8,128)(2,1)S(1)}, u32[]{:S(2)}, u32[]{:S(2)}) collective-permute-start(bf16[24,4096]{1,0:T(8,128)(2,1)S(1)} %apply_layer.25.refs_4_), channel_id=1, source_target_pairs={{0,4},{1,5},{2,6},{3,7},{4,8},{5,9},{6,10},{7,11},{8,12},{9,13},{1... | collective-permute-start | bytes 589832 | tf_op jit(solution)/shard_map/ppermute | solution.py:112
  118.2 14.3 %collective-permute-start.34 = (bf16[32,4096]{1,0:T(8,128)(2,1)S(1)}, bf16[32,4096]{1,0:T(8,128)(2,1)S(1)}, u32[]{:S(2)}, u32[]{:S(2)}) collective-permute-start(bf16[32,4096]{1,0:T(8,128)(2,1)S(1)} %apply_layer.26.refs_4_), channel_id=1, source_target_pairs={{0,5},{1,4},{2,7},{3,6},{4,9},{5,8},{6,11},{7,10},{8,13},{9,12},{1... | collective-permute-start | bytes 786440 | tf_op jit(solution)/shard_map/ppermute | solution.py:112
  120.2 15.5 %collective-permute-start.35 = (bf16[32,4096]{1,0:T(8,128)(2,1)S(1)}, bf16[32,4096]{1,0:T(8,128)(2,1)S(1)}, u32[]{:S(2)}, u32[]{:S(2)}) collective-permute-start(bf16[32,4096]{1,0:T(8,128)(2,1)S(1)} %apply_layer.26.refs_4_), channel_id=1, source_target_pairs={{0,4},{1,5},{2,6},{3,7},{4,8},{5,9},{6,10},{7,11},{8,12},{9,13},{1... | collective-permute-start | bytes 786440 | tf_op jit(solution)/shard_map/ppermute | solution.py:112
  122.1 14.1 %collective-permute-start.36 = (bf16[32,4096]{1,0:T(8,128)(2,1)S(1)}, bf16[32,4096]{1,0:T(8,128)(2,1)S(1)}, u32[]{:S(2)}, u32[]{:S(2)}) collective-permute-start(bf16[32,4096]{1,0:T(8,128)(2,1)S(1)} %apply_layer.26.refs_4_), channel_id=1, source_target_pairs={{1,6},{2,5},{5,10},{6,9},{9,14},{10,13},{13,18},{14,17},{17,22},{1... | collective-permute-start | bytes 786440 | tf_op jit(solution)/shard_map/ppermute | solution.py:112
  127.5 14.3 %collective-permute-start.37 = (bf16[24,4096]{1,0:T(8,128)(2,1)S(1)}, bf16[24,4096]{1,0:T(8,128)(2,1)S(1)}, u32[]{:S(2)}, u32[]{:S(2)}) collective-permute-start(bf16[24,4096]{1,0:T(8,128)(2,1)S(1)} %apply_layer.27.refs_4_), channel_id=1, source_target_pairs={{0,5},{1,4},{2,7},{3,6},{4,9},{5,8},{6,11},{7,10},{8,13},{9,12},{1... | collective-permute-start | bytes 589832 | tf_op jit(solution)/shard_map/ppermute | solution.py:112
  129.4 15.9 %collective-permute-start.38 = (bf16[24,4096]{1,0:T(8,128)(2,1)S(1)}, bf16[24,4096]{1,0:T(8,128)(2,1)S(1)}, u32[]{:S(2)}, u32[]{:S(2)}) collective-permute-start(bf16[24,4096]{1,0:T(8,128)(2,1)S(1)} %apply_layer.27.refs_4_), channel_id=1, source_target_pairs={{0,4},{1,5},{2,6},{3,7},{4,8},{5,9},{6,10},{7,11},{8,12},{9,13},{1... | collective-permute-start | bytes 589832 | tf_op jit(solution)/shard_map/ppermute | solution.py:112
  137.9 14.3 %collective-permute-start.40 = (bf16[32,4096]{1,0:T(8,128)(2,1)S(1)}, bf16[32,4096]{1,0:T(8,128)(2,1)S(1)}, u32[]{:S(2)}, u32[]{:S(2)}) collective-permute-start(bf16[32,4096]{1,0:T(8,128)(2,1)S(1)} %apply_layer.28.refs_4_), channel_id=1, source_target_pairs={{0,5},{1,4},{2,7},{3,6},{4,9},{5,8},{6,11},{7,10},{8,13},{9,12},{1... | collective-permute-start | bytes 786440 | tf_op jit(solution)/shard_map/ppermute | solution.py:112
  139.9 15.5 %collective-permute-start.41 = (bf16[32,4096]{1,0:T(8,128)(2,1)S(1)}, bf16[32,4096]{1,0:T(8,128)(2,1)S(1)}, u32[]{:S(2)}, u32[]{:S(2)}) collective-permute-start(bf16[32,4096]{1,0:T(8,128)(2,1)S(1)} %apply_layer.28.refs_4_), channel_id=1, source_target_pairs={{0,4},{1,5},{2,6},{3,7},{4,8},{5,9},{6,10},{7,11},{8,12},{9,13},{1... | collective-permute-start | bytes 786440 | tf_op jit(solution)/shard_map/ppermute | solution.py:112
  141.8 14.0 %collective-permute-start.42 = (bf16[32,4096]{1,0:T(8,128)(2,1)S(1)}, bf16[32,4096]{1,0:T(8,128)(2,1)S(1)}, u32[]{:S(2)}, u32[]{:S(2)}) collective-permute-start(bf16[32,4096]{1,0:T(8,128)(2,1)S(1)} %apply_layer.28.refs_4_), channel_id=1, source_target_pairs={{1,6},{2,5},{5,10},{6,9},{9,14},{10,13},{13,18},{14,17},{17,22},{1... | collective-permute-start | bytes 786440 | tf_op jit(solution)/shard_map/ppermute | solution.py:112
  (16 other events, 182.2 us)
